TPU v7x, 32 devices: a whole 2x2x4 slice. The times are simulated.
32 devices in a mesh: lat: 4 (over x, core), lon: 4 (over z), lev: 2 (over y).
Axes of the slice: x: 2, y: 2, z: 4, core: 2. Of those that a mesh axis runs over, the one named last changes fastest.
Arguments:
- fields: float32 [32, 32, 4, 512], P('lat', 'lon', 'lev'), may hold values from -6 to 6
- gain: float32 [512], replicated, may hold values from 0.1 to 1.9
- w_qkv: float32 [512, 1536], replicated, may hold values from -2 to 2
- w_out: float32 [512, 512], replicated, may hold values from -0.25 to 0.25
- cotangent: float32 [32, 32, 4, 512], P('lat', 'lon', 'lev'), may hold values from -6 to 6
Outputs:
- output: float32 [32, 32, 4, 512], P('lat', 'lon', 'lev')
- grad_fields: float32 [32, 32, 4, 512], P('lat', 'lon', 'lev')
- grad_gain: float32 [512], replicated
- grad_qkv: float32 [512, 1536], replicated
- grad_w_out: float32 [512, 512], replicated
All inputs are finite; a program needn't handle non-finite values.
Results may differ from a plain program's by a relative error of at most 0.0003.
Values sent between devices are 32-bit elements; how exact they have to be, the bound alone decides.
No kernel may reach another device: no remote copies, remote signals or barrier semaphores. Data moves between devices by JAX's collectives and lax.ppermute only.
A program may use at most 128 MiB of HBM per device.

v0:
```python
import jax
import jax.numpy as jnp
import numpy as np
from jax import lax
from jax.experimental import pallas as pl
from jax.experimental.pallas import tpu as pltpu
from jax.sharding import PartitionSpec as P

D = 512
HEADS = 16
HEAD_DIM = 32
LAT_REACH = 3
LON_REACH = 3
LEV_REACH = 1
EPSILON = 1e-06
GROUP = 128
SLAB = 48
TAIL = 64
NEVER = -1e30
F32 = jnp.float32
BF16 = jnp.bfloat16


def split(x):
    high = x.astype(BF16)
    return high, (x - high.astype(F32)).astype(BF16)


def split3(x):
    high = x.astype(BF16)
    rest = x - high.astype(F32)
    middle = rest.astype(BF16)
    return high, middle, (rest - middle.astype(F32)).astype(BF16)


def dot(a, b, ca=1, cb=0):
    return lax.dot_general(a, b, (((ca,), (cb,)), ((), ())), preferred_element_type=F32)


def dot3(a, b, ca=1, cb=0):
    (ah, al), (bh, bl) = a, b
    return dot(ah, bh, ca, cb) + dot(ah, bl, ca, cb) + dot(al, bh, ca, cb)


def dot6(a, b, ca=1, cb=0):
    (ah, am, al), (bh, bm, bl) = a, b
    small = dot(am, bm, ca, cb) + dot(ah, bl, ca, cb) + dot(al, bh, ca, cb)
    return dot(ah, bh, ca, cb) + (dot(ah, bm, ca, cb) + dot(am, bh, ca, cb) + small)


def attention_kernel(
    first, pos_ref, top_ref, mid_ref, bot_ref, gain_ref, wq_ref, wk_ref, wv_ref, wo_ref, cot_ref,
    bias0_ref, bias1_ref, *refs,
):
    if not first:
        out0_ref, bn0_ref, *refs = refs
    if first:
        out_ref, bn_ref, g_ref, *refs = refs
    else:
        out_ref, btop_ref, bmid_ref, bbot_ref, g_ref, *refs = refs
    x_s, n_hi, n_md, n_lo, nt_hi, nt_lo, ot_hi, ot_lo, bn_s, dkv_s, kcat_s, vcat_s, kl_s, vl_s = refs
    step = pl.program_id(0)
    last = pl.num_programs(0) - 1
    rows = x_s.shape[0]
    lats = rows // SLAB
    mid_lats = mid_ref.shape[0]
    tok = mid_lats * 16
    half_tok = tok // 2
    scale = HEAD_DIM ** (-0.5)

    def own_rows(x):
        return x.reshape(lats, SLAB, D)[LAT_REACH:LAT_REACH + mid_lats, :16].reshape(tok, D)

    @pl.when(step == 0)
    def _():
        x = jnp.concatenate([top_ref[...], mid_ref[...], bot_ref[...]], axis=0).reshape(rows, D)
        x_s[...] = x
        inv = lax.rsqrt(jnp.mean(x * x, axis=-1, keepdims=True) + EPSILON)
        normed = x * inv * gain_ref[...]
        n_hi[...], n_md[...], n_lo[...] = split3(normed)
        pad = jnp.zeros((nt_hi.shape[1] - rows, D), F32)
        nt_hi[...], nt_lo[...] = split(jnp.concatenate([normed, pad], axis=0).T)
        ot_hi[...], ot_lo[...] = split(own_rows(normed).T)
        if first:
            bn_s[...] = jnp.zeros(bn_s.shape, F32)
            out_ref[...] = mid_ref[...][:, :16].reshape(tok, D)
        else:
            bn_s[...] = bn0_ref[...].reshape(rows, D)
            out_ref[...] = out0_ref[...]

    wq = split3(wq_ref[...])
    wkv = split3(jnp.concatenate([wk_ref[...], wv_ref[...]], axis=1))
    wo = split3(wo_ref[...])
    normed = (n_hi[...], n_md[...], n_lo[...])
    kv = dot6(normed, wkv)
    k_hi, k_md, k_lo = split3(kv[:, :GROUP])
    v_hi, v_md, v_lo = split3(kv[:, GROUP:])
    kcat_s[:, :GROUP] = k_hi
    kcat_s[:, GROUP:] = k_md
    kl_s[...] = k_lo
    vcat_s[:, :GROUP] = v_hi
    vcat_s[:, GROUP:] = v_md
    vl_s[...] = v_lo
    own_t = (ot_hi[...], ot_lo[...])
    own = tuple(own_rows(x) for x in normed)
    q_t = (dot6(own, wq) * scale).T
    cot = split3(cot_ref[...])
    b_t = dot6(cot, wo, 1, 1).T
    dkv_s[...] = jnp.zeros(dkv_s.shape, F32)
    heads = GROUP // HEAD_DIM
    cols = heads * half_tok
    head_row = lax.broadcasted_iota(jnp.int32, (GROUP, cols), 0) // HEAD_DIM
    head_col = lax.broadcasted_iota(jnp.int32, (GROUP, cols), 1) // half_tok
    same = head_row == head_col
    keys = bias0_ref.shape[1]

    def spread(x):
        return jnp.where(same, jnp.concatenate([x] * heads, axis=1), 0.0)

    def gather(x):
        x = jnp.where(same, x, 0.0)
        y = x[:, :half_tok]
        for h in range(1, heads):
            y = y + x[:, h * half_tok:(h + 1) * half_tok]
        return y

    def against(cat, low, columns):
        hi, md, lo = split3(columns)
        small = dot(jnp.concatenate([cat[:, :GROUP], low], axis=1), jnp.concatenate([lo, hi], axis=0))
        small = small + dot(cat, jnp.concatenate([md, md], axis=0))
        return dot(cat, jnp.concatenate([hi, hi], axis=0)) + small

    mixed_parts, dq_parts = [], []
    for half in range(2):
        lo_row = half * (rows - keys)
        here = slice(lo_row, lo_row + keys)
        kcat = kcat_s[here, :]
        vcat = vcat_s[here, :]
        q_cols = spread(q_t[:, half * half_tok:(half + 1) * half_tok])
        b_cols = spread(b_t[:, half * half_tok:(half + 1) * half_tok])
        bias = (bias0_ref, bias1_ref)[half][0]
        s = against(kcat, kl_s[here, :], q_cols)
        s = s + jnp.concatenate([bias] * (cols // bias.shape[1]), axis=1)
        p = jnp.exp(s - jnp.max(s, axis=0, keepdims=True))
        inv_sum = 1.0 / jnp.sum(p, axis=0, keepdims=True)
        p_hi, p_lo = split(p)
        kcat_t = kcat.T
        vcat_t = vcat.T
        m2 = dot(vcat_t, p_hi)
        mixed_parts.append(gather((m2[:GROUP] + m2[GROUP:] + dot(vcat_t[:GROUP], p_lo)) * inv_sum))
        b_cols = b_cols * inv_sum
        dp = against(vcat, vl_s[here, :], b_cols)
        agreement = jnp.sum(p * dp, axis=0, keepdims=True) * inv_sum
        ds = p * (dp - agreement)
        ds_hi, ds_lo = split(ds)
        dq2 = dot(kcat_t, ds_hi)
        dq_parts.append(gather(dq2[:GROUP] + dq2[GROUP:] + dot(kcat_t[:GROUP], ds_lo)))
        q_rows = split(q_cols.T)
        b_rows = split(b_cols.T)
        dk2 = dot(ds_hi, jnp.concatenate(q_rows, axis=1))
        dk = dk2[:, :GROUP] + dk2[:, GROUP:] + dot(ds_lo, q_rows[0])
        dv2 = dot(p_hi, jnp.concatenate(b_rows, axis=1))
        dv = dv2[:, :GROUP] + dv2[:, GROUP:] + dot(p_lo, b_rows[0])
        dkv_s[here, :GROUP] += dk
        dkv_s[here, GROUP:] += dv
    mixed_t = jnp.concatenate(mixed_parts, axis=1)
    dq = split((jnp.concatenate(dq_parts, axis=1) * scale).T)
    out_ref[...] += dot3(split(mixed_t.T), wo[:2])
    gwo = dot3(split(mixed_t), cot[:2])
    gq = dot3(own_t, dq)
    dkv = split(dkv_s[...])
    gkv = dot3((nt_hi[...], nt_lo[...]), dkv)
    g_ref[0, 0:D, :] = gq
    g_ref[0, D:2 * D, :] = gkv[:, :GROUP]
    g_ref[0, 2 * D:3 * D, :] = gkv[:, GROUP:]
    for j in range(D // GROUP):
        g_ref[0, 3 * D + j * GROUP:3 * D + (j + 1) * GROUP, :] = gwo[:, j * GROUP:(j + 1) * GROUP]
    if not first:
        g_ref[0, 4 * D:, :] = jnp.zeros((TAIL, GROUP), F32)
    bn_s[...] += dot3((dkv[0][:rows], dkv[1][:rows]), wkv[:2], 1, 1)
    back_q = dot3(dq, wq[:2], 1, 1)
    for i in range(mid_lats):
        at = (LAT_REACH + i) * SLAB
        bn_s[at:at + 16, :] += back_q[i * 16:(i + 1) * 16]

    @pl.when(step == last)
    def _():
        bn3 = bn_s[...].reshape(lats, SLAB, D)
        if first:
            bn_ref[...] = bn3
        else:
            btop_ref[...] = bn3[:LAT_REACH]
            bbot_ref[...] = bn3[LAT_REACH + mid_lats:]
            bmid_ref[...] = bn3[LAT_REACH:LAT_REACH + mid_lats]
            x = x_s[...]
            inv = lax.rsqrt(jnp.mean(x * x, axis=-1, keepdims=True) + EPSILON)
            unit = x * inv
            gg = jnp.sum(bn_s[...] * unit, axis=0, keepdims=True)
            for j in range(D // GROUP):
                g_ref[0, 4 * D + j:4 * D + j + 1, :] = gg[:, j * GROUP:(j + 1) * GROUP]


def attention(first, pos, top, mid, bot, gain, w_qkv, w_out, cot, bias, *before):
    mid_lats = mid.shape[0]
    lats = mid_lats + 2 * LAT_REACH
    rows = lats * SLAB
    tok = mid_lats * 16
    padded = -(-rows // 256) * 256
    groups = D // GROUP
    whole = lambda *shape: pl.BlockSpec(shape, lambda s, pos: (0,) * len(shape))
    slab = lambda n: whole(n, SLAB, D)
    like = lambda *shape: jax.ShapeDtypeStruct(shape, F32)
    base = 0 if first else 2
    group = lambda s, pos: base + (1 - pos[0]) * (1 - s) + pos[0] * s
    outs, out_specs = [like(tok, D)], [whole(tok, D)]
    tail = 0 if first else TAIL
    if first:
        outs.append(like(lats, SLAB, D))
        out_specs.append(slab(lats))
    else:
        for n in (LAT_REACH, mid_lats, LAT_REACH):
            outs.append(like(n, SLAB, D))
            out_specs.append(slab(n))
    outs.append(like(2, 4 * D + tail, GROUP))
    out_specs.append(pl.BlockSpec((1, 4 * D + tail, GROUP), lambda s, pos: (s, 0, 0)))
    body = lambda *refs: attention_kernel(first, *refs)
    return pl.pallas_call(
        body,
        grid_spec=pltpu.PrefetchScalarGridSpec(
            num_scalar_prefetch=1,
            grid=(2,),
            in_specs=[
                slab(LAT_REACH), slab(mid_lats), slab(LAT_REACH), whole(1, D),
                pl.BlockSpec((D, GROUP), lambda s, pos: (0, group(s, pos))),
                pl.BlockSpec((D, GROUP), lambda s, pos: (0, groups + group(s, pos))),
                pl.BlockSpec((D, GROUP), lambda s, pos: (0, 2 * groups + group(s, pos))),
                pl.BlockSpec((GROUP, D), lambda s, pos: (group(s, pos), 0)),
                whole(tok, D),
                pl.BlockSpec((1,) + bias.shape[1:], lambda s, pos: (pos[1], 0, 0)),
                pl.BlockSpec((1,) + bias.shape[1:], lambda s, pos: (pos[2], 0, 0)),
            ] + [whole(*x.shape) for x in before],
            out_specs=out_specs,
            scratch_shapes=[
                pltpu.VMEM((rows, D), F32),
                pltpu.VMEM((rows, D), BF16), pltpu.VMEM((rows, D), BF16), pltpu.VMEM((rows, D), BF16),
                pltpu.VMEM((D, padded), BF16), pltpu.VMEM((D, padded), BF16),
                pltpu.VMEM((D, tok), BF16), pltpu.VMEM((D, tok), BF16),
                pltpu.VMEM((rows, D), F32),
                pltpu.VMEM((padded, 2 * GROUP), F32),
                pltpu.VMEM((rows, 2 * GROUP), BF16), pltpu.VMEM((rows, 2 * GROUP), BF16),
                pltpu.VMEM((rows, GROUP), BF16), pltpu.VMEM((rows, GROUP), BF16),
            ],
        ),
        out_shape=outs,
        compiler_params=pltpu.CompilerParams(vmem_limit_bytes=48 * 1024 * 1024),
        cost_estimate=pl.CostEstimate(flops=8_000_000_000, bytes_accessed=16_000_000, transcendentals=1_000_000),
        name="attention",
    )(pos, top, mid, bot, gain.reshape(1, D), w_qkv, w_qkv, w_qkv, w_out, cot, bias, bias, *before)


def unpack_kernel(factor, core_ref, *refs):
    groups = D // GROUP
    *parts, gain_ref, qkv_ref, out_ref = refs
    core = core_ref[0]
    for i, ref in enumerate(parts):
        k, other = divmod(i, 2)
        g = 2 * k + jnp.where(other == 1, 1 - core, core)
        for j in range(3):
            at = pl.multiple_of((j * groups + g) * GROUP, GROUP)
            qkv_ref[:, pl.ds(at, GROUP)] = ref[j * D:(j + 1) * D, :] * factor
        at = pl.multiple_of(g * GROUP, GROUP)
        for j in range(groups):
            out_ref[pl.ds(at, GROUP), j * GROUP:(j + 1) * GROUP] = (
                ref[3 * D + j * GROUP:3 * D + (j + 1) * GROUP, :] * factor
            )
    both = (parts[2][4 * D:4 * D + 8, :] + parts[3][4 * D:4 * D + 8, :]) * factor
    gain_ref[...] = both


def unpack(core, factor, parts):
    return pl.pallas_call(
        lambda *refs: unpack_kernel(factor, *refs),
        in_specs=[pl.BlockSpec(memory_space=pltpu.SMEM)] + [pl.BlockSpec(memory_space=pltpu.VMEM)] * 4,
        out_specs=[pl.BlockSpec(memory_space=pltpu.VMEM)] * 3,
        out_shape=[
            jax.ShapeDtypeStruct((8, GROUP), F32),
            jax.ShapeDtypeStruct((D, 3 * D), F32),
            jax.ShapeDtypeStruct((D, D), F32),
        ],
        compiler_params=pltpu.CompilerParams(vmem_limit_bytes=32 * 1024 * 1024),
        cost_estimate=pl.CostEstimate(flops=1_000_000, bytes_accessed=8_000_000, transcendentals=0),
        name="unpack",
    )(core, *parts)


def shift(x, axis, step, closed):
    count = lax.axis_size(axis)
    ends = count if closed else count - 1
    pairs = [(i, (i + 1) % count) for i in range(ends)]
    if step < 0:
        pairs = [(j, i) for i, j in pairs]
    return lax.ppermute(x, axis, pairs)


def shift_across(x, step):
    count = lax.axis_size("lon")
    pairs = []
    for i in range(count):
        for e in range(2):
            pairs.append((i * 2 + e, ((i + step) % count) * 2 + 1 - e))
    return lax.ppermute(x, ("lon", "lev"), pairs)


def swap_lev(x):
    return lax.ppermute(x, "lev", [(0, 1), (1, 0)])


def window_bias(lat_dev, lon_dev, keys):
    left = np.arange(-LON_REACH, 0)
    right = np.arange(lon_dev, lon_dev + LON_REACH)
    lon = np.concatenate([
        np.repeat(np.arange(lon_dev), 2), np.arange(lon_dev), np.repeat(left, 2), np.repeat(right, 2),
        left, right,
    ])
    level = np.concatenate([
        np.tile([0, 1], lon_dev), np.full(lon_dev, 2), np.tile([0, 1], 2 * LON_REACH),
        np.full(2 * LON_REACH, 2),
    ])
    unused = SLAB - lon.shape[0]
    lon = np.concatenate([lon, np.full(unused, 1000)])
    level = np.concatenate([level, np.full(unused, 0)])
    lats = lat_dev + 2 * LAT_REACH
    rows = lats * SLAB
    lat = np.repeat(np.arange(lats) - LAT_REACH, SLAB)[:, None]
    lon = np.tile(lon, lats)[:, None]
    level = np.tile(level, lats)[:, None]
    q_lat = np.repeat(np.arange(lat_dev), lon_dev * 2)
    q_lon = np.tile(np.repeat(np.arange(lon_dev), 2), lat_dev)
    q_level = np.tile([0, 1], lat_dev * lon_dev)
    near = (np.abs(lat - q_lat) <= LAT_REACH) & (np.abs(lon - q_lon) <= LON_REACH)
    half = q_lat.shape[0] // 2
    table = []
    for part in range(2):
        first = part * (rows - keys)
        ks = slice(first, first + keys)
        qs = np.tile(np.arange(part * half, (part + 1) * half), 2)
        for side in range(2):
            lev_k = np.where(level == 2, 2 - side, side * 2 + level)
            seen = near & (np.abs(lev_k - (side * 2 + q_level)) <= LEV_REACH)
            for edge in range(2):
                kept = seen
                if edge == 1:
                    kept = seen & ((lat >= 0) if part == 0 else (lat < lat_dev))
                table.append(np.where(kept[ks][:, qs], 0.0, NEVER))
    return np.stack(table).astype(np.float32)


def bit_of(axis, bit):
    return (lax.axis_index(axis) >> bit) & 1


def swap_bit(x, axis, bit):
    return lax.ppermute(x, axis, [(i, i ^ (1 << bit)) for i in range(lax.axis_size(axis))])


def halve(blocks, bits):
    sent = []
    for x, (axis, bit) in zip(blocks, bits):
        n = x.shape[0] // 2
        mine = bit_of(axis, bit)
        sent.append(swap_bit(lax.dynamic_slice_in_dim(x, (1 - mine) * n, n, 0), axis, bit))
    kept = []
    for x, s, (axis, bit) in zip(blocks, sent, bits):
        n = x.shape[0] // 2
        kept.append(lax.dynamic_slice_in_dim(x, bit_of(axis, bit) * n, n, 0) + s)
    return kept


def double(blocks, bits):
    came = [swap_bit(x, axis, bit) for x, (axis, bit) in zip(blocks, bits)]
    grown = []
    for x, s, (axis, bit) in zip(blocks, came, bits):
        mine = bit_of(axis, bit) == 1
        grown.append(jnp.concatenate([jnp.where(mine, s, x), jnp.where(mine, x, s)], axis=0))
    return grown


def bits_in(axis):
    count = lax.axis_size(axis)
    assert count & (count - 1) == 0
    return [(axis, b) for b in range(count.bit_length() - 1)]


def exchange_add(blocks, bits):
    came = [swap_bit(x, axis, bit) for x, (axis, bit) in zip(blocks, bits)]
    return [x + y for x, y in zip(blocks, came)]


def after(x, done):
    return lax.optimization_barrier((x, done))[0]


def per_device(fields, gain, w_qkv, w_out, cotangent):
    lat_dev, lon_dev, lev_dev = fields.shape[:3]
    assert lev_dev == 2 and lax.axis_size("lev") == 2 and lon_dev * lev_dev == 16
    tok = lat_dev * lon_dev * lev_dev
    low = lax.axis_index("lev") == 0
    r = LON_REACH
    edge = jnp.where(low, fields[:, :, 1], fields[:, :, 0])
    own = fields.reshape(lat_dev, 16, D)
    left_own = shift(own[:, 16 - 2 * r:], "lon", 1, True)
    right_own = shift(own[:, :2 * r], "lon", -1, True)
    left_far = shift_across(edge[:, lon_dev - r:], 1)
    right_far = shift_across(edge[:, :r], -1)
    far = swap_lev(edge)
    blank = jnp.zeros((lat_dev, SLAB - 24 - 6 * r, D), F32)
    mid = jnp.concatenate([own, far, left_own, right_own, left_far, right_far, blank], axis=1)
    top = shift(mid[lat_dev - LAT_REACH:], "lat", 1, False)
    bot = shift(mid[:LAT_REACH], "lat", -1, False)
    bias = jnp.asarray(window_bias(lat_dev, lon_dev, 512))
    lat_id, lev_id = lax.axis_index("lat"), lax.axis_index("lev")
    core = lat_id & 1
    pos = jnp.stack([
        core, lev_id * 2 + (lat_id == 0), 4 + lev_id * 2 + (lat_id == lax.axis_size("lat") - 1),
    ]).astype(jnp.int32)
    shared = (gain, w_qkv, w_out, cotangent.reshape(tok, D), bias)
    out, bn, g1 = attention(True, pos, top, mid, bot, *shared)
    (pair,), x_bits = bits_in("lat")[:1], bits_in("lat")[1:]
    y_bits, z_bits = bits_in("lev"), bits_in("lon")
    one = g1[1] + swap_bit(g1[0], *pair)
    mid = after(mid, one)
    out, btop, bmid, bbot, g2 = attention(False, pos, top, mid, bot, *shared, out, bn)
    two = g2[1] + swap_bit(g2[0], *pair)
    orders = [
        x_bits + y_bits + z_bits,
        x_bits + y_bits + z_bits,
        z_bits[:-1] + x_bits + y_bits + z_bits[-1:],
    ]
    stages = len(orders[0])
    (one,) = halve([one], [orders[0][0]])
    blocks = [one, two[:2 * D], two[2 * D:]]
    ahead = [1, 0, 0]
    marks = []
    for stage in range(stages - 1):
        live = [i for i in range(3) if stage + ahead[i] < stages - 1]
        new = halve([blocks[i] for i in live], [orders[i][stage + ahead[i]] for i in live])
        for i, x in zip(live, new):
            blocks[i] = x
        marks.append(new[-1])
    blocks = exchange_add(blocks, [order[-1] for order in orders])
    marks.append(blocks[-1])
    for stage in reversed(range(stages - 1)):
        blocks = double(blocks, [order[stage] for order in orders])
        marks.append(blocks[-1])
    one, two = blocks[0], jnp.concatenate(blocks[1:], axis=0)
    one_other, two_other = swap_bit(one, *pair), swap_bit(two, *pair)
    devices = lax.axis_size("lat") * lax.axis_size("lon") * lax.axis_size("lev")
    factor = (tok * devices) ** (-0.5)
    grad_gain, grad_qkv, grad_out = unpack(
        core.reshape(1).astype(jnp.int32), factor, (one, one_other, two, two_other)
    )
    grad_gain = grad_gain[:D // GROUP].reshape(D)
    btop, bbot = after((btop, bbot), marks[0])
    from_low = shift(bbot, "lat", 1, False)
    from_high = shift(btop, "lat", -1, False)
    rest = lat_dev - LAT_REACH
    back = bmid + jnp.pad(from_low, ((0, rest), (0, 0), (0, 0)))
    back = back + jnp.pad(from_high, ((rest, 0), (0, 0), (0, 0)))
    a = 24
    to_left = shift(back[:, a:a + 2 * r], "lon", -1, True)
    to_right = shift(back[:, a + 2 * r:a + 4 * r], "lon", 1, True)
    to_left_far = shift_across(back[:, a + 4 * r:a + 5 * r], -1)
    to_right_far = shift_across(back[:, a + 5 * r:a + 6 * r], 1)
    to_far = swap_lev(back[:, 16:24])
    total = back[:, :16]
    total = total + jnp.pad(to_left, ((0, 0), (16 - 2 * r, 0), (0, 0)))
    total = total + jnp.pad(to_right, ((0, 0), (0, 16 - 2 * r), (0, 0)))
    edge_sum = to_far + jnp.pad(to_left_far, ((0, 0), (lon_dev - r, 0), (0, 0)))
    edge_sum = edge_sum + jnp.pad(to_right_far, ((0, 0), (0, lon_dev - r), (0, 0)))
    at_edge = jnp.where(low, jnp.array([0.0, 1.0]), jnp.array([1.0, 0.0])).astype(F32)
    spread = edge_sum[:, :, None, :] * at_edge[None, None, :, None]
    back_normed = (total + spread.reshape(lat_dev, 16, D)).reshape(tok, D)
    x = fields.reshape(tok, D)
    inv_rms = lax.rsqrt(jnp.mean(x * x, axis=-1, keepdims=True) + EPSILON)
    gain_back = gain * back_normed
    grad_fields = cotangent.reshape(tok, D) + inv_rms * gain_back
    grad_fields = grad_fields - x * inv_rms**3 * jnp.mean(gain_back * x, axis=-1, keepdims=True)
    return (out.reshape(fields.shape), grad_fields.reshape(fields.shape), grad_gain, grad_qkv, grad_out)


def solution(mesh):
    cells = P("lat", "lon", "lev", None)
    return jax.shard_map(
        per_device, mesh=mesh, in_specs=(cells, P(), P(), P(), cells),
        out_specs=(cells, cells, P(), P(), P()), check_vma=False,
    )
```

profile of v0, /device:TPU:0, one launch (start us, length us, event | category | flops | bytes accessed | tf_op | source)
XLA Modules:
  0.0 175.0 jit_solution(7100754397018048665)
XLA Ops:
  1.9 5.1 %collective-permute-start.2 = (f32[8,6,512]{2,1,0:T(8,128)S(1)}, f32[8,6,512]{2,1,0:T(8,128)S(1)}, u32[]{:S(2)}, u32[]{:S(2)}) collective-permute-start(f32[8,6,512]{2,1,0:T(8,128)S(1)} %get-tuple-element.55), channel_id=1, source_target_pairs={{2,0},{4,2},{6,4},{0,6},{3,1},{5,3},{7,5},{1,7},{10,8},{12,10},{14... | collective-permute-start | bytes 294920 | tf_op jit(solution)/shard_map/ppermute | solution.py:302
  8.9 3.8 %collective-permute-start.4 = (f32[8,3,512]{2,1,0:T(4,128)S(1)}, f32[8,3,512]{2,1,0:T(4,128)S(1)}, u32[]{:S(2)}, u32[]{:S(2)}) collective-permute-start(f32[8,3,512]{2,1,0:T(4,128)S(1)} %get-tuple-element.63), channel_id=1, source_target_pairs={{0,7},{1,6},{2,1},{3,0},{4,3},{5,2},{6,5},{7,4},{8,15},{9,14},{10,... | collective-permute-start | bytes 147464 | tf_op jit(solution)/shard_map/ppermute | solution.py:311
  12.7 3.2 %collective-permute-done.4 = f32[8,3,512]{2,1,0:T(4,128)S(1)} collective-permute-done((f32[8,3,512]{2,1,0:T(4,128)S(1)}, f32[8,3,512]{2,1,0:T(4,128)S(1)}, u32[]{:S(2)}, u32[]{:S(2)}) %collective-permute-start.4) | collective-permute-done | bytes 49184 | tf_op jit(solution)/shard_map/ppermute | solution.py:311
  15.9 3.7 %collective-permute-done.3 = f32[8,3,512]{2,1,0:T(4,128)S(1)} collective-permute-done((f32[8,3,512]{2,1,0:T(4,128)S(1)}, f32[8,3,512]{2,1,0:T(4,128)S(1)}, u32[]{:S(2)}, u32[]{:S(2)}) %collective-permute-start.3) | collective-permute-done | bytes 49184 | tf_op jit(solution)/shard_map/ppermute | solution.py:311
  22.3 3.0 %collective-permute-start.5 = (f32[3,48,512]{2,1,0:T(8,128)S(1)}, f32[3,48,512]{2,1,0:T(8,128)S(1)}, u32[]{:S(2)}, u32[]{:S(2)}) collective-permute-start(f32[3,48,512]{2,1,0:T(8,128)S(1)} %get-tuple-element.42), channel_id=1, source_target_pairs={{0,8},{8,16},{16,24},{1,9},{9,17},{17,25},{2,10},{10,18},{18,26},{... | collective-permute-start | bytes 884744 | tf_op jit(solution)/shard_map/ppermute | solution.py:302
  26.5 19.7 %attention.2 = (f32[128,512]{1,0:T(8,128)S(1)}, f32[14,48,512]{2,1,0:T(8,128)S(1)}, f32[2,2048,128]{2,1,0:T(8,128)}) custom-call(s32[3]{0:T(128)S(1)} %pad_add_fusion.2.refs_0_, f32[3,48,512]{2,1,0:T(8,128)S(1)} %collective-permute-done.5.refs_1_, f32[8,48,512]{2,1,0:T(8,128)S(1)} %concatenate.27.refs_2_, f32[3,48,512]{2,1,0:T(8,128)S(1)} %collective-permute-done.6.refs_3_, ...), custom_call_target="tpu_custom_call" | custom-call | flops 8000000000 | bytes 16000000 | tf_op jit(solution)/shard_map/attention/pallas_call | solution.py:227
  47.4 2.4 %slice_bitcast_fusion.1 = f32[2048,128]{1,0:T(8,128)} fusion(f32[2,2048,128]{2,1,0:T(8,128)} %get-tuple-element.19), kind=kLoop, calls=%fused_computation.5 | loop fusion | bytes 2097152 | tf_op jit(solution)/shard_map/squeeze | solution.py:430
  49.7 3.6 %collective-permute-start.7 = (f32[2048,128]{1,0:T(8,128)}, f32[2048,128]{1,0:T(8,128)}, u32[]{:S(2)}, u32[]{:S(2)}) collective-permute-start(f32[2048,128]{1,0:T(8,128)} %slice_bitcast_fusion.1), channel_id=1, source_target_pairs={{0,8},{8,0},{16,24},{24,16},{1,9},{9,1},{17,25},{25,17},{2,10},{10... | collective-permute-start | bytes 3145736 | tf_op jit(solution)/shard_map/ppermute | solution.py:363
  53.3 2.6 %collective-permute-done.7 = f32[2048,128]{1,0:T(8,128)} collective-permute-done((f32[2048,128]{1,0:T(8,128)}, f32[2048,128]{1,0:T(8,128)}, u32[]{:S(2)}, u32[]{:S(2)}) %collective-permute-start.7) | collective-permute-done | bytes 1048608 | tf_op jit(solution)/shard_map/ppermute | solution.py:363
  57.6 2.8 %collective-permute-start.17 = (f32[1024,128]{1,0:T(8,128)S(1)}, f32[1024,128]{1,0:T(8,128)S(1)}, u32[]{:S(2)}, u32[]{:S(2)}) collective-permute-start(f32[1024,128]{1,0:T(8,128)S(1)} %constant_dynamic-slice_fusion.7), channel_id=1, source_target_pairs={{0,16},{8,24},{16,0},{24,8},{1,17},{9,25},{17,1},{25,9},{2,18},{10... | collective-permute-start | bytes 1572872 | tf_op jit(solution)/shard_map/ppermute | solution.py:363
  61.4 20.1 %attention.3 = (f32[128,512]{1,0:T(8,128)S(1)}, f32[3,48,512]{2,1,0:T(8,128)S(1)}, f32[8,48,512]{2,1,0:T(8,128)S(1)}, f32[3,48,512]{2,1,0:T(8,128)S(1)}, f32[2,2112,128]{2,1,0:T(8,128)}) custom-call(s32[3]{0:T(128)S(1)} %pad_add_fusion.2.refs_0_, f32[3,48,512]{2,1,0:T(8,128)S(1)} %copy-done.7, f32[8,48,512]{2,1,0:T(8,128)S(1)} %concatenate.27.refs_2_, ...), custom_call_target="tpu_custom_call" | custom-call | flops 8000000000 | bytes 16000000 | tf_op jit(solution)/shard_map/attention/pallas_call | solution.py:227
  84.0 2.3 %slice_bitcast_fusion = f32[2112,128]{1,0:T(8,128)} fusion(f32[2,2112,128]{2,1,0:T(8,128)} %get-tuple-element.27), kind=kLoop, calls=%fused_computation.2 | loop fusion | bytes 2162688 | tf_op jit(solution)/shard_map/squeeze | solution.py:433
  86.4 4.4 %collective-permute-done.18 = f32[512,128]{1,0:T(8,128)} collective-permute-done((f32[512,128]{1,0:T(8,128)}, f32[512,128]{1,0:T(8,128)}, u32[]{:S(2)}, u32[]{:S(2)}) %collective-permute-start.18) | collective-permute-done | bytes 262176 | tf_op jit(solution)/shard_map/ppermute | solution.py:363
  93.3 5.3 %collective-permute-done.19 = f32[256,128]{1,0:T(8,128)} collective-permute-done((f32[256,128]{1,0:T(8,128)}, f32[256,128]{1,0:T(8,128)}, u32[]{:S(2)}, u32[]{:S(2)}) %collective-permute-start.19) | collective-permute-done | bytes 131104 | tf_op jit(solution)/shard_map/ppermute | solution.py:363
  101.1 6.1 %collective-permute-done.20 = f32[256,128]{1,0:T(8,128)} collective-permute-done((f32[256,128]{1,0:T(8,128)}, f32[256,128]{1,0:T(8,128)}, u32[]{:S(2)}, u32[]{:S(2)}) %collective-permute-start.20) | collective-permute-done | bytes 131104 | tf_op jit(solution)/shard_map/ppermute | solution.py:363
  110.5 2.1 %collective-permute-start.9 = (f32[544,128]{1,0:T(8,128)S(1)}, f32[544,128]{1,0:T(8,128)S(1)}, u32[]{:S(2)}, u32[]{:S(2)}) collective-permute-start(f32[544,128]{1,0:T(8,128)S(1)} %constant_dynamic-slice_fusion.8), channel_id=1, source_target_pairs={{0,2},{2,0},{4,6},{6,4},{1,3},{3,1},{5,7},{7,5},{8,10},{10,8},{12,... | collective-permute-start | bytes 835592 | tf_op jit(solution)/shard_map/ppermute | solution.py:363
  112.5 2.1 %collective-permute-done.21 = f32[256,128]{1,0:T(8,128)S(1)} collective-permute-done((f32[256,128]{1,0:T(8,128)S(1)}, f32[256,128]{1,0:T(8,128)S(1)}, u32[]{:S(2)}, u32[]{:S(2)}) %collective-permute-start.21) | collective-permute-done | bytes 131104 | tf_op jit(solution)/shard_map/ppermute | solution.py:363
  130.0 4.4 %collective-permute-start.23 = (f32[1024,128]{1,0:T(8,128)S(1)}, f32[1024,128]{1,0:T(8,128)S(1)}, u32[]{:S(2)}, u32[]{:S(2)}) collective-permute-start(f32[1024,128]{1,0:T(8,128)S(1)} %pad_maximum_fusion.2), channel_id=1, source_target_pairs={{0,16},{8,24},{16,0},{24,8},{1,17},{9,25},{17,1},{25,9},{2,18},{10... | collective-permute-start | bytes 1572872 | tf_op jit(solution)/shard_map/ppermute | solution.py:363
  140.2 2.2 %collective-permute-start.16 = (f32[8,3,512]{2,1,0:T(4,128)S(1)}, f32[8,3,512]{2,1,0:T(4,128)S(1)}, u32[]{:S(2)}, u32[]{:S(2)}) collective-permute-start(f32[8,3,512]{2,1,0:T(4,128)S(1)} %get-tuple-element.40), channel_id=1, source_target_pairs={{0,3},{1,2},{2,5},{3,4},{4,7},{5,6},{6,1},{7,0},{8,11},{9,10},{10,... | collective-permute-start | bytes 147464 | tf_op jit(solution)/shard_map/ppermute | solution.py:311
  142.7 2.9 %collective-permute-start.12 = (f32[8,6,512]{2,1,0:T(8,128)}, f32[8,6,512]{2,1,0:T(8,128)}, u32[]{:S(2)}, u32[]{:S(2)}) collective-permute-start(f32[8,6,512]{2,1,0:T(8,128)} %get-tuple-element.37), channel_id=1, source_target_pairs={{2,0},{4,2},{6,4},{0,6},{3,1},{5,3},{7,5},{1,7},{10,8},{12,10},{14... | collective-permute-start | bytes 294920 | tf_op jit(solution)/shard_map/ppermute | solution.py:302
  156.5 3.5 %collective-permute-done.31 = f32[512,128]{1,0:T(8,128)S(1)} collective-permute-done((f32[512,128]{1,0:T(8,128)S(1)}, f32[512,128]{1,0:T(8,128)S(1)}, u32[]{:S(2)}, u32[]{:S(2)}) %collective-permute-start.31) | collective-permute-done | bytes 262176 | tf_op jit(solution)/shard_map/ppermute | solution.py:363
  160.0 2.7 %collective-permute-done.37 = f32[544,128]{1,0:T(8,128)S(1)} collective-permute-done((f32[544,128]{1,0:T(8,128)S(1)}, f32[544,128]{1,0:T(8,128)S(1)}, u32[]{:S(2)}, u32[]{:S(2)}) %collective-permute-start.37) | collective-permute-done | bytes 278560 | tf_op jit(solution)/shard_map/ppermute | solution.py:363
  168.6 2.0 %multiply_subtract_fusion = f32[8,8,2,512]{3,2,1,0:T(2,128)} fusion(f32[8,8,2,512]{3,2,1,0:T(2,128)S(1)} %copy-done.13, f32[8,8,2,512]{3,2,1,0:T(2,128)} %param.12, f32[8,8,2,512]{3,2,1,0:T(2,128)} %reshape.96, f32[8,8,2]{2,1,0:T(8,128)S(1)} %broadcast_multiply_fusion, f32[8,8,2]{2,1,0:T(8,128)S(1)} %get-tuple-element.66, f32[512]{0:T(512)S(1)} %copy-done, ...), kind=kLoop, calls=%fused_computation.18 | loop fusion | flops 393216 | bytes 1052160 | tf_op jit(solution)/shard_map/sub | solution.py:487
  170.7 3.8 %unpack.1 = (f32[8,128]{1,0:T(8,128)S(1)}, f32[512,1536]{1,0:T(8,128)}, f32[512,512]{1,0:T(8,128)}) custom-call(s32[1]{0:T(128)} %bitcast.refs_0_, f32[2048,128]{1,0:T(8,128)S(1)} %pad_maximum_fusion.1.refs_1_, f32[2048,128]{1,0:T(8,128)} %collective-permute-done.24.refs_2_, f32[2112,128]{1,0:T(8,128)S(1)} %pad_maximum_fusion.refs_3_, ...), custom_call_target="tpu_custom_call" | custom-call | flops 1000000 | bytes 8000000 | tf_op jit(solution)/shard_map/unpack/pallas_call | solution.py:281
  (171 shorter events, 59.9 us)
Async XLA Ops:
  1.9 17.8 %collective-permute-start.2 = (f32[8,6,512]{2,1,0:T(8,128)S(1)}, f32[8,6,512]{2,1,0:T(8,128)S(1)}, u32[]{:S(2)}, u32[]{:S(2)}) collective-permute-start(f32[8,6,512]{2,1,0:T(8,128)S(1)} %get-tuple-element.55), channel_id=1, source_target_pairs={{2,0},{4,2},{6,4},{0,6},{3,1},{5,3},{7,5},{1,7},{10,8},{12,10},{14... | collective-permute-start | bytes 294920 | tf_op jit(solution)/shard_map/ppermute | solution.py:302
  7.0 12.7 %collective-permute-start.1 = (f32[8,6,512]{2,1,0:T(8,128)S(1)}, f32[8,6,512]{2,1,0:T(8,128)S(1)}, u32[]{:S(2)}, u32[]{:S(2)}) collective-permute-start(f32[8,6,512]{2,1,0:T(8,128)S(1)} %get-tuple-element.56), channel_id=1, source_target_pairs={{0,2},{2,4},{4,6},{6,0},{1,3},{3,5},{5,7},{7,1},{8,10},{10,12},{12... | collective-permute-start | bytes 294920 | tf_op jit(solution)/shard_map/ppermute | solution.py:302
  7.3 12.4 %collective-permute-start = (f32[8,8,512]{2,1,0:T(8,128)S(1)}, f32[8,8,512]{2,1,0:T(8,128)S(1)}, u32[]{:S(2)}, u32[]{:S(2)}) collective-permute-start(f32[8,8,512]{2,1,0:T(8,128)S(1)} %fusion.2), channel_id=1, source_target_pairs={{0,1},{1,0},{2,3},{3,2},{4,5},{5,4},{6,7},{7,6},{8,9},{9,8},{10,11... | collective-permute-start | bytes 393224 | tf_op jit(solution)/shard_map/ppermute | solution.py:315
  8.9 7.0 %collective-permute-start.4 = (f32[8,3,512]{2,1,0:T(4,128)S(1)}, f32[8,3,512]{2,1,0:T(4,128)S(1)}, u32[]{:S(2)}, u32[]{:S(2)}) collective-permute-start(f32[8,3,512]{2,1,0:T(4,128)S(1)} %get-tuple-element.63), channel_id=1, source_target_pairs={{0,7},{1,6},{2,1},{3,0},{4,3},{5,2},{6,5},{7,4},{8,15},{9,14},{10,... | collective-permute-start | bytes 147464 | tf_op jit(solution)/shard_map/ppermute | solution.py:311
  12.7 7.0 %collective-permute-start.3 = (f32[8,3,512]{2,1,0:T(4,128)S(1)}, f32[8,3,512]{2,1,0:T(4,128)S(1)}, u32[]{:S(2)}, u32[]{:S(2)}) collective-permute-start(f32[8,3,512]{2,1,0:T(4,128)S(1)} %get-tuple-element.64), channel_id=1, source_target_pairs={{0,3},{1,2},{2,5},{3,4},{4,7},{5,6},{6,1},{7,0},{8,11},{9,10},{10,... | collective-permute-start | bytes 147464 | tf_op jit(solution)/shard_map/ppermute | solution.py:311
  57.6 23.9 %collective-permute-start.17 = (f32[1024,128]{1,0:T(8,128)S(1)}, f32[1024,128]{1,0:T(8,128)S(1)}, u32[]{:S(2)}, u32[]{:S(2)}) collective-permute-start(f32[1024,128]{1,0:T(8,128)S(1)} %constant_dynamic-slice_fusion.7), channel_id=1, source_target_pairs={{0,16},{8,24},{16,0},{24,8},{1,17},{9,25},{17,1},{25,9},{2,18},{10... | collective-permute-start | bytes 1572872 | tf_op jit(solution)/shard_map/ppermute | solution.py:363
  82.4 8.4 %collective-permute-start.18 = (f32[512,128]{1,0:T(8,128)}, f32[512,128]{1,0:T(8,128)}, u32[]{:S(2)}, u32[]{:S(2)}) collective-permute-start(f32[512,128]{1,0:T(8,128)} %constant_dynamic-slice_fusion.6), channel_id=1, source_target_pairs={{0,1},{1,0},{2,3},{3,2},{4,5},{5,4},{6,7},{7,6},{8,9},{9,8},{10,11... | collective-permute-start | bytes 786440 | tf_op jit(solution)/shard_map/ppermute | solution.py:363
  86.3 22.0 %collective-permute-start.8 = (f32[2112,128]{1,0:T(8,128)}, f32[2112,128]{1,0:T(8,128)}, u32[]{:S(2)}, u32[]{:S(2)}) collective-permute-start(f32[2112,128]{1,0:T(8,128)} %slice_bitcast_fusion), channel_id=1, source_target_pairs={{0,8},{8,0},{16,24},{24,16},{1,9},{9,1},{17,25},{25,17},{2,10},{10... | collective-permute-start | bytes 3244040 | tf_op jit(solution)/shard_map/ppermute | solution.py:363
  100.2 7.0 %collective-permute-start.20 = (f32[256,128]{1,0:T(8,128)}, f32[256,128]{1,0:T(8,128)}, u32[]{:S(2)}, u32[]{:S(2)}) collective-permute-start(f32[256,128]{1,0:T(8,128)} %dynamic-slice_add_fusion.6), channel_id=1, source_target_pairs={{0,4},{2,6},{4,0},{6,2},{1,5},{3,7},{5,1},{7,3},{8,12},{10,14},{12... | collective-permute-start | bytes 393224 | tf_op jit(solution)/shard_map/ppermute | solution.py:363
  110.5 8.6 %collective-permute-start.9 = (f32[544,128]{1,0:T(8,128)S(1)}, f32[544,128]{1,0:T(8,128)S(1)}, u32[]{:S(2)}, u32[]{:S(2)}) collective-permute-start(f32[544,128]{1,0:T(8,128)S(1)} %constant_dynamic-slice_fusion.8), channel_id=1, source_target_pairs={{0,2},{2,0},{4,6},{6,4},{1,3},{3,1},{5,7},{7,5},{8,10},{10,8},{12,... | collective-permute-start | bytes 835592 | tf_op jit(solution)/shard_map/ppermute | solution.py:363
  114.7 7.4 %collective-permute-start.22 = (f32[512,128]{1,0:T(8,128)S(1)}, f32[512,128]{1,0:T(8,128)S(1)}, u32[]{:S(2)}, u32[]{:S(2)}) collective-permute-start(f32[512,128]{1,0:T(8,128)S(1)} %pad_maximum_fusion.4), channel_id=1, source_target_pairs={{0,1},{1,0},{2,3},{3,2},{4,5},{5,4},{6,7},{7,6},{8,9},{9,8},{10,11... | collective-permute-start | bytes 786440 | tf_op jit(solution)/shard_map/ppermute | solution.py:363
  119.5 19.0 %collective-permute-start.10 = (f32[3,48,512]{2,1,0:T(8,128)S(1)}, f32[3,48,512]{2,1,0:T(8,128)S(1)}, u32[]{:S(2)}, u32[]{:S(2)}) collective-permute-start(f32[3,48,512]{2,1,0:T(8,128)S(1)} %copy-done.3), channel_id=1, source_target_pairs={{0,8},{8,16},{16,24},{1,9},{9,17},{17,25},{2,10},{10,18},{18,26},{... | collective-permute-start | bytes 884744 | tf_op jit(solution)/shard_map/ppermute | solution.py:302
  120.8 17.7 %collective-permute-start.11 = (f32[3,48,512]{2,1,0:T(8,128)S(1)}, f32[3,48,512]{2,1,0:T(8,128)S(1)}, u32[]{:S(2)}, u32[]{:S(2)}) collective-permute-start(f32[3,48,512]{2,1,0:T(8,128)S(1)} %get-tuple-element.29), channel_id=1, source_target_pairs={{8,0},{16,8},{24,16},{9,1},{17,9},{25,17},{10,2},{18,10},{26,18},{... | collective-permute-start | bytes 884744 | tf_op jit(solution)/shard_map/ppermute | solution.py:302
  126.9 8.2 %collective-permute-start.28 = (f32[128,128]{1,0:T(8,128)S(1)}, f32[128,128]{1,0:T(8,128)S(1)}, u32[]{:S(2)}, u32[]{:S(2)}) collective-permute-start(f32[128,128]{1,0:T(8,128)S(1)} %dynamic-slice_add_fusion.8), channel_id=1, source_target_pairs={{0,4},{2,6},{4,0},{6,2},{1,5},{3,7},{5,1},{7,3},{8,12},{10,14},{12... | collective-permute-start | bytes 196616 | tf_op jit(solution)/shard_map/ppermute | solution.py:363
  128.7 7.9 %collective-permute-start.34 = (f32[136,128]{1,0:T(8,128)S(1)}, f32[136,128]{1,0:T(8,128)S(1)}, u32[]{:S(2)}, u32[]{:S(2)}) collective-permute-start(f32[136,128]{1,0:T(8,128)S(1)} %dynamic-slice_add_fusion.7), channel_id=1, source_target_pairs={{0,4},{2,6},{4,0},{6,2},{1,5},{3,7},{5,1},{7,3},{8,12},{10,14},{12... | collective-permute-start | bytes 208904 | tf_op jit(solution)/shard_map/ppermute | solution.py:363
  130.0 26.2 %collective-permute-start.23 = (f32[1024,128]{1,0:T(8,128)S(1)}, f32[1024,128]{1,0:T(8,128)S(1)}, u32[]{:S(2)}, u32[]{:S(2)}) collective-permute-start(f32[1024,128]{1,0:T(8,128)S(1)} %pad_maximum_fusion.2), channel_id=1, source_target_pairs={{0,16},{8,24},{16,0},{24,8},{1,17},{9,25},{17,1},{25,9},{2,18},{10... | collective-permute-start | bytes 1572872 | tf_op jit(solution)/shard_map/ppermute | solution.py:363
  135.1 7.3 %collective-permute-start.29 = (f32[128,128]{1,0:T(8,128)S(1)}, f32[128,128]{1,0:T(8,128)S(1)}, u32[]{:S(2)}, u32[]{:S(2)}) collective-permute-start(f32[128,128]{1,0:T(8,128)S(1)} %add.189), channel_id=1, source_target_pairs={{0,2},{2,0},{4,6},{6,4},{1,3},{3,1},{5,7},{7,5},{8,10},{10,8},{12,... | collective-permute-start | bytes 196616 | tf_op jit(solution)/shard_map/ppermute | solution.py:363
  140.2 7.6 %collective-permute-start.16 = (f32[8,3,512]{2,1,0:T(4,128)S(1)}, f32[8,3,512]{2,1,0:T(4,128)S(1)}, u32[]{:S(2)}, u32[]{:S(2)}) collective-permute-start(f32[8,3,512]{2,1,0:T(4,128)S(1)} %get-tuple-element.40), channel_id=1, source_target_pairs={{0,3},{1,2},{2,5},{3,4},{4,7},{5,6},{6,1},{7,0},{8,11},{9,10},{10,... | collective-permute-start | bytes 147464 | tf_op jit(solution)/shard_map/ppermute | solution.py:311
  142.4 7.0 %collective-permute-start.14 = (f32[8,8,512]{2,1,0:T(8,128)S(1)}, f32[8,8,512]{2,1,0:T(8,128)S(1)}, u32[]{:S(2)}, u32[]{:S(2)}) collective-permute-start(f32[8,8,512]{2,1,0:T(8,128)S(1)} %slice.94), channel_id=1, source_target_pairs={{0,1},{1,0},{2,3},{3,2},{4,5},{5,4},{6,7},{7,6},{8,9},{9,8},{10,11... | collective-permute-start | bytes 393224 | tf_op jit(solution)/shard_map/ppermute | solution.py:315
  142.7 20.2 %collective-permute-start.12 = (f32[8,6,512]{2,1,0:T(8,128)}, f32[8,6,512]{2,1,0:T(8,128)}, u32[]{:S(2)}, u32[]{:S(2)}) collective-permute-start(f32[8,6,512]{2,1,0:T(8,128)} %get-tuple-element.37), channel_id=1, source_target_pairs={{2,0},{4,2},{6,4},{0,6},{3,1},{5,3},{7,5},{1,7},{10,8},{12,10},{14... | collective-permute-start | bytes 294920 | tf_op jit(solution)/shard_map/ppermute | solution.py:302
  145.7 17.2 %collective-permute-start.13 = (f32[8,6,512]{2,1,0:T(8,128)}, f32[8,6,512]{2,1,0:T(8,128)}, u32[]{:S(2)}, u32[]{:S(2)}) collective-permute-start(f32[8,6,512]{2,1,0:T(8,128)} %get-tuple-element.38), channel_id=1, source_target_pairs={{0,2},{2,4},{4,6},{6,0},{1,3},{3,5},{5,7},{7,1},{8,10},{10,12},{12... | collective-permute-start | bytes 294920 | tf_op jit(solution)/shard_map/ppermute | solution.py:302
  152.9 7.1 %collective-permute-start.31 = (f32[512,128]{1,0:T(8,128)S(1)}, f32[512,128]{1,0:T(8,128)S(1)}, u32[]{:S(2)}, u32[]{:S(2)}) collective-permute-start(f32[512,128]{1,0:T(8,128)S(1)} %pad_maximum_fusion.5), channel_id=1, source_target_pairs={{0,16},{8,24},{16,0},{24,8},{1,17},{9,25},{17,1},{25,9},{2,18},{10... | collective-permute-start | bytes 786440 | tf_op jit(solution)/shard_map/ppermute | solution.py:363
  156.4 14.3 %collective-permute-start.24 = (f32[2048,128]{1,0:T(8,128)S(1)}, f32[2048,128]{1,0:T(8,128)}, u32[]{:S(2)}, u32[]{:S(2)}) collective-permute-start(f32[2048,128]{1,0:T(8,128)S(1)} %pad_maximum_fusion.1.refs_1_), channel_id=1, source_target_pairs={{0,8},{8,0},{16,24},{24,16},{1,9},{9,1},{17,25},{25,17},{2,10},{10... | collective-permute-start | bytes 3145736 | tf_op jit(solution)/shard_map/ppermute | solution.py:363
  162.8 7.9 %collective-permute-start.38 = (f32[2112,128]{1,0:T(8,128)S(1)}, f32[2112,128]{1,0:T(8,128)S(1)}, u32[]{:S(2)}, u32[]{:S(2)}) collective-permute-start(f32[2112,128]{1,0:T(8,128)S(1)} %pad_maximum_fusion.refs_3_), channel_id=1, source_target_pairs={{0,8},{8,0},{16,24},{24,16},{1,9},{9,1},{17,25},{25,17},{2,10},{10... | collective-permute-start | bytes 3244040 | tf_op jit(solution)/shard_map/ppermute | solution.py:363
  (36 other events, 250.5 us)
where the time goes:
time: 176 us; the launch traced here: 175 us
  starting transfers between devices  53.4 us (30%)
  waiting for transfers between devices  45.8 us (26%)
  Pallas kernels  43.6 us (25%)
  local copies, waits for them, and re-layouts  18.1 us (10%)
  other arithmetic  12.9 us (7%)
    pallas_call x2, Pallas kernels, attention(): pl.pallas_call(body, grid_spec=pltpu.PrefetchScalarGridSpec(num_scalar_pr...  39.8 us
    ppermute x25, waiting for transfers between devices, swap_bit(): lax.ppermute(x, axis, [(i, i ^ 1 << bit) for i in range(lax.axis_size(axi...  36 us
    ppermute x25, starting transfers between devices, swap_bit(): lax.ppermute(x, axis, [(i, i ^ 1 << bit) for i in range(lax.axis_size(axi...  29.6 us
    ppermute x8, starting transfers between devices, shift(): return lax.ppermute(x, axis, pairs)  15.2 us
    ppermute x4, waiting for transfers between devices, shift_across(): return lax.ppermute(x, ('lon', 'lev'), pairs)  8.85 us
    ppermute x4, starting transfers between devices, shift_across(): return lax.ppermute(x, ('lon', 'lev'), pairs)  6.8 us
    pallas_call x1, Pallas kernels, unpack(): pl.pallas_call(lambda *refs: unpack_kernel(factor, *refs), in_specs=[pl.B...  3.79 us
    unnamed x42, local copies, waits for them, and re-layouts  3.6 us
  transfers between devices with their start and end apart: 39, of which 20 were waited for; matrix products, arithmetic and copies ran while one was open for 11% of the time, Pallas kernels for 11%

commit v1 on v0

v1 whole, which is shorter than its diff:
```python
import jax
import jax.numpy as jnp
import numpy as np
from jax import lax
from jax.experimental import pallas as pl
from jax.experimental.pallas import tpu as pltpu
from jax.sharding import PartitionSpec as P

D = 512
HEADS = 16
HEAD_DIM = 32
LAT_REACH = 3
LON_REACH = 3
LEV_REACH = 1
EPSILON = 1e-06
GROUP = 128
SLAB = 48
TAIL = 64
NEVER = -1e30
F32 = jnp.float32
BF16 = jnp.bfloat16


def split(x):
    high = x.astype(BF16)
    return high, (x - high.astype(F32)).astype(BF16)


def split3(x):
    high = x.astype(BF16)
    rest = x - high.astype(F32)
    middle = rest.astype(BF16)
    return high, middle, (rest - middle.astype(F32)).astype(BF16)


def dot(a, b, ca=1, cb=0):
    return lax.dot_general(a, b, (((ca,), (cb,)), ((), ())), preferred_element_type=F32)


def dot3(a, b, ca=1, cb=0):
    (ah, al), (bh, bl) = a, b
    return dot(ah, bh, ca, cb) + dot(ah, bl, ca, cb) + dot(al, bh, ca, cb)


def left6(parts, axis=1):
    h, m, l = parts
    return jnp.concatenate([h, h, m, m, h, l], axis=axis)


def right6(parts, axis=0):
    h, m, l = parts
    return jnp.concatenate([h, m, h, m, l, h], axis=axis)


def left3(parts, axis=1):
    return jnp.concatenate([parts[0], parts[0], parts[1]], axis=axis)


def right3(parts, axis=0):
    return jnp.concatenate([parts[0], parts[1], parts[0]], axis=axis)


def attention_kernel(
    first, pos_ref, top_ref, mid_ref, bot_ref, gain_ref, wq_ref, wk_ref, wv_ref, wo_ref, cot_ref,
    bias0_ref, bias1_ref, *refs,
):
    if not first:
        out0_ref, bn0_ref, *refs = refs
    if first:
        out_ref, bn_ref, send_ref, keep_ref, *refs = refs
    else:
        out_ref, btop_ref, bmid_ref, bbot_ref, send_ref, keep_ref, *refs = refs
    x_s, n_s, nt_s, own_s, ot_s, c_s, bn_s, dkv_s, k_s, v_s, g_s, sems = refs
    step = pl.program_id(0)
    last = pl.num_programs(0) - 1
    rows = x_s.shape[0]
    lats = rows // SLAB
    mid_lats = mid_ref.shape[0]
    tok = mid_lats * 16
    half_tok = tok // 2
    scale = HEAD_DIM ** (-0.5)
    padded = dkv_s.shape[0]

    def own_rows(x):
        return x.reshape(lats, SLAB, D)[LAT_REACH:LAT_REACH + mid_lats, :16].reshape(tok, D)

    @pl.when(step == 0)
    def _():
        x = jnp.concatenate([top_ref[...], mid_ref[...], bot_ref[...]], axis=0).reshape(rows, D)
        x_s[...] = x
        inv = lax.rsqrt(jnp.mean(x * x, axis=-1, keepdims=True) + EPSILON)
        normed = x * inv * gain_ref[...]
        parts = split3(normed)
        for i, j in enumerate((0, 0, 1, 1, 0, 2)):
            n_s[:, i * D:(i + 1) * D] = parts[j]
            own_s[:, i * D:(i + 1) * D] = own_rows(parts[j])
        pad = jnp.zeros((padded - rows, D), F32)
        parts = split(jnp.concatenate([normed, pad], axis=0).T)
        for i, j in enumerate((0, 0, 1)):
            nt_s[:, i * padded:(i + 1) * padded] = parts[j]
        parts = split(own_rows(normed).T)
        for i, j in enumerate((0, 0, 1)):
            ot_s[:, i * tok:(i + 1) * tok] = parts[j]
        c_s[...] = left6(split3(cot_ref[...]))
        if first:
            bn_s[...] = jnp.zeros(bn_s.shape, F32)
            out_ref[...] = mid_ref[...][:, :16].reshape(tok, D)
        else:
            bn_s[...] = bn0_ref[...].reshape(rows, D)
            out_ref[...] = out0_ref[...]

    wq = split3(wq_ref[...])
    wkv = split3(jnp.concatenate([wk_ref[...], wv_ref[...]], axis=1))
    wo = split3(wo_ref[...])
    kv = dot(n_s[...], right6(wkv))
    k_s[...] = left6(split3(kv[:, :GROUP]))
    v_s[...] = left6(split3(kv[:, GROUP:]))
    q_t = (dot(own_s[...], right6(wq)) * scale).T
    b_t = dot(c_s[...], right6(wo, 1), 1, 1).T
    dkv_s[...] = jnp.zeros(dkv_s.shape, F32)
    heads = GROUP // HEAD_DIM
    cols = heads * half_tok
    head_row = lax.broadcasted_iota(jnp.int32, (GROUP, cols), 0) // HEAD_DIM
    head_col = lax.broadcasted_iota(jnp.int32, (GROUP, cols), 1) // half_tok
    same = head_row == head_col
    keys = bias0_ref.shape[1]

    def spread(x):
        return jnp.where(same, jnp.concatenate([x] * heads, axis=1), 0.0)

    def gather(x):
        x = jnp.where(same, x, 0.0)
        y = x[:, :half_tok]
        for h in range(1, heads):
            y = y + x[:, h * half_tok:(h + 1) * half_tok]
        return y

    mixed_parts, dq_parts = [], []
    for half in range(2):
        lo_row = half * (rows - keys)
        here = slice(lo_row, lo_row + keys)
        q_cols = spread(q_t[:, half * half_tok:(half + 1) * half_tok])
        b_cols = spread(b_t[:, half * half_tok:(half + 1) * half_tok])
        bias = (bias0_ref, bias1_ref)[half][0]
        s = dot(k_s[here, :], right6(split3(q_cols)))
        s = s + jnp.concatenate([bias] * (cols // bias.shape[1]), axis=1)
        p = jnp.exp(s - jnp.max(s, axis=0, keepdims=True))
        inv_sum = 1.0 / jnp.sum(p, axis=0, keepdims=True)
        p_hi, p_lo = split(p)
        kcat_t = k_s[here, GROUP:3 * GROUP].T
        vcat_t = v_s[here, GROUP:3 * GROUP].T
        m2 = dot(vcat_t, p_hi)
        mixed_parts.append(gather((m2[:GROUP] + m2[GROUP:] + dot(vcat_t[:GROUP], p_lo)) * inv_sum))
        b_cols = b_cols * inv_sum
        dp = dot(v_s[here, :], right6(split3(b_cols)))
        agreement = jnp.sum(p * dp, axis=0, keepdims=True) * inv_sum
        ds = p * (dp - agreement)
        ds_hi, ds_lo = split(ds)
        dq2 = dot(kcat_t, ds_hi)
        dq_parts.append(gather(dq2[:GROUP] + dq2[GROUP:] + dot(kcat_t[:GROUP], ds_lo)))
        q_rows = split(q_cols.T)
        b_rows = split(b_cols.T)
        dk2 = dot(ds_hi, jnp.concatenate(q_rows, axis=1))
        dk = dk2[:, :GROUP] + dk2[:, GROUP:] + dot(ds_lo, q_rows[0])
        dv2 = dot(p_hi, jnp.concatenate(b_rows, axis=1))
        dv = dv2[:, :GROUP] + dv2[:, GROUP:] + dot(p_lo, b_rows[0])
        dkv_s[here, :GROUP] += dk
        dkv_s[here, GROUP:] += dv
    mixed_t = jnp.concatenate(mixed_parts, axis=1)
    dq = split((jnp.concatenate(dq_parts, axis=1) * scale).T)
    out_ref[...] += dot(left3(split(mixed_t.T)), right3(wo))
    cot = (c_s[:, :D], c_s[:, 2 * D:3 * D])
    gwo = dot(left3(split(mixed_t)), right3(cot))
    gq = dot(ot_s[...], right3(dq))
    dkv = split(dkv_s[...])
    gkv = dot(nt_s[...], right3(dkv))
    g_s[step, 0:D, :] = gq
    g_s[step, D:2 * D, :] = gkv[:, :GROUP]
    g_s[step, 2 * D:3 * D, :] = gkv[:, GROUP:]
    for j in range(D // GROUP):
        g_s[step, 3 * D + j * GROUP:3 * D + (j + 1) * GROUP, :] = gwo[:, j * GROUP:(j + 1) * GROUP]
    if not first:
        g_s[step, 4 * D:, :] = jnp.zeros((TAIL, GROUP), F32)
    send_copy = pltpu.make_async_copy(g_s.at[0], send_ref, sems.at[0])
    keep_copy = pltpu.make_async_copy(g_s.at[1], keep_ref, sems.at[1])

    @pl.when(step == 0)
    def _():
        send_copy.start()

    bn_s[...] += dot(left3((dkv[0][:rows], dkv[1][:rows])), right3(wkv, 1), 1, 1)
    back_q = dot(left3(dq), right3(wq, 1), 1, 1)
    for i in range(mid_lats):
        at = (LAT_REACH + i) * SLAB
        bn_s[at:at + 16, :] += back_q[i * 16:(i + 1) * 16]

    @pl.when(step == last)
    def _():
        bn3 = bn_s[...].reshape(lats, SLAB, D)
        if first:
            bn_ref[...] = bn3
        else:
            btop_ref[...] = bn3[:LAT_REACH]
            bbot_ref[...] = bn3[LAT_REACH + mid_lats:]
            bmid_ref[...] = bn3[LAT_REACH:LAT_REACH + mid_lats]
            x = x_s[...]
            inv = lax.rsqrt(jnp.mean(x * x, axis=-1, keepdims=True) + EPSILON)
            unit = x * inv
            gg = jnp.sum(bn_s[...] * unit, axis=0, keepdims=True)
            for j in range(D // GROUP):
                g_s[1, 4 * D + j:4 * D + j + 1, :] = gg[:, j * GROUP:(j + 1) * GROUP]
        keep_copy.start()
        send_copy.wait()
        keep_copy.wait()


def attention(first, pos, top, mid, bot, gain, w_qkv, w_out, cot, bias, *before):
    mid_lats = mid.shape[0]
    lats = mid_lats + 2 * LAT_REACH
    rows = lats * SLAB
    tok = mid_lats * 16
    padded = -(-rows // 256) * 256
    groups = D // GROUP
    whole = lambda *shape: pl.BlockSpec(shape, lambda s, pos: (0,) * len(shape))
    slab = lambda n: whole(n, SLAB, D)
    like = lambda *shape: jax.ShapeDtypeStruct(shape, F32)
    base = 0 if first else 2
    group = lambda s, pos: base + (1 - pos[0]) * (1 - s) + pos[0] * s
    outs, out_specs = [like(tok, D)], [whole(tok, D)]
    tail = 0 if first else TAIL
    if first:
        outs.append(like(lats, SLAB, D))
        out_specs.append(slab(lats))
    else:
        for n in (LAT_REACH, mid_lats, LAT_REACH):
            outs.append(like(n, SLAB, D))
            out_specs.append(slab(n))
    for _ in range(2):
        outs.append(like(4 * D + tail, GROUP))
        out_specs.append(pl.BlockSpec(memory_space=pl.ANY))
    body = lambda *refs: attention_kernel(first, *refs)
    return pl.pallas_call(
        body,
        grid_spec=pltpu.PrefetchScalarGridSpec(
            num_scalar_prefetch=1,
            grid=(2,),
            in_specs=[
                slab(LAT_REACH), slab(mid_lats), slab(LAT_REACH), whole(1, D),
                pl.BlockSpec((D, GROUP), lambda s, pos: (0, group(s, pos))),
                pl.BlockSpec((D, GROUP), lambda s, pos: (0, groups + group(s, pos))),
                pl.BlockSpec((D, GROUP), lambda s, pos: (0, 2 * groups + group(s, pos))),
                pl.BlockSpec((GROUP, D), lambda s, pos: (group(s, pos), 0)),
                whole(tok, D),
                pl.BlockSpec((1,) + bias.shape[1:], lambda s, pos: (pos[1], 0, 0)),
                pl.BlockSpec((1,) + bias.shape[1:], lambda s, pos: (pos[2], 0, 0)),
            ] + [whole(*x.shape) for x in before],
            out_specs=out_specs,
            scratch_shapes=[
                pltpu.VMEM((rows, D), F32),
                pltpu.VMEM((rows, 6 * D), BF16), pltpu.VMEM((D, 3 * padded), BF16),
                pltpu.VMEM((tok, 6 * D), BF16), pltpu.VMEM((D, 3 * tok), BF16),
                pltpu.VMEM((tok, 6 * D), BF16),
                pltpu.VMEM((rows, D), F32), pltpu.VMEM((padded, 2 * GROUP), F32),
                pltpu.VMEM((rows, 6 * GROUP), BF16), pltpu.VMEM((rows, 6 * GROUP), BF16),
                pltpu.VMEM((2, 4 * D + tail, GROUP), F32), pltpu.SemaphoreType.DMA((2,)),
            ],
        ),
        out_shape=outs,
        compiler_params=pltpu.CompilerParams(vmem_limit_bytes=48 * 1024 * 1024),
        cost_estimate=pl.CostEstimate(flops=8_000_000_000, bytes_accessed=16_000_000, transcendentals=1_000_000),
        name="attention",
    )(pos, top, mid, bot, gain.reshape(1, D), w_qkv, w_qkv, w_qkv, w_out, cot, bias, bias, *before)


def unpack_kernel(factor, counts, core_ref, mine_ref, other_ref, gain_ref, qkv_ref, out_ref):
    groups = D // GROUP
    core = core_ref[0]
    nz, nx, ny = counts
    count = nz * nx * ny
    rows_a = 2 * D // count
    rows_b = (2 * D + TAIL) // count
    moves = [(0, 0, 0, 4 * D)]
    for i in range(count):
        at = 4 * D + i * (rows_a + rows_b)
        z, x, y = i // (nx * ny), i // ny % nx, i % ny
        moves.append((1, at, ((x * ny + y) * nz + z) * rows_a, rows_a))
        moves.append((1, at + rows_a, 2 * D + i * rows_b, rows_b))
    gain_at = {}
    for ref, keeper in ((mine_ref, core), (other_ref, 1 - core)):
        for k, at, to, size in moves:
            g = 2 * k + keeper
            stop = to + size
            while to < stop:
                tile = to // GROUP
                n = min(stop, (tile + 1) * GROUP) - to
                off = to - tile * GROUP
                j, part = divmod(tile, groups)
                if j < 3:
                    cols = pl.ds(pl.multiple_of((j * groups + g) * GROUP, GROUP), GROUP)
                    row = part * GROUP + off
                    qkv_ref[row:row + n, cols] = ref[at:at + n, :] * factor
                elif j == 3:
                    out_ref[g, off:off + n, part * GROUP:(part + 1) * GROUP] = ref[at:at + n, :] * factor
                else:
                    for row in range(n):
                        gain_at[to - 4 * D + row] = at + row
                to += n
                at += n
    for row in range(D // GROUP):
        at = gain_at[row]
        gain_ref[row:row + 1, :] = (mine_ref[at:at + 1, :] + other_ref[at:at + 1, :]) * factor


def unpack(core, factor, counts, mine, other):
    return pl.pallas_call(
        lambda *refs: unpack_kernel(factor, counts, *refs),
        in_specs=[pl.BlockSpec(memory_space=pltpu.SMEM)] + [pl.BlockSpec(memory_space=pltpu.VMEM)] * 2,
        out_specs=[pl.BlockSpec(memory_space=pltpu.VMEM)] * 3,
        out_shape=[
            jax.ShapeDtypeStruct((D // GROUP, GROUP), F32),
            jax.ShapeDtypeStruct((D, 3 * D), F32),
            jax.ShapeDtypeStruct((D // GROUP, GROUP, D), F32),
        ],
        compiler_params=pltpu.CompilerParams(vmem_limit_bytes=32 * 1024 * 1024),
        cost_estimate=pl.CostEstimate(flops=1_000_000, bytes_accessed=8_000_000, transcendentals=0),
        name="unpack",
    )(core, mine, other)


def shift(x, axis, step, closed):
    count = lax.axis_size(axis)
    ends = count if closed else count - 1
    pairs = [(i, (i + 1) % count) for i in range(ends)]
    if step < 0:
        pairs = [(j, i) for i, j in pairs]
    return lax.ppermute(x, axis, pairs)


def shift_across(x, step):
    count = lax.axis_size("lon")
    pairs = []
    for i in range(count):
        for e in range(2):
            pairs.append((i * 2 + e, ((i + step) % count) * 2 + 1 - e))
    return lax.ppermute(x, ("lon", "lev"), pairs)


def swap_lev(x):
    return lax.ppermute(x, "lev", [(0, 1), (1, 0)])


def window_bias(lat_dev, lon_dev, keys):
    left = np.arange(-LON_REACH, 0)
    right = np.arange(lon_dev, lon_dev + LON_REACH)
    lon = np.concatenate([
        np.repeat(np.arange(lon_dev), 2), np.arange(lon_dev), np.repeat(left, 2), left,
        np.repeat(right, 2), right,
    ])
    level = np.concatenate([
        np.tile([0, 1], lon_dev), np.full(lon_dev, 2), np.tile([0, 1], LON_REACH),
        np.full(LON_REACH, 2), np.tile([0, 1], LON_REACH), np.full(LON_REACH, 2),
    ])
    unused = SLAB - lon.shape[0]
    lon = np.concatenate([lon, np.full(unused, 1000)])
    level = np.concatenate([level, np.full(unused, 0)])
    lats = lat_dev + 2 * LAT_REACH
    rows = lats * SLAB
    lat = np.repeat(np.arange(lats) - LAT_REACH, SLAB)[:, None]
    lon = np.tile(lon, lats)[:, None]
    level = np.tile(level, lats)[:, None]
    q_lat = np.repeat(np.arange(lat_dev), lon_dev * 2)
    q_lon = np.tile(np.repeat(np.arange(lon_dev), 2), lat_dev)
    q_level = np.tile([0, 1], lat_dev * lon_dev)
    near = (np.abs(lat - q_lat) <= LAT_REACH) & (np.abs(lon - q_lon) <= LON_REACH)
    half = q_lat.shape[0] // 2
    table = []
    for part in range(2):
        first = part * (rows - keys)
        ks = slice(first, first + keys)
        qs = np.tile(np.arange(part * half, (part + 1) * half), 2)
        for side in range(2):
            lev_k = np.where(level == 2, 2 - side, side * 2 + level)
            seen = near & (np.abs(lev_k - (side * 2 + q_level)) <= LEV_REACH)
            for edge in range(2):
                kept = seen
                if edge == 1:
                    kept = seen & ((lat >= 0) if part == 0 else (lat < lat_dev))
                table.append(np.where(kept[ks][:, qs], 0.0, NEVER))
    return np.stack(table).astype(np.float32)


def bit_of(axis, bit):
    return (lax.axis_index(axis) >> bit) & 1


def swap_bit(x, axis, bit):
    return lax.ppermute(x, axis, [(i, i ^ (1 << bit)) for i in range(lax.axis_size(axis))])


def halve(blocks, bits):
    def half(block, which):
        terms, start, size = block
        n = size // 2
        return sum(lax.dynamic_slice_in_dim(x, start + which * n, n, 0) for x in terms)

    mine = [bit_of(*bit) for bit in bits]
    given = [half(x, 1 - m) for x, m in zip(blocks, mine)]
    came = [swap_bit(x, *bit) for x, bit in zip(given, bits)]
    if len(came) > 1:
        came = [after(x, given) for x in came]
    kept = [((half(x, m) + s,), 0, s.shape[0]) for x, m, s in zip(blocks, mine, came)]
    return kept, given, came


def double(blocks, bits):
    came = [after(swap_bit(x, *bit), blocks) for x, bit in zip(blocks, bits)]
    grown = []
    for x, s, (axis, bit) in zip(blocks, came, bits):
        mine = bit_of(axis, bit) == 1
        grown.append([jnp.where(mine, s, x), jnp.where(mine, x, s)])
    return grown


def bits_in(axis):
    count = lax.axis_size(axis)
    assert count & (count - 1) == 0
    return [(axis, b) for b in range(count.bit_length() - 1)]


def after(x, done):
    return lax.optimization_barrier((x, done))[0]


def fold(bmid, from_low, from_high, low):
    r = LON_REACH
    lat_dev = bmid.shape[0]
    lon_dev = 8
    rest = lat_dev - LAT_REACH
    back = bmid + jnp.pad(from_low, ((0, rest), (0, 0), (0, 0)))
    back = back + jnp.pad(from_high, ((rest, 0), (0, 0), (0, 0)))
    low_at, high_at = 24, 24 + 3 * r
    to_left = shift(back[:, low_at:high_at], "lon", -1, True)
    to_right = shift(back[:, high_at:high_at + 3 * r], "lon", 1, True)
    total = back[:, :16]
    total = total + jnp.pad(to_left[:, :2 * r], ((0, 0), (16 - 2 * r, 0), (0, 0)))
    total = total + jnp.pad(to_right[:, :2 * r], ((0, 0), (0, 16 - 2 * r), (0, 0)))
    other = back[:, 16:24] + jnp.pad(to_left[:, 2 * r:], ((0, 0), (lon_dev - r, 0), (0, 0)))
    other = other + jnp.pad(to_right[:, 2 * r:], ((0, 0), (0, lon_dev - r), (0, 0)))
    edge_sum = swap_lev(other)
    at_edge = jnp.where(low, jnp.array([0.0, 1.0]), jnp.array([1.0, 0.0])).astype(F32)
    spread = edge_sum[:, :, None, :] * at_edge[None, None, :, None]
    return total + spread.reshape(lat_dev, 16, D), to_left, to_right, edge_sum


def per_device(fields, gain, w_qkv, w_out, cotangent):
    lat_dev, lon_dev, lev_dev = fields.shape[:3]
    assert lev_dev == 2 and lax.axis_size("lev") == 2 and lon_dev * lev_dev == 16
    tok = lat_dev * lon_dev * lev_dev
    low = lax.axis_index("lev") == 0
    r = LON_REACH
    edge = jnp.where(low, fields[:, :, 1], fields[:, :, 0])
    own = fields.reshape(lat_dev, 16, D)
    left_own = shift(own[:, 16 - 2 * r:], "lon", 1, True)
    right_own = shift(own[:, :2 * r], "lon", -1, True)
    left_far = shift_across(edge[:, lon_dev - r:], 1)
    right_far = shift_across(edge[:, :r], -1)
    far = swap_lev(edge)
    blank = jnp.zeros((lat_dev, SLAB - 24 - 6 * r, D), F32)
    mid = jnp.concatenate([own, far, left_own, left_far, right_own, right_far, blank], axis=1)
    top = shift(mid[lat_dev - LAT_REACH:], "lat", 1, False)
    bot = shift(mid[:LAT_REACH], "lat", -1, False)
    bias = jnp.asarray(window_bias(lat_dev, lon_dev, 512))
    lat_id, lev_id = lax.axis_index("lat"), lax.axis_index("lev")
    core = lat_id & 1
    pos = jnp.stack([
        core, lev_id * 2 + (lat_id == 0), 4 + lev_id * 2 + (lat_id == lax.axis_size("lat") - 1),
    ]).astype(jnp.int32)
    shared = (gain, w_qkv, w_out, cotangent.reshape(tok, D), bias)
    out, bn, send, keep = attention(True, pos, top, mid, bot, *shared)
    (pair,), x_bits = bits_in("lat")[:1], bits_in("lat")[1:]
    y_bits, z_bits = bits_in("lev"), bits_in("lon")
    zh_bits = z_bits[:-1]
    orders = [x_bits + y_bits + zh_bits, x_bits + y_bits + zh_bits, zh_bits + x_bits + y_bits]
    stages = len(orders[0])
    (one,), (given,), (came,) = halve([((keep, swap_bit(send, *pair)), 0, 4 * D)], orders[0][:1])
    mid = after(mid, given)
    out, btop, bmid, bbot, send, keep = attention(False, pos, top, mid, bot, *shared, out, bn)
    from_low = shift(bbot, "lat", 1, False)
    from_high = shift(btop, "lat", -1, False)
    two = (keep, swap_bit(after(send, came), *pair))
    blocks = [one, (two, 0, 2 * D), (two, 2 * D, 2 * D + TAIL)]
    for stage in range(stages):
        bits = [order[stage] for order in orders[1:]]
        if stage + 1 < stages:
            blocks, _, _ = halve(blocks, [orders[0][stage + 1]] + bits)
        else:
            blocks[1:], _, _ = halve(blocks[1:], bits)
    size = blocks[0][2]
    every = jnp.concatenate([x[0][0] for x in blocks], axis=0)
    every = every + swap_bit(every, *z_bits[-1])
    every, from_low, from_high = lax.optimization_barrier((every, from_low, from_high))
    back_normed, to_left, to_right, edge_sum = fold(bmid, from_low, from_high, low)
    blocks = [every[:size], every[size:]]
    for stage in reversed(range(stages)):
        if stage == 0:
            blocks[1] = after(blocks[1], (to_left, to_right))
        parts = double(blocks, [orders[0][stage], orders[2][stage]])
        if stage > 0:
            blocks = [jnp.concatenate(x, axis=0) for x in parts]
    mine = after(jnp.concatenate(parts[0] + parts[1], axis=0), edge_sum)
    devices = lax.axis_size("lat") * lax.axis_size("lon") * lax.axis_size("lev")
    factor = (tok * devices) ** (-0.5)
    counts = tuple(1 << len(bits) for bits in (zh_bits, x_bits, y_bits))
    grad_gain, grad_qkv, grad_out = unpack(
        core.reshape(1).astype(jnp.int32), factor, counts,
        mine, swap_bit(mine, *pair),
    )
    grad_gain, grad_out = grad_gain.reshape(D), grad_out.reshape(D, D)
    back_normed = back_normed.reshape(tok, D)
    x = fields.reshape(tok, D)
    inv_rms = lax.rsqrt(jnp.mean(x * x, axis=-1, keepdims=True) + EPSILON)
    gain_back = gain * back_normed
    grad_fields = cotangent.reshape(tok, D) + inv_rms * gain_back
    grad_fields = grad_fields - x * inv_rms**3 * jnp.mean(gain_back * x, axis=-1, keepdims=True)
    return (out.reshape(fields.shape), grad_fields.reshape(fields.shape), grad_gain, grad_qkv, grad_out)


def solution(mesh):
    cells = P("lat", "lon", "lev", None)
    return jax.shard_map(
        per_device, mesh=mesh, in_specs=(cells, P(), P(), P(), cells),
        out_specs=(cells, cells, P(), P(), P()), check_vma=False,
    )
```

time: 176 us -> 168 us (0.955)
  starting transfers between devices: 53.4 us -> 48.5 us
  other arithmetic: 12.9 us -> 10.5 us
  local copies, waits for them, and re-layouts: 18.1 us -> 15.8 us
    ppermute x4 -> x2, waiting for transfers between devices: 8.85 us -> 3.19 us  [shift_across(): return lax.ppermute(x, ('lon', 'lev'), pairs)]
    unnamed x42 -> x40, local copies, waits for them, and re-layouts: 3.6 us -> 8.4 us
    squeeze x2 -> x0, local copies, waits for them, and re-layouts: 4.69 us -> none  [the longest x1 2.36 us: per_device(): one = g1[1] + swap_bit(g1[0], *pair)]
    ppermute x25 -> x19, waiting for transfers between devices: 36 us -> 40.3 us  [swap_bit(): lax.ppermute(x, axis, [(i, i ^ 1 << bit) for i in range(lax.axis_size(axi...]
    ppermute x25 -> x19, starting transfers between devices: 29.6 us -> 25.7 us  [swap_bit(): lax.ppermute(x, axis, [(i, i ^ 1 << bit) for i in range(lax.axis_size(axi...]
    ppermute x2, starting transfers between devices: 1.8 us -> 5.14 us  [swap_lev(): return lax.ppermute(x, 'lev', [(0, 1), (1, 0)])]
    ppermute x8, waiting for transfers between devices: 0.89 us -> 3.6 us  [shift(): return lax.ppermute(x, axis, pairs)]
    ppermute x8, starting transfers between devices: 15.2 us -> 12.9 us  [shift(): return lax.ppermute(x, axis, pairs)]
  transfers between devices with their start and end apart: 39 -> 31, of which waited for: 20 -> 16; matrix products, arithmetic and copies ran while one was open for 11% -> 9% of each run, Pallas kernels for 11% -> 12%
where the time goes in v1:
time: 168 us
  starting transfers between devices  48.5 us (29%)
  waiting for transfers between devices  47.1 us (28%)
  Pallas kernels  44.3 us (26%)
  local copies, waits for them, and re-layouts  15.8 us (9%)
  other arithmetic  10.5 us (6%)
    ppermute x19, waiting for transfers between devices, swap_bit(): lax.ppermute(x, axis, [(i, i ^ 1 << bit) for i in range(lax.axis_size(axi...  40.3 us
    pallas_call x2, Pallas kernels, attention(): pl.pallas_call(body, grid_spec=pltpu.PrefetchScalarGridSpec(num_scalar_pr...  40.2 us
    ppermute x19, starting transfers between devices, swap_bit(): lax.ppermute(x, axis, [(i, i ^ 1 << bit) for i in range(lax.axis_size(axi...  25.7 us
    ppermute x8, starting transfers between devices, shift(): return lax.ppermute(x, axis, pairs)  12.9 us
    unnamed x40, local copies, waits for them, and re-layouts  8.4 us
    ppermute x2, starting transfers between devices, swap_lev(): return lax.ppermute(x, 'lev', [(0, 1), (1, 0)])  5.14 us
    ppermute x2, starting transfers between devices, shift_across(): return lax.ppermute(x, ('lon', 'lev'), pairs)  4.77 us
    add x9, other arithmetic, halve(): half(x, m) + s  4.34 us
  transfers between devices with their start and end apart: 31, of which 16 were waited for; matrix products, arithmetic and copies ran while one was open for 9% of the time, Pallas kernels for 12%

profile of v1, /device:TPU:0, one launch (start us, length us, event | category | flops | bytes accessed | tf_op | source)
XLA Modules:
  0.0 167.6 jit_solution(14541832877041911893)
XLA Ops:
  2.0 3.0 %collective-permute-start = (f32[8,8,512]{2,1,0:T(8,128)S(1)}, f32[8,8,512]{2,1,0:T(8,128)S(1)}, u32[]{:S(2)}, u32[]{:S(2)}) collective-permute-start(f32[8,8,512]{2,1,0:T(8,128)S(1)} %fusion.3), channel_id=1, source_target_pairs={{0,1},{1,0},{2,3},{3,2},{4,5},{5,4},{6,7},{7,6},{8,9},{9,8},{10,11... | collective-permute-start | bytes 393224 | tf_op jit(solution)/shard_map/ppermute | solution.py:349
  7.9 2.2 %collective-permute-start.3 = (f32[8,6,512]{2,1,0:T(8,128)S(1)}, f32[8,6,512]{2,1,0:T(8,128)S(1)}, u32[]{:S(2)}, u32[]{:S(2)}) collective-permute-start(f32[8,6,512]{2,1,0:T(8,128)S(1)} %get-tuple-element.91), channel_id=1, source_target_pairs={{2,0},{4,2},{6,4},{0,6},{3,1},{5,3},{7,5},{1,7},{10,8},{12,10},{14... | collective-permute-start | bytes 294920 | tf_op jit(solution)/shard_map/ppermute | solution.py:336
  10.2 4.7 %collective-permute-start.4 = (f32[8,3,512]{2,1,0:T(4,128)S(1)}, f32[8,3,512]{2,1,0:T(4,128)S(1)}, u32[]{:S(2)}, u32[]{:S(2)}) collective-permute-start(f32[8,3,512]{2,1,0:T(4,128)S(1)} %get-tuple-element.95), channel_id=1, source_target_pairs={{0,7},{1,6},{2,1},{3,0},{4,3},{5,2},{6,5},{7,4},{8,15},{9,14},{10,... | collective-permute-start | bytes 147464 | tf_op jit(solution)/shard_map/ppermute | solution.py:345
  14.9 3.1 %collective-permute-done.2 = f32[8,3,512]{2,1,0:T(4,128)S(1)} collective-permute-done((f32[8,3,512]{2,1,0:T(4,128)S(1)}, f32[8,3,512]{2,1,0:T(4,128)S(1)}, u32[]{:S(2)}, u32[]{:S(2)}) %collective-permute-start.2) | collective-permute-done | bytes 49184 | tf_op jit(solution)/shard_map/ppermute | solution.py:345
  22.3 3.6 %collective-permute-done.6.refs_3_ = f32[3,48,512]{2,1,0:T(8,128)S(1)} collective-permute-done((f32[3,48,512]{2,1,0:T(8,128)S(1)}, f32[3,48,512]{2,1,0:T(8,128)S(1)}, u32[]{:S(2)}, u32[]{:S(2)}) %collective-permute-start.6) | collective-permute-done | bytes 294944 | tf_op jit(solution)/shard_map/ppermute | solution.py:336
  27.6 19.7 %attention.2 = (f32[128,512]{1,0:T(8,128)S(1)}, f32[14,48,512]{2,1,0:T(8,128)}, f32[2048,128]{1,0:T(8,128)}, f32[2048,128]{1,0:T(8,128)S(1)}) custom-call(s32[3]{0:T(128)S(1)} %pad_add_fusion.1.refs_0_, f32[3,48,512]{2,1,0:T(8,128)S(1)} %collective-permute-done.5.refs_1_, f32[8,48,512]{2,1,0:T(8,128)S(1)} %concatenate.21.refs_2_, ...), custom_call_target="tpu_custom_call" | custom-call | flops 8000000000 | bytes 16000000 | tf_op jit(solution)/shard_map/attention/pallas_call | solution.py:242
  48.0 5.1 %collective-permute-start.7 = (f32[2048,128]{1,0:T(8,128)}, f32[2048,128]{1,0:T(8,128)S(1)}, u32[]{:S(2)}, u32[]{:S(2)}) collective-permute-start(f32[2048,128]{1,0:T(8,128)} %get-tuple-element.40), channel_id=1, source_target_pairs={{0,8},{8,0},{16,24},{24,16},{1,9},{9,1},{17,25},{25,17},{2,10},{10... | collective-permute-start | bytes 3145736 | tf_op jit(solution)/shard_map/ppermute | solution.py:397
  53.0 2.5 %collective-permute-done.7 = f32[2048,128]{1,0:T(8,128)S(1)} collective-permute-done((f32[2048,128]{1,0:T(8,128)}, f32[2048,128]{1,0:T(8,128)S(1)}, u32[]{:S(2)}, u32[]{:S(2)}) %collective-permute-start.7) | collective-permute-done | bytes 1048608 | tf_op jit(solution)/shard_map/ppermute | solution.py:397
  60.6 20.5 %attention.3 = (f32[128,512]{1,0:T(8,128)S(1)}, f32[3,48,512]{2,1,0:T(8,128)S(1)}, f32[8,48,512]{2,1,0:T(8,128)S(1)}, f32[3,48,512]{2,1,0:T(8,128)S(1)}, f32[2112,128]{1,0:T(8,128)}, /*index=5*/f32[2112,128]{1,0:T(8,128)}) custom-call(s32[3]{0:T(128)S(1)} %pad_add_fusion.1.refs_0_, f32[3,48,512]{2,1,0:T(8,128)S(1)} %copy-done.6, ...), custom_call_target="tpu_custom_call" | custom-call | flops 8000000000 | bytes 16000000 | tf_op jit(solution)/shard_map/attention/pallas_call | solution.py:242
  89.5 2.6 %collective-permute-done.9 = f32[512,128]{1,0:T(8,128)} collective-permute-done((f32[512,128]{1,0:T(8,128)S(1)}, f32[512,128]{1,0:T(8,128)}, u32[]{:S(2)}, u32[]{:S(2)}) %collective-permute-start.9) | collective-permute-done | bytes 262176 | tf_op jit(solution)/shard_map/ppermute | solution.py:397
  94.3 2.3 %collective-permute-done.12 = f32[512,128]{1,0:T(8,128)S(1)} collective-permute-done((f32[512,128]{1,0:T(8,128)S(1)}, f32[512,128]{1,0:T(8,128)S(1)}, u32[]{:S(2)}, u32[]{:S(2)}) %collective-permute-start.12) | collective-permute-done | bytes 262176 | tf_op jit(solution)/shard_map/ppermute | solution.py:397
  107.1 2.8 %collective-permute-done.17 = f32[136,128]{1,0:T(8,128)S(1)} collective-permute-done((f32[136,128]{1,0:T(8,128)S(1)}, f32[136,128]{1,0:T(8,128)S(1)}, u32[]{:S(2)}, u32[]{:S(2)}) %collective-permute-start.17) | collective-permute-done | bytes 69664 | tf_op jit(solution)/shard_map/ppermute | solution.py:397
  109.9 2.3 %collective-permute-start.18 = (f32[520,128]{1,0:T(8,128)S(1)}, f32[520,128]{1,0:T(8,128)S(1)}, u32[]{:S(2)}, u32[]{:S(2)}) collective-permute-start(f32[520,128]{1,0:T(8,128)S(1)} %pad_maximum_fusion.4), channel_id=1, source_target_pairs={{0,4},{2,6},{4,0},{6,2},{1,5},{3,7},{5,1},{7,3},{8,12},{10,14},{12... | collective-permute-start | bytes 798728 | tf_op jit(solution)/shard_map/ppermute | solution.py:397
  114.8 7.0 %collective-permute-done.18 = f32[520,128]{1,0:T(8,128)S(1)} collective-permute-done((f32[520,128]{1,0:T(8,128)S(1)}, f32[520,128]{1,0:T(8,128)S(1)}, u32[]{:S(2)}, u32[]{:S(2)}) %collective-permute-start.18) | collective-permute-done | bytes 266272 | tf_op jit(solution)/shard_map/ppermute | solution.py:397
  122.1 2.1 %collective-permute-start.22 = (f32[8,9,512]{2,1,0:T(8,128)S(1)}, f32[8,9,512]{2,1,0:T(8,128)S(1)}, u32[]{:S(2)}, u32[]{:S(2)}) collective-permute-start(f32[8,9,512]{2,1,0:T(8,128)S(1)} %get-tuple-element.80), channel_id=1, source_target_pairs={{0,2},{2,4},{4,6},{6,0},{1,3},{3,5},{5,7},{7,1},{8,10},{10,12},{12... | collective-permute-start | bytes 442376 | tf_op jit(solution)/shard_map/ppermute | solution.py:336
  124.2 1.8 %collective-permute-start.21 = (f32[8,9,512]{2,1,0:T(8,128)S(1)}, f32[8,9,512]{2,1,0:T(8,128)S(1)}, u32[]{:S(2)}, u32[]{:S(2)}) collective-permute-start(f32[8,9,512]{2,1,0:T(8,128)S(1)} %get-tuple-element.79), channel_id=1, source_target_pairs={{2,0},{4,2},{6,4},{0,6},{3,1},{5,3},{7,5},{1,7},{10,8},{12,10},{14... | collective-permute-start | bytes 442376 | tf_op jit(solution)/shard_map/ppermute | solution.py:336
  128.2 4.1 %collective-permute-done.26 = f32[264,128]{1,0:T(8,128)S(1)} collective-permute-done((f32[264,128]{1,0:T(8,128)S(1)}, f32[264,128]{1,0:T(8,128)S(1)}, u32[]{:S(2)}, u32[]{:S(2)}) %collective-permute-start.26) | collective-permute-done | bytes 135200 | tf_op jit(solution)/shard_map/ppermute | solution.py:397
  132.4 2.3 %collective-permute-start.28 = (f32[528,128]{1,0:T(8,128)S(1)}, f32[528,128]{1,0:T(8,128)S(1)}, u32[]{:S(2)}, u32[]{:S(2)}) collective-permute-start(f32[528,128]{1,0:T(8,128)S(1)} %pad_maximum_fusion.3), channel_id=1, source_target_pairs={{0,16},{8,24},{16,0},{24,8},{1,17},{9,25},{17,1},{25,9},{2,18},{10... | collective-permute-start | bytes 811016 | tf_op jit(solution)/shard_map/ppermute | solution.py:397
  135.2 5.6 %collective-permute-start.27 = (f32[1024,128]{1,0:T(8,128)S(1)}, f32[1024,128]{1,0:T(8,128)S(1)}, u32[]{:S(2)}, u32[]{:S(2)}) collective-permute-start(f32[1024,128]{1,0:T(8,128)S(1)} %pad_maximum_fusion.2), channel_id=1, source_target_pairs={{0,16},{8,24},{16,0},{24,8},{1,17},{9,25},{17,1},{25,9},{2,18},{10... | collective-permute-start | bytes 1572872 | tf_op jit(solution)/shard_map/ppermute | solution.py:397
  141.8 2.1 %collective-permute-start.23 = (f32[8,8,512]{2,1,0:T(8,128)S(1)}, f32[8,8,512]{2,1,0:T(8,128)S(1)}, u32[]{:S(2)}, u32[]{:S(2)}) collective-permute-start(f32[8,8,512]{2,1,0:T(8,128)S(1)} %fusion.2), channel_id=1, source_target_pairs={{0,1},{1,0},{2,3},{3,2},{4,5},{5,4},{6,7},{7,6},{8,9},{9,8},{10,11... | collective-permute-start | bytes 393224 | tf_op jit(solution)/shard_map/ppermute | solution.py:349
  144.0 9.3 %collective-permute-done.27 = f32[1024,128]{1,0:T(8,128)S(1)} collective-permute-done((f32[1024,128]{1,0:T(8,128)S(1)}, f32[1024,128]{1,0:T(8,128)S(1)}, u32[]{:S(2)}, u32[]{:S(2)}) %collective-permute-start.27) | collective-permute-done | bytes 524320 | tf_op jit(solution)/shard_map/ppermute | solution.py:397
  153.4 2.9 %collective-permute-done.29 = f32[1056,128]{1,0:T(8,128)S(1)} collective-permute-done((f32[1056,128]{1,0:T(8,128)S(1)}, f32[1056,128]{1,0:T(8,128)S(1)}, u32[]{:S(2)}, u32[]{:S(2)}) %collective-permute-start.29) | collective-permute-done | bytes 540704 | tf_op jit(solution)/shard_map/ppermute | solution.py:397
  159.2 1.8 %fusion.1 = f32[8,16,512]{2,1,0:T(8,128)} fusion(f32[8,48,512]{2,1,0:T(8,128)} %copy-done.13, f32[8,16,512]{2,1,0:T(8,128)S(1)} %mul.152, f32[8,6,512]{2,1,0:T(8,128)S(1)} %slice.82, f32[8,6,512]{2,1,0:T(8,128)S(1)} %slice.80, f32[16]{0:T(128)S(1)} %mul.154), kind=kLoop, calls=%fused_computation.14 | loop fusion | flops 262144 | bytes 983104 | tf_op jit(solution)/shard_map/add | solution.py:452
  163.4 4.2 %unpack.1 = (f32[4,128]{1,0:T(4,128)}, f32[512,1536]{1,0:T(8,128)}, f32[4,128,512]{2,1,0:T(8,128)}) custom-call(s32[1]{0:T(128)} %bitcast.refs_0_, f32[4160,128]{1,0:T(8,128)S(1)} %pad_maximum_fusion.refs_1_, f32[4160,128]{1,0:T(8,128)} %collective-permute-done.30.refs_2_), custom_call_target="tpu_custom_call" | custom-call | flops 1000000 | bytes 8000000 | tf_op jit(solution)/shard_map/unpack/pallas_call | solution.py:315
  (143 shorter events, 48.7 us)
Async XLA Ops:
  2.0 16.1 %collective-permute-start = (f32[8,8,512]{2,1,0:T(8,128)S(1)}, f32[8,8,512]{2,1,0:T(8,128)S(1)}, u32[]{:S(2)}, u32[]{:S(2)}) collective-permute-start(f32[8,8,512]{2,1,0:T(8,128)S(1)} %fusion.3), channel_id=1, source_target_pairs={{0,1},{1,0},{2,3},{3,2},{4,5},{5,4},{6,7},{7,6},{8,9},{9,8},{10,11... | collective-permute-start | bytes 393224 | tf_op jit(solution)/shard_map/ppermute | solution.py:349
  6.2 11.9 %collective-permute-start.1 = (f32[8,6,512]{2,1,0:T(8,128)S(1)}, f32[8,6,512]{2,1,0:T(8,128)S(1)}, u32[]{:S(2)}, u32[]{:S(2)}) collective-permute-start(f32[8,6,512]{2,1,0:T(8,128)S(1)} %get-tuple-element.92), channel_id=1, source_target_pairs={{0,2},{2,4},{4,6},{6,0},{1,3},{3,5},{5,7},{7,1},{8,10},{10,12},{12... | collective-permute-start | bytes 294920 | tf_op jit(solution)/shard_map/ppermute | solution.py:336
  7.9 10.2 %collective-permute-start.3 = (f32[8,6,512]{2,1,0:T(8,128)S(1)}, f32[8,6,512]{2,1,0:T(8,128)S(1)}, u32[]{:S(2)}, u32[]{:S(2)}) collective-permute-start(f32[8,6,512]{2,1,0:T(8,128)S(1)} %get-tuple-element.91), channel_id=1, source_target_pairs={{2,0},{4,2},{6,4},{0,6},{3,1},{5,3},{7,5},{1,7},{10,8},{12,10},{14... | collective-permute-start | bytes 294920 | tf_op jit(solution)/shard_map/ppermute | solution.py:336
  10.1 7.9 %collective-permute-start.2 = (f32[8,3,512]{2,1,0:T(4,128)S(1)}, f32[8,3,512]{2,1,0:T(4,128)S(1)}, u32[]{:S(2)}, u32[]{:S(2)}) collective-permute-start(f32[8,3,512]{2,1,0:T(4,128)S(1)} %get-tuple-element.96), channel_id=1, source_target_pairs={{0,3},{1,2},{2,5},{3,4},{4,7},{5,6},{6,1},{7,0},{8,11},{9,10},{10,... | collective-permute-start | bytes 147464 | tf_op jit(solution)/shard_map/ppermute | solution.py:345
  10.2 7.9 %collective-permute-start.4 = (f32[8,3,512]{2,1,0:T(4,128)S(1)}, f32[8,3,512]{2,1,0:T(4,128)S(1)}, u32[]{:S(2)}, u32[]{:S(2)}) collective-permute-start(f32[8,3,512]{2,1,0:T(4,128)S(1)} %get-tuple-element.95), channel_id=1, source_target_pairs={{0,7},{1,6},{2,1},{3,0},{4,3},{5,2},{6,5},{7,4},{8,15},{9,14},{10,... | collective-permute-start | bytes 147464 | tf_op jit(solution)/shard_map/ppermute | solution.py:345
  48.0 7.6 %collective-permute-start.7 = (f32[2048,128]{1,0:T(8,128)}, f32[2048,128]{1,0:T(8,128)S(1)}, u32[]{:S(2)}, u32[]{:S(2)}) collective-permute-start(f32[2048,128]{1,0:T(8,128)} %get-tuple-element.40), channel_id=1, source_target_pairs={{0,8},{8,0},{16,24},{24,16},{1,9},{9,1},{17,25},{25,17},{2,10},{10... | collective-permute-start | bytes 3145736 | tf_op jit(solution)/shard_map/ppermute | solution.py:397
  55.6 26.2 %collective-permute-start.8 = (f32[1024,128]{1,0:T(8,128)S(1)}, f32[1024,128]{1,0:T(8,128)}, u32[]{:S(2)}, u32[]{:S(2)}) collective-permute-start(f32[1024,128]{1,0:T(8,128)S(1)} %dynamic-slice_add_fusion), channel_id=1, source_target_pairs={{0,16},{8,24},{16,0},{24,8},{1,17},{9,25},{17,1},{25,9},{2,18},{10... | collective-permute-start | bytes 1572872 | tf_op jit(solution)/shard_map/ppermute | solution.py:397
  83.6 8.5 %collective-permute-start.9 = (f32[512,128]{1,0:T(8,128)S(1)}, f32[512,128]{1,0:T(8,128)}, u32[]{:S(2)}, u32[]{:S(2)}) collective-permute-start(f32[512,128]{1,0:T(8,128)S(1)} %constant_dynamic-slice_fusion.5), channel_id=1, source_target_pairs={{0,1},{1,0},{2,3},{3,2},{4,5},{5,4},{6,7},{7,6},{8,9},{9,8},{10,11... | collective-permute-start | bytes 786440 | tf_op jit(solution)/shard_map/ppermute | solution.py:397
  86.2 13.0 %collective-permute-start.13 = (f32[544,128]{1,0:T(8,128)S(1)}, f32[544,128]{1,0:T(8,128)S(1)}, u32[]{:S(2)}, u32[]{:S(2)}) collective-permute-start(f32[544,128]{1,0:T(8,128)S(1)} %dynamic-slice_add_fusion.1), channel_id=1, source_target_pairs={{0,2},{2,0},{4,6},{6,4},{1,3},{3,1},{5,7},{7,5},{8,10},{10,8},{12,... | collective-permute-start | bytes 835592 | tf_op jit(solution)/shard_map/ppermute | solution.py:397
  88.5 8.1 %collective-permute-start.12 = (f32[512,128]{1,0:T(8,128)S(1)}, f32[512,128]{1,0:T(8,128)S(1)}, u32[]{:S(2)}, u32[]{:S(2)}) collective-permute-start(f32[512,128]{1,0:T(8,128)S(1)} %dynamic-slice_add_fusion.2), channel_id=1, source_target_pairs={{0,16},{8,24},{16,0},{24,8},{1,17},{9,25},{17,1},{25,9},{2,18},{10... | collective-permute-start | bytes 786440 | tf_op jit(solution)/shard_map/ppermute | solution.py:397
  93.1 8.2 %collective-permute-start.11 = (f32[256,128]{1,0:T(8,128)S(1)}, f32[256,128]{1,0:T(8,128)S(1)}, u32[]{:S(2)}, u32[]{:S(2)}) collective-permute-start(f32[256,128]{1,0:T(8,128)S(1)} %constant_dynamic-slice_fusion.3), channel_id=1, source_target_pairs={{0,2},{2,0},{4,6},{6,4},{1,3},{3,1},{5,7},{7,5},{8,10},{10,8},{12,... | collective-permute-start | bytes 393224 | tf_op jit(solution)/shard_map/ppermute | solution.py:397
  109.9 11.9 %collective-permute-start.18 = (f32[520,128]{1,0:T(8,128)S(1)}, f32[520,128]{1,0:T(8,128)S(1)}, u32[]{:S(2)}, u32[]{:S(2)}) collective-permute-start(f32[520,128]{1,0:T(8,128)S(1)} %pad_maximum_fusion.4), channel_id=1, source_target_pairs={{0,4},{2,6},{4,0},{6,2},{1,5},{3,7},{5,1},{7,3},{8,12},{10,14},{12... | collective-permute-start | bytes 798728 | tf_op jit(solution)/shard_map/ppermute | solution.py:397
  112.2 9.6 %collective-permute-start.19 = (f32[3,48,512]{2,1,0:T(8,128)S(1)}, f32[3,48,512]{2,1,0:T(8,128)S(1)}, u32[]{:S(2)}, u32[]{:S(2)}) collective-permute-start(f32[3,48,512]{2,1,0:T(8,128)S(1)} %copy-done.4), channel_id=1, source_target_pairs={{0,8},{8,16},{16,24},{1,9},{9,17},{17,25},{2,10},{10,18},{18,26},{... | collective-permute-start | bytes 884744 | tf_op jit(solution)/shard_map/ppermute | solution.py:336
  113.5 8.3 %collective-permute-start.20 = (f32[3,48,512]{2,1,0:T(8,128)S(1)}, f32[3,48,512]{2,1,0:T(8,128)S(1)}, u32[]{:S(2)}, u32[]{:S(2)}) collective-permute-start(f32[3,48,512]{2,1,0:T(8,128)S(1)} %get-tuple-element.58), channel_id=1, source_target_pairs={{8,0},{16,8},{24,16},{9,1},{17,9},{25,17},{10,2},{18,10},{26,18},{... | collective-permute-start | bytes 884744 | tf_op jit(solution)/shard_map/ppermute | solution.py:336
  121.9 6.1 %collective-permute-start.24 = (f32[256,128]{1,0:T(8,128)S(1)}, f32[256,128]{1,0:T(8,128)S(1)}, u32[]{:S(2)}, u32[]{:S(2)}) collective-permute-start(f32[256,128]{1,0:T(8,128)S(1)} %slice.70), channel_id=1, source_target_pairs={{0,2},{2,0},{4,6},{6,4},{1,3},{3,1},{5,7},{7,5},{8,10},{10,8},{12,... | collective-permute-start | bytes 393224 | tf_op jit(solution)/shard_map/ppermute | solution.py:397
  122.1 19.5 %collective-permute-start.22 = (f32[8,9,512]{2,1,0:T(8,128)S(1)}, f32[8,9,512]{2,1,0:T(8,128)S(1)}, u32[]{:S(2)}, u32[]{:S(2)}) collective-permute-start(f32[8,9,512]{2,1,0:T(8,128)S(1)} %get-tuple-element.80), channel_id=1, source_target_pairs={{0,2},{2,4},{4,6},{6,0},{1,3},{3,5},{5,7},{7,1},{8,10},{10,12},{12... | collective-permute-start | bytes 442376 | tf_op jit(solution)/shard_map/ppermute | solution.py:336
  124.2 17.4 %collective-permute-start.21 = (f32[8,9,512]{2,1,0:T(8,128)S(1)}, f32[8,9,512]{2,1,0:T(8,128)S(1)}, u32[]{:S(2)}, u32[]{:S(2)}) collective-permute-start(f32[8,9,512]{2,1,0:T(8,128)S(1)} %get-tuple-element.79), channel_id=1, source_target_pairs={{2,0},{4,2},{6,4},{0,6},{3,1},{5,3},{7,5},{1,7},{10,8},{12,10},{14... | collective-permute-start | bytes 442376 | tf_op jit(solution)/shard_map/ppermute | solution.py:336
  126.0 6.3 %collective-permute-start.26 = (f32[264,128]{1,0:T(8,128)S(1)}, f32[264,128]{1,0:T(8,128)S(1)}, u32[]{:S(2)}, u32[]{:S(2)}) collective-permute-start(f32[264,128]{1,0:T(8,128)S(1)} %slice.71), channel_id=1, source_target_pairs={{0,1},{1,0},{2,3},{3,2},{4,5},{5,4},{6,7},{7,6},{8,9},{9,8},{10,11... | collective-permute-start | bytes 405512 | tf_op jit(solution)/shard_map/ppermute | solution.py:397
  128.1 7.1 %collective-permute-start.25 = (f32[512,128]{1,0:T(8,128)S(1)}, f32[512,128]{1,0:T(8,128)S(1)}, u32[]{:S(2)}, u32[]{:S(2)}) collective-permute-start(f32[512,128]{1,0:T(8,128)S(1)} %pad_maximum_fusion.5), channel_id=1, source_target_pairs={{0,1},{1,0},{2,3},{3,2},{4,5},{5,4},{6,7},{7,6},{8,9},{9,8},{10,11... | collective-permute-start | bytes 786440 | tf_op jit(solution)/shard_map/ppermute | solution.py:397
  132.4 9.2 %collective-permute-start.28 = (f32[528,128]{1,0:T(8,128)S(1)}, f32[528,128]{1,0:T(8,128)S(1)}, u32[]{:S(2)}, u32[]{:S(2)}) collective-permute-start(f32[528,128]{1,0:T(8,128)S(1)} %pad_maximum_fusion.3), channel_id=1, source_target_pairs={{0,16},{8,24},{16,0},{24,8},{1,17},{9,25},{17,1},{25,9},{2,18},{10... | collective-permute-start | bytes 811016 | tf_op jit(solution)/shard_map/ppermute | solution.py:397
  135.2 18.0 %collective-permute-start.27 = (f32[1024,128]{1,0:T(8,128)S(1)}, f32[1024,128]{1,0:T(8,128)S(1)}, u32[]{:S(2)}, u32[]{:S(2)}) collective-permute-start(f32[1024,128]{1,0:T(8,128)S(1)} %pad_maximum_fusion.2), channel_id=1, source_target_pairs={{0,16},{8,24},{16,0},{24,8},{1,17},{9,25},{17,1},{25,9},{2,18},{10... | collective-permute-start | bytes 1572872 | tf_op jit(solution)/shard_map/ppermute | solution.py:397
  141.7 14.6 %collective-permute-start.29 = (f32[1056,128]{1,0:T(8,128)S(1)}, f32[1056,128]{1,0:T(8,128)S(1)}, u32[]{:S(2)}, u32[]{:S(2)}) collective-permute-start(f32[1056,128]{1,0:T(8,128)S(1)} %pad_maximum_fusion.1), channel_id=1, source_target_pairs={{0,2},{2,0},{4,6},{6,4},{1,3},{3,1},{5,7},{7,5},{8,10},{10,8},{12,... | collective-permute-start | bytes 1622024 | tf_op jit(solution)/shard_map/ppermute | solution.py:397
  141.8 14.7 %collective-permute-start.23 = (f32[8,8,512]{2,1,0:T(8,128)S(1)}, f32[8,8,512]{2,1,0:T(8,128)S(1)}, u32[]{:S(2)}, u32[]{:S(2)}) collective-permute-start(f32[8,8,512]{2,1,0:T(8,128)S(1)} %fusion.2), channel_id=1, source_target_pairs={{0,1},{1,0},{2,3},{3,2},{4,5},{5,4},{6,7},{7,6},{8,9},{9,8},{10,11... | collective-permute-start | bytes 393224 | tf_op jit(solution)/shard_map/ppermute | solution.py:349
  156.5 6.9 %collective-permute-start.30 = (f32[4160,128]{1,0:T(8,128)S(1)}, f32[4160,128]{1,0:T(8,128)}, u32[]{:S(2)}, u32[]{:S(2)}) collective-permute-start(f32[4160,128]{1,0:T(8,128)S(1)} %pad_maximum_fusion.refs_1_), channel_id=1, source_target_pairs={{0,8},{8,0},{16,24},{24,16},{1,9},{9,1},{17,25},{25,17},{2,10},{10... | collective-permute-start | bytes 6389768 | tf_op jit(solution)/shard_map/ppermute | solution.py:397
  (27 other events, 212.4 us)

commit v2 on v1

v2 whole, which is shorter than its diff:
```python
import jax
import jax.numpy as jnp
import numpy as np
from jax import lax
from jax.experimental import pallas as pl
from jax.experimental.pallas import tpu as pltpu
from jax.sharding import PartitionSpec as P

D = 512
HEADS = 16
HEAD_DIM = 32
LAT_REACH = 3
LON_REACH = 3
LEV_REACH = 1
EPSILON = 1e-06
GROUP = 128
SLAB = 48
TAIL = 64
NEVER = -1e30
F32 = jnp.float32
BF16 = jnp.bfloat16


def split(x):
    high = x.astype(BF16)
    return high, (x - high.astype(F32)).astype(BF16)


def split3(x):
    high = x.astype(BF16)
    rest = x - high.astype(F32)
    middle = rest.astype(BF16)
    return high, middle, (rest - middle.astype(F32)).astype(BF16)


def dot(a, b, ca=1, cb=0):
    return lax.dot_general(a, b, (((ca,), (cb,)), ((), ())), preferred_element_type=F32)


def dot3(a, b, ca=1, cb=0):
    (ah, al), (bh, bl) = a, b
    return dot(ah, bh, ca, cb) + dot(ah, bl, ca, cb) + dot(al, bh, ca, cb)


def left6(parts, axis=1):
    h, m, l = parts
    return jnp.concatenate([h, h, m, m, h, l], axis=axis)


def right6(parts, axis=0):
    h, m, l = parts
    return jnp.concatenate([h, m, h, m, l, h], axis=axis)


def left3(parts, axis=1):
    return jnp.concatenate([parts[0], parts[0], parts[1]], axis=axis)


def right3(parts, axis=0):
    return jnp.concatenate([parts[0], parts[1], parts[0]], axis=axis)


def attention_kernel(
    pos_ref, top_ref, mid_ref, bot_ref, gain_ref, wq_ref, wk_ref, wv_ref, wo_ref, cot_ref,
    bias0_ref, bias1_ref, out_ref, btop_ref, bmid_ref, bbot_ref, send_ref, keep_ref,
    x_s, n_s, nt_s, own_s, ot_s, c_s, bn_s, dkv_s, k_s, v_s, g_s, t_s, sems,
):
    step = pl.program_id(0)
    last = pl.num_programs(0) - 1
    rows = x_s.shape[0]
    lats = rows // SLAB
    mid_lats = mid_ref.shape[0]
    tok = mid_lats * 16
    half_tok = tok // 2
    scale = HEAD_DIM ** (-0.5)
    padded = dkv_s.shape[0]

    def own_rows(x):
        return x.reshape(lats, SLAB, D)[LAT_REACH:LAT_REACH + mid_lats, :16].reshape(tok, D)

    @pl.when(step == 0)
    def _():
        x = jnp.concatenate([top_ref[...], mid_ref[...], bot_ref[...]], axis=0).reshape(rows, D)
        x_s[...] = x
        inv = lax.rsqrt(jnp.mean(x * x, axis=-1, keepdims=True) + EPSILON)
        normed = x * inv * gain_ref[...]
        parts = split3(normed)
        for i, j in enumerate((0, 0, 1, 1, 0, 2)):
            n_s[:, i * D:(i + 1) * D] = parts[j]
            own_s[:, i * D:(i + 1) * D] = own_rows(parts[j])
        pad = jnp.zeros((padded - rows, D), F32)
        parts = split(jnp.concatenate([normed, pad], axis=0).T)
        for i, j in enumerate((0, 0, 1)):
            nt_s[:, i * padded:(i + 1) * padded] = parts[j]
        parts = split(own_rows(normed).T)
        for i, j in enumerate((0, 0, 1)):
            ot_s[:, i * tok:(i + 1) * tok] = parts[j]
        c_s[...] = left6(split3(cot_ref[...]))
        bn_s[...] = jnp.zeros(bn_s.shape, F32)
        out_ref[...] = mid_ref[...][:, :16].reshape(tok, D)

    wq = split3(wq_ref[...])
    wkv = split3(jnp.concatenate([wk_ref[...], wv_ref[...]], axis=1))
    wo = split3(wo_ref[...])
    kv = dot(n_s[...], right6(wkv))
    k_s[...] = left6(split3(kv[:, :GROUP]))
    v_s[...] = left6(split3(kv[:, GROUP:]))
    q_t = (dot(own_s[...], right6(wq)) * scale).T
    b_t = dot(c_s[...], right6(wo, 1), 1, 1).T
    dkv_s[...] = jnp.zeros(dkv_s.shape, F32)
    heads = GROUP // HEAD_DIM
    cols = heads * half_tok
    head_row = lax.broadcasted_iota(jnp.int32, (GROUP, cols), 0) // HEAD_DIM
    head_col = lax.broadcasted_iota(jnp.int32, (GROUP, cols), 1) // half_tok
    same = head_row == head_col
    keys = bias0_ref.shape[1]

    def spread(x):
        return jnp.where(same, jnp.concatenate([x] * heads, axis=1), 0.0)

    def gather(x):
        x = jnp.where(same, x, 0.0)
        y = x[:, :half_tok]
        for h in range(1, heads):
            y = y + x[:, h * half_tok:(h + 1) * half_tok]
        return y

    halves = range(2)
    here = [slice(h * (rows - keys), h * (rows - keys) + keys) for h in halves]
    q_cols = [spread(q_t[:, h * half_tok:(h + 1) * half_tok]) for h in halves]
    b_cols = [spread(b_t[:, h * half_tok:(h + 1) * half_tok]) for h in halves]
    p, inv_sum, parts, kt, vt = [], [], [], [], []
    for h, bias_ref in enumerate((bias0_ref, bias1_ref)):
        bias = bias_ref[0]
        s = dot(k_s[here[h], :], right6(split3(q_cols[h])))
        s = s + jnp.concatenate([bias] * (cols // bias.shape[1]), axis=1)
        p.append(jnp.exp(s - jnp.max(s, axis=0, keepdims=True)))
        kt.append(k_s[here[h], GROUP:3 * GROUP].T)
        vt.append(v_s[here[h], GROUP:3 * GROUP].T)
    for h in halves:
        inv_sum.append(1.0 / jnp.sum(p[h], axis=0, keepdims=True))
        parts.append(split(p[h]))
        b_cols[h] = b_cols[h] * inv_sum[h]
    mixed_parts, dp = [], []
    for h in halves:
        dp.append(dot(v_s[here[h], :], right6(split3(b_cols[h]))))
        m2 = dot(vt[h], parts[h][0])
        mixed_parts.append(gather((m2[:GROUP] + m2[GROUP:] + dot(vt[h][:GROUP], parts[h][1])) * inv_sum[h]))
    ds = []
    for h in halves:
        agreement = jnp.sum(p[h] * dp[h], axis=0, keepdims=True) * inv_sum[h]
        ds.append(split(p[h] * (dp[h] - agreement)))
        b_rows = split(b_cols[h].T)
        dv2 = dot(parts[h][0], jnp.concatenate(b_rows, axis=1))
        dkv_s[here[h], GROUP:] += dv2[:, :GROUP] + dv2[:, GROUP:] + dot(parts[h][1], b_rows[0])
    dq_parts = []
    for h in halves:
        q_rows = split(q_cols[h].T)
        dk2 = dot(ds[h][0], jnp.concatenate(q_rows, axis=1))
        dkv_s[here[h], :GROUP] += dk2[:, :GROUP] + dk2[:, GROUP:] + dot(ds[h][1], q_rows[0])
        dq2 = dot(kt[h], ds[h][0])
        dq_parts.append(gather(dq2[:GROUP] + dq2[GROUP:] + dot(kt[h][:GROUP], ds[h][1])))
    mixed_t = jnp.concatenate(mixed_parts, axis=1)
    dq = split((jnp.concatenate(dq_parts, axis=1) * scale).T)
    out_ref[...] += dot(left3(split(mixed_t.T)), right3(wo))
    cot = (c_s[:, :D], c_s[:, 2 * D:3 * D])
    gwo = dot(left3(split(mixed_t)), right3(cot))
    gq = dot(ot_s[...], right3(dq))
    dkv = split(dkv_s[...])
    gkv = dot(nt_s[...], right3(dkv))
    copies = [
        pltpu.make_async_copy(
            g_s.at[i % 2], (send_ref, keep_ref)[i // 2].at[pl.ds(i % 2 * 4 * D, 4 * D)], sems.at[i]
        )
        for i in range(4)
    ]
    for i in range(2):
        @pl.when(step == i + 2)
        def _(i=i):
            copies[i].wait()
    slot = step % 2
    g_s[slot, 0:D, :] = gq
    g_s[slot, D:2 * D, :] = gkv[:, :GROUP]
    g_s[slot, 2 * D:3 * D, :] = gkv[:, GROUP:]
    for j in range(D // GROUP):
        g_s[slot, 3 * D + j * GROUP:3 * D + (j + 1) * GROUP, :] = gwo[:, j * GROUP:(j + 1) * GROUP]
    for i in range(4):
        @pl.when(step == i)
        def _(i=i):
            copies[i].start()

    bn_s[...] += dot(left3((dkv[0][:rows], dkv[1][:rows])), right3(wkv, 1), 1, 1)
    back_q = dot(left3(dq), right3(wq, 1), 1, 1)
    for i in range(mid_lats):
        at = (LAT_REACH + i) * SLAB
        bn_s[at:at + 16, :] += back_q[i * 16:(i + 1) * 16]

    @pl.when(step == last)
    def _():
        bn3 = bn_s[...].reshape(lats, SLAB, D)
        btop_ref[...] = bn3[:LAT_REACH]
        bbot_ref[...] = bn3[LAT_REACH + mid_lats:]
        bmid_ref[...] = bn3[LAT_REACH:LAT_REACH + mid_lats]
        x = x_s[...]
        inv = lax.rsqrt(jnp.mean(x * x, axis=-1, keepdims=True) + EPSILON)
        gg = jnp.sum(bn_s[...] * (x * inv), axis=0, keepdims=True)
        t_s[...] = jnp.zeros(t_s.shape, F32)
        for j in range(D // GROUP):
            t_s[1, j:j + 1, :] = gg[:, j * GROUP:(j + 1) * GROUP]
        tails = [
            pltpu.make_async_copy(t_s.at[i], ref.at[pl.ds(8 * D, TAIL)], sems.at[4 + i])
            for i, ref in enumerate((send_ref, keep_ref))
        ]
        for copy in tails:
            copy.start()
        for copy in tails + copies[2:]:
            copy.wait()


def attention(pos, top, mid, bot, gain, w_qkv, w_out, cot, bias):
    mid_lats = mid.shape[0]
    lats = mid_lats + 2 * LAT_REACH
    rows = lats * SLAB
    tok = mid_lats * 16
    padded = -(-rows // 256) * 256
    groups = D // GROUP
    whole = lambda *shape: pl.BlockSpec(shape, lambda s, pos: (0,) * len(shape))
    slab = lambda n: whole(n, SLAB, D)
    like = lambda *shape: jax.ShapeDtypeStruct(shape, F32)
    group = lambda s, pos: 2 * (s % 2) + jnp.where(s < 2, 1 - pos[0], pos[0])
    outs, out_specs = [like(tok, D)], [whole(tok, D)]
    for n in (LAT_REACH, mid_lats, LAT_REACH):
        outs.append(like(n, SLAB, D))
        out_specs.append(slab(n))
    for _ in range(2):
        outs.append(like(8 * D + TAIL, GROUP))
        out_specs.append(pl.BlockSpec(memory_space=pl.ANY))
    return pl.pallas_call(
        attention_kernel,
        grid_spec=pltpu.PrefetchScalarGridSpec(
            num_scalar_prefetch=1,
            grid=(4,),
            in_specs=[
                slab(LAT_REACH), slab(mid_lats), slab(LAT_REACH), whole(1, D),
                pl.BlockSpec((D, GROUP), lambda s, pos: (0, group(s, pos))),
                pl.BlockSpec((D, GROUP), lambda s, pos: (0, groups + group(s, pos))),
                pl.BlockSpec((D, GROUP), lambda s, pos: (0, 2 * groups + group(s, pos))),
                pl.BlockSpec((GROUP, D), lambda s, pos: (group(s, pos), 0)),
                whole(tok, D),
                pl.BlockSpec((1,) + bias.shape[1:], lambda s, pos: (pos[1], 0, 0)),
                pl.BlockSpec((1,) + bias.shape[1:], lambda s, pos: (pos[2], 0, 0)),
            ],
            out_specs=out_specs,
            scratch_shapes=[
                pltpu.VMEM((rows, D), F32),
                pltpu.VMEM((rows, 6 * D), BF16), pltpu.VMEM((D, 3 * padded), BF16),
                pltpu.VMEM((tok, 6 * D), BF16), pltpu.VMEM((D, 3 * tok), BF16),
                pltpu.VMEM((tok, 6 * D), BF16),
                pltpu.VMEM((rows, D), F32), pltpu.VMEM((padded, 2 * GROUP), F32),
                pltpu.VMEM((rows, 6 * GROUP), BF16), pltpu.VMEM((rows, 6 * GROUP), BF16),
                pltpu.VMEM((2, 4 * D, GROUP), F32), pltpu.VMEM((2, TAIL, GROUP), F32),
                pltpu.SemaphoreType.DMA((6,)),
            ],
        ),
        out_shape=outs,
        compiler_params=pltpu.CompilerParams(vmem_limit_bytes=48 * 1024 * 1024),
        cost_estimate=pl.CostEstimate(flops=20_000_000_000, bytes_accessed=24_000_000, transcendentals=2_000_000),
        name="attention",
    )(pos, top, mid, bot, gain.reshape(1, D), w_qkv, w_qkv, w_qkv, w_out, cot, bias, bias)


def unpack_kernel(factor, core_ref, mine_ref, other_ref, gain_ref, qkv_ref, out_ref):
    groups = D // GROUP
    core = core_ref[0]
    for ref, keeper in ((mine_ref, core), (other_ref, 1 - core)):
        for k in range(2):
            g = 2 * k + keeper
            for j in range(3):
                cols = pl.ds(pl.multiple_of((j * groups + g) * GROUP, GROUP), GROUP)
                qkv_ref[:, cols] = ref[(4 * k + j) * D:(4 * k + j + 1) * D, :] * factor
            for j in range(groups):
                at = (4 * k + 3) * D + j * GROUP
                out_ref[g, :, j * GROUP:(j + 1) * GROUP] = ref[at:at + GROUP, :] * factor
    for row in range(D // GROUP):
        at = 8 * D + row
        gain_ref[row:row + 1, :] = (mine_ref[at:at + 1, :] + other_ref[at:at + 1, :]) * factor


def unpack(core, factor, mine, other):
    return pl.pallas_call(
        lambda *refs: unpack_kernel(factor, *refs),
        in_specs=[pl.BlockSpec(memory_space=pltpu.SMEM)] + [pl.BlockSpec(memory_space=pltpu.VMEM)] * 2,
        out_specs=[pl.BlockSpec(memory_space=pltpu.VMEM)] * 3,
        out_shape=[
            jax.ShapeDtypeStruct((D // GROUP, GROUP), F32),
            jax.ShapeDtypeStruct((D, 3 * D), F32),
            jax.ShapeDtypeStruct((D // GROUP, GROUP, D), F32),
        ],
        compiler_params=pltpu.CompilerParams(vmem_limit_bytes=32 * 1024 * 1024),
        cost_estimate=pl.CostEstimate(flops=1_000_000, bytes_accessed=8_000_000, transcendentals=0),
        name="unpack",
    )(core, mine, other)


def shift(x, axis, step, closed):
    count = lax.axis_size(axis)
    ends = count if closed else count - 1
    pairs = [(i, (i + 1) % count) for i in range(ends)]
    if step < 0:
        pairs = [(j, i) for i, j in pairs]
    return lax.ppermute(x, axis, pairs)


def shift_across(x, step):
    count = lax.axis_size("lon")
    pairs = []
    for i in range(count):
        for e in range(2):
            pairs.append((i * 2 + e, ((i + step) % count) * 2 + 1 - e))
    return lax.ppermute(x, ("lon", "lev"), pairs)


def swap_lev(x):
    return lax.ppermute(x, "lev", [(0, 1), (1, 0)])


def window_bias(lat_dev, lon_dev, keys):
    left = np.arange(-LON_REACH, 0)
    right = np.arange(lon_dev, lon_dev + LON_REACH)
    lon = np.concatenate([
        np.repeat(np.arange(lon_dev), 2), np.arange(lon_dev), np.repeat(left, 2), left,
        np.repeat(right, 2), right,
    ])
    level = np.concatenate([
        np.tile([0, 1], lon_dev), np.full(lon_dev, 2), np.tile([0, 1], LON_REACH),
        np.full(LON_REACH, 2), np.tile([0, 1], LON_REACH), np.full(LON_REACH, 2),
    ])
    unused = SLAB - lon.shape[0]
    lon = np.concatenate([lon, np.full(unused, 1000)])
    level = np.concatenate([level, np.full(unused, 0)])
    lats = lat_dev + 2 * LAT_REACH
    rows = lats * SLAB
    lat = np.repeat(np.arange(lats) - LAT_REACH, SLAB)[:, None]
    lon = np.tile(lon, lats)[:, None]
    level = np.tile(level, lats)[:, None]
    q_lat = np.repeat(np.arange(lat_dev), lon_dev * 2)
    q_lon = np.tile(np.repeat(np.arange(lon_dev), 2), lat_dev)
    q_level = np.tile([0, 1], lat_dev * lon_dev)
    near = (np.abs(lat - q_lat) <= LAT_REACH) & (np.abs(lon - q_lon) <= LON_REACH)
    half = q_lat.shape[0] // 2
    table = []
    for part in range(2):
        first = part * (rows - keys)
        ks = slice(first, first + keys)
        qs = np.tile(np.arange(part * half, (part + 1) * half), 2)
        for side in range(2):
            lev_k = np.where(level == 2, 2 - side, side * 2 + level)
            seen = near & (np.abs(lev_k - (side * 2 + q_level)) <= LEV_REACH)
            for edge in range(2):
                kept = seen
                if edge == 1:
                    kept = seen & ((lat >= 0) if part == 0 else (lat < lat_dev))
                table.append(np.where(kept[ks][:, qs], 0.0, NEVER))
    return np.stack(table).astype(np.float32)


def bit_of(axis, bit):
    return (lax.axis_index(axis) >> bit) & 1


def swap_bit(x, axis, bit):
    return lax.ppermute(x, axis, [(i, i ^ (1 << bit)) for i in range(lax.axis_size(axis))])


def halve(blocks, bits):
    def half(block, which):
        terms, start, size = block
        n = size // 2
        return sum(lax.dynamic_slice_in_dim(x, start + which * n, n, 0) for x in terms)

    mine = [bit_of(*bit) for bit in bits]
    given = [half(x, 1 - m) for x, m in zip(blocks, mine)]
    came = [swap_bit(x, *bit) for x, bit in zip(given, bits)]
    if len(came) > 1:
        came = [after(x, given) for x in came]
    kept = [((half(x, m) + s,), 0, s.shape[0]) for x, m, s in zip(blocks, mine, came)]
    return kept


def double(blocks, bits):
    came = [after(swap_bit(x, *bit), blocks) for x, bit in zip(blocks, bits)]
    grown = []
    for x, s, (axis, bit) in zip(blocks, came, bits):
        mine = bit_of(axis, bit) == 1
        grown.append([jnp.where(mine, s, x), jnp.where(mine, x, s)])
    return grown


def bits_in(axis):
    count = lax.axis_size(axis)
    assert count & (count - 1) == 0
    return [(axis, b) for b in range(count.bit_length() - 1)]


def after(x, done):
    return lax.optimization_barrier((x, done))[0]


def finish_kernel(low_ref, back_ref, left_ref, right_ref, edge_ref, x_ref, cot_ref, gain_ref, out_ref):
    r = LON_REACH
    lats, lons = edge_ref.shape[:2]
    low = low_ref[0]
    row = lax.broadcasted_iota(jnp.int32, (2 * lons, lons), 0)
    col = lax.broadcasted_iota(jnp.int32, (2 * lons, lons), 1)
    place = jnp.where(row == 2 * col + low, 1.0, 0.0).astype(F32)
    cells = lax.broadcasted_iota(jnp.int32, (2 * lons, 1), 0)
    gain = gain_ref[...]
    for i in range(lats):
        total = back_ref[i, :16, :]
        none = jnp.zeros((16 - 2 * r, D), F32)
        total = total + jnp.concatenate([none, left_ref[i, :2 * r, :]], axis=0)
        total = total + jnp.concatenate([right_ref[i, :2 * r, :], none], axis=0)
        total = total + jnp.dot(place, edge_ref[i], precision=lax.Precision.HIGHEST, preferred_element_type=F32)
        x = x_ref[i]
        inv_rms = lax.rsqrt(jnp.mean(x * x, axis=-1, keepdims=True) + EPSILON)
        scaled = gain * total
        grad = cot_ref[i * 16:(i + 1) * 16, :] + inv_rms * scaled
        dots = jnp.mean(scaled * x, axis=-1, keepdims=True)
        out_ref[i * 16:(i + 1) * 16, :] = grad - x * (inv_rms * inv_rms * inv_rms * dots)


def finish(low, back, to_left, to_right, edge_sum, own, cot, gain):
    vmem = pl.BlockSpec(memory_space=pltpu.VMEM)
    return pl.pallas_call(
        finish_kernel,
        in_specs=[pl.BlockSpec(memory_space=pltpu.SMEM)] + [vmem] * 7,
        out_specs=vmem,
        out_shape=jax.ShapeDtypeStruct(cot.shape, F32),
        compiler_params=pltpu.CompilerParams(vmem_limit_bytes=16 * 1024 * 1024),
        cost_estimate=pl.CostEstimate(flops=3_000_000, bytes_accessed=3_000_000, transcendentals=0),
        name="finish",
    )(low.astype(jnp.int32).reshape(1), back, to_left, to_right, edge_sum, own, cot, gain.reshape(1, D))


def per_device(fields, gain, w_qkv, w_out, cotangent):
    lat_dev, lon_dev, lev_dev = fields.shape[:3]
    assert lev_dev == 2 and lax.axis_size("lev") == 2 and lon_dev * lev_dev == 16
    tok = lat_dev * lon_dev * lev_dev
    low = lax.axis_index("lev") == 0
    r = LON_REACH
    edge = jnp.where(low, fields[:, :, 1], fields[:, :, 0])
    own = fields.reshape(lat_dev, 16, D)
    left_own = shift(own[:, 16 - 2 * r:], "lon", 1, True)
    right_own = shift(own[:, :2 * r], "lon", -1, True)
    left_far = shift_across(edge[:, lon_dev - r:], 1)
    right_far = shift_across(edge[:, :r], -1)
    far = swap_lev(edge)
    blank = jnp.zeros((lat_dev, SLAB - 24 - 6 * r, D), F32)
    mid = jnp.concatenate([own, far, left_own, left_far, right_own, right_far, blank], axis=1)
    top = shift(mid[lat_dev - LAT_REACH:], "lat", 1, False)
    bot = shift(mid[:LAT_REACH], "lat", -1, False)
    bias = jnp.asarray(window_bias(lat_dev, lon_dev, 512))
    lat_id, lev_id = lax.axis_index("lat"), lax.axis_index("lev")
    core = lat_id & 1
    pos = jnp.stack([
        core, lev_id * 2 + (lat_id == 0), 4 + lev_id * 2 + (lat_id == lax.axis_size("lat") - 1),
    ]).astype(jnp.int32)
    shared = (gain, w_qkv, w_out, cotangent.reshape(tok, D), bias)
    out, btop, bmid, bbot, send, keep = attention(pos, top, mid, bot, *shared)
    from_low = shift(bbot, "lat", 1, False)
    from_high = shift(btop, "lat", -1, False)
    (pair,), x_bits = bits_in("lat")[:1], bits_in("lat")[1:]
    y_bits, z_bits = bits_in("lev"), bits_in("lon")
    zh_bits = z_bits[:-1]
    orders = [x_bits + y_bits + zh_bits, y_bits + zh_bits + x_bits, zh_bits + x_bits + y_bits]
    stages = len(orders[0])
    total = (keep, swap_bit(send, *pair))
    blocks, at, unit = [], 0, (8 * D + TAIL) // TAIL
    for i in range(3):
        size = (unit + 2 - i) // 3 * TAIL
        blocks.append((total, at, size))
        at += size
    rest = lat_dev - LAT_REACH
    low_at, high_at = 24, 24 + 3 * r
    for stage in range(stages):
        blocks = halve(blocks, [order[stage] for order in orders])
        if stage == 0:
            tied = lax.optimization_barrier(([x[0] for x in blocks], from_low, from_high))
            blocks = [(t,) + x[1:] for t, x in zip(tied[0], blocks)]
            back = bmid + jnp.pad(tied[1], ((0, rest), (0, 0), (0, 0)))
            back = back + jnp.pad(tied[2], ((rest, 0), (0, 0), (0, 0)))
            to_left = shift(back[:, low_at:high_at], "lon", -1, True)
            to_right = shift(back[:, high_at:high_at + 3 * r], "lon", 1, True)
    sizes = [x[2] for x in blocks]
    every = jnp.concatenate([x[0][0] for x in blocks], axis=0)
    every, to_left, to_right = lax.optimization_barrier((every, to_left, to_right))
    every = every + swap_bit(every, *z_bits[-1])
    other = back[:, 16:24] + jnp.pad(to_left[:, 2 * r:], ((0, 0), (lon_dev - r, 0), (0, 0)))
    other = other + jnp.pad(to_right[:, 2 * r:], ((0, 0), (0, lon_dev - r), (0, 0)))
    every, edge_sum = lax.optimization_barrier((every, swap_lev(other)))
    grad_fields = finish(
        low, back, to_left, to_right, edge_sum, own, cotangent.reshape(tok, D), gain
    ).reshape(fields.shape)
    blocks = [every[:sizes[0]], every[sizes[0]:sizes[0] + sizes[1]], every[sizes[0] + sizes[1]:]]
    for stage in reversed(range(stages)):
        if stage == 0:
            blocks[0] = after(blocks[0], grad_fields)
        parts = double(blocks, [order[stage] for order in orders])
        if stage > 0:
            blocks = [jnp.concatenate(x, axis=0) for x in parts]
    mine = jnp.concatenate(parts[0] + parts[1] + parts[2], axis=0)
    devices = lax.axis_size("lat") * lax.axis_size("lon") * lax.axis_size("lev")
    factor = (tok * devices) ** (-0.5)
    grad_gain, grad_qkv, grad_out = unpack(
        core.reshape(1).astype(jnp.int32), factor,
        mine, swap_bit(mine, *pair),
    )
    grad_gain, grad_out = grad_gain.reshape(D), grad_out.reshape(D, D)
    return (out.reshape(fields.shape), grad_fields, grad_gain, grad_qkv, grad_out)


def solution(mesh):
    cells = P("lat", "lon", "lev", None)
    return jax.shard_map(
        per_device, mesh=mesh, in_specs=(cells, P(), P(), P(), cells),
        out_specs=(cells, cells, P(), P(), P()), check_vma=False,
    )
```

time: 168 us -> 163 us (0.970)
  waiting for transfers between devices: 47.1 us -> 54.7 us
  local copies, waits for them, and re-layouts: 15.8 us -> 11.7 us
  Pallas kernels: 44.3 us -> 40.9 us
  other arithmetic: 10.5 us -> 7.59 us
  starting transfers between devices: 48.5 us -> 46.6 us
    ppermute x19 -> x21, waiting for transfers between devices: 40.3 us -> 47.7 us  [swap_bit(): lax.ppermute(x, axis, [(i, i ^ 1 << bit) for i in range(lax.axis_size(axi...]
    ppermute x2, waiting for transfers between devices: 3.19 us -> 6.96 us  [shift_across(): return lax.ppermute(x, ('lon', 'lev'), pairs)]
    unnamed x40 -> x20, local copies, waits for them, and re-layouts: 8.4 us -> 4.81 us
    ppermute x8, waiting for transfers between devices: 3.6 us -> 0.02 us  [shift(): return lax.ppermute(x, axis, pairs)]
    pallas_call x3, Pallas kernels: 44.3 us -> 40.9 us  [the longest x1 36.1 us: attention(): pl.pallas_call(attention_kernel, grid_spec=pltpu.PrefetchScalarGridSpec(n...]
    ppermute x8, starting transfers between devices: 12.9 us -> 16.1 us  [shift(): return lax.ppermute(x, axis, pairs)]
    ppermute x19 -> x21, starting transfers between devices: 25.7 us -> 23.5 us  [swap_bit(): lax.ppermute(x, axis, [(i, i ^ 1 << bit) for i in range(lax.axis_size(axi...]
    ppermute x2, starting transfers between devices: 5.14 us -> 3.18 us  [swap_lev(): return lax.ppermute(x, 'lev', [(0, 1), (1, 0)])]
  transfers between devices with their start and end apart: 31 -> 33, of which waited for: 16 -> 16; matrix products, arithmetic and copies ran while one was open for 9% -> 6% of each run, Pallas kernels for 12% -> 0%
where the time goes in v2:
time: 163 us
  waiting for transfers between devices  54.7 us (34%)
  starting transfers between devices  46.6 us (29%)
  Pallas kernels  40.9 us (25%)
  local copies, waits for them, and re-layouts  11.7 us (7%)
  other arithmetic  7.59 us (5%)
    ppermute x21, waiting for transfers between devices, swap_bit(): lax.ppermute(x, axis, [(i, i ^ 1 << bit) for i in range(lax.axis_size(axi...  47.7 us
    pallas_call x1, Pallas kernels, attention(): pl.pallas_call(attention_kernel, grid_spec=pltpu.PrefetchScalarGridSpec(n...  36.1 us
    ppermute x21, starting transfers between devices, swap_bit(): lax.ppermute(x, axis, [(i, i ^ 1 << bit) for i in range(lax.axis_size(axi...  23.5 us
    ppermute x8, starting transfers between devices, shift(): return lax.ppermute(x, axis, pairs)  16.1 us
    ppermute x2, waiting for transfers between devices, shift_across(): return lax.ppermute(x, ('lon', 'lev'), pairs)  6.96 us
    unnamed x20, local copies, waits for them, and re-layouts  4.81 us
    pallas_call x1, Pallas kernels, unpack(): pl.pallas_call(lambda *refs: unpack_kernel(factor, *refs), in_specs=[pl.B...  4.17 us
    add x2, other arithmetic, half(): sum((lax.dynamic_slice_in_dim(x, start + which * n, n, 0) for x in terms))  3.96 us
  transfers between devices with their start and end apart: 33, of which 16 were waited for; matrix products, arithmetic and copies ran while one was open for 6% of the time, Pallas kernels for 0%

profile of v2, /device:TPU:0, one launch (start us, length us, event | category | flops | bytes accessed | tf_op | source)
XLA Modules:
  0.0 162.6 jit_solution(14392212782007622405)
XLA Ops:
  1.8 5.1 %collective-permute-start.3 = (f32[8,6,512]{2,1,0:T(8,128)S(1)}, f32[8,6,512]{2,1,0:T(8,128)S(1)}, u32[]{:S(2)}, u32[]{:S(2)}) collective-permute-start(f32[8,6,512]{2,1,0:T(8,128)S(1)} %get-tuple-element.105), channel_id=1, source_target_pairs={{2,0},{4,2},{6,4},{0,6},{3,1},{5,3},{7,5},{1,7},{10,8},{12,10},{14... | collective-permute-start | bytes 294920 | tf_op jit(solution)/shard_map/ppermute | solution.py:311
  9.9 3.8 %collective-permute-start.4 = (f32[8,3,512]{2,1,0:T(4,128)S(1)}, f32[8,3,512]{2,1,0:T(4,128)S(1)}, u32[]{:S(2)}, u32[]{:S(2)}) collective-permute-start(f32[8,3,512]{2,1,0:T(4,128)S(1)} %get-tuple-element.109), channel_id=1, source_target_pairs={{0,7},{1,6},{2,1},{3,0},{4,3},{5,2},{6,5},{7,4},{8,15},{9,14},{10,... | collective-permute-start | bytes 147464 | tf_op jit(solution)/shard_map/ppermute | solution.py:320
  13.7 2.4 %collective-permute-done.4 = f32[8,3,512]{2,1,0:T(4,128)S(1)} collective-permute-done((f32[8,3,512]{2,1,0:T(4,128)S(1)}, f32[8,3,512]{2,1,0:T(4,128)S(1)}, u32[]{:S(2)}, u32[]{:S(2)}) %collective-permute-start.4) | collective-permute-done | bytes 49184 | tf_op jit(solution)/shard_map/ppermute | solution.py:320
  16.1 4.6 %collective-permute-done.2 = f32[8,3,512]{2,1,0:T(4,128)S(1)} collective-permute-done((f32[8,3,512]{2,1,0:T(4,128)S(1)}, f32[8,3,512]{2,1,0:T(4,128)S(1)}, u32[]{:S(2)}, u32[]{:S(2)}) %collective-permute-start.2) | collective-permute-done | bytes 49184 | tf_op jit(solution)/shard_map/ppermute | solution.py:320
  23.4 3.0 %collective-permute-start.5 = (f32[3,48,512]{2,1,0:T(8,128)}, f32[3,48,512]{2,1,0:T(8,128)S(1)}, u32[]{:S(2)}, u32[]{:S(2)}) collective-permute-start(f32[3,48,512]{2,1,0:T(8,128)} %get-tuple-element.88), channel_id=1, source_target_pairs={{0,8},{8,16},{16,24},{1,9},{9,17},{17,25},{2,10},{10,18},{18,26},{... | collective-permute-start | bytes 884744 | tf_op jit(solution)/shard_map/ppermute | solution.py:311
  31.0 36.1 %attention.1 = (f32[128,512]{1,0:T(8,128)S(1)}, f32[3,48,512]{2,1,0:T(8,128)S(1)}, f32[8,48,512]{2,1,0:T(8,128)S(1)}, f32[3,48,512]{2,1,0:T(8,128)S(1)}, f32[4160,128]{1,0:T(8,128)}, /*index=5*/f32[4160,128]{1,0:T(8,128)}) custom-call(s32[3]{0:T(128)S(1)} %pad_add_fusion.1.pos_ref, f32[3,48,512]{2,1,0:T(8,128)S(1)} %copy-done.9, ...), custom_call_target="tpu_custom_call" | custom-call | flops 20000000000 | bytes 24000000 | tf_op jit(solution)/shard_map/attention/pallas_call | solution.py:238
  68.6 3.1 %collective-permute-start.7 = (f32[4160,128]{1,0:T(8,128)}, f32[4160,128]{1,0:T(8,128)}, u32[]{:S(2)}, u32[]{:S(2)}) collective-permute-start(f32[4160,128]{1,0:T(8,128)} %get-tuple-element.46), channel_id=1, source_target_pairs={{0,8},{8,0},{16,24},{24,16},{1,9},{9,1},{17,25},{25,17},{2,10},{10... | collective-permute-start | bytes 6389768 | tf_op jit(solution)/shard_map/ppermute | solution.py:372
  71.7 4.2 %collective-permute-done.7 = f32[4160,128]{1,0:T(8,128)} collective-permute-done((f32[4160,128]{1,0:T(8,128)}, f32[4160,128]{1,0:T(8,128)}, u32[]{:S(2)}, u32[]{:S(2)}) %collective-permute-start.7) | collective-permute-done | bytes 2129952 | tf_op jit(solution)/shard_map/ppermute | solution.py:372
  75.9 1.8 %dynamic-slice_add_fusion.2 = f32[672,128]{1,0:T(8,128)} fusion(f32[4160,128]{1,0:T(8,128)} %collective-permute-done.7, s32[]{:T(128)S(6)} %select_n.179, f32[4160,128]{1,0:T(8,128)} %get-tuple-element.45), kind=kLoop, calls=%fused_computation.15 | loop fusion | flops 86016 | bytes 1032196 | tf_op jit(solution)/shard_map/add | solution.py:379
  77.7 2.1 %dynamic-slice_add_fusion = (f32[704,128]{1,0:T(8,128)}, f32[704,128]{1,0:T(8,128)S(1)}) fusion(f32[4160,128]{1,0:T(8,128)} %collective-permute-done.7, s32[]{:T(128)S(6)} %select_n.178, f32[4160,128]{1,0:T(8,128)} %get-tuple-element.45, s32[]{:T(128)S(6)} %select_n.177), kind=kLoop, calls=%fused_computation.8 | loop fusion | flops 180224 | bytes 2162696 | tf_op jit(solution)/shard_map/add | solution.py:379
  81.4 2.6 %collective-permute-start.8 = (f32[704,128]{1,0:T(8,128)S(1)}, f32[704,128]{1,0:T(8,128)S(1)}, u32[]{:S(2)}, u32[]{:S(2)}) collective-permute-start(f32[704,128]{1,0:T(8,128)S(1)} %get-tuple-element.84), channel_id=1, source_target_pairs={{0,16},{8,24},{16,0},{24,8},{1,17},{9,25},{17,1},{25,9},{2,18},{10... | collective-permute-start | bytes 1081352 | tf_op jit(solution)/shard_map/ppermute | solution.py:372
  90.8 2.1 %collective-permute-done.8 = f32[704,128]{1,0:T(8,128)S(1)} collective-permute-done((f32[704,128]{1,0:T(8,128)S(1)}, f32[704,128]{1,0:T(8,128)S(1)}, u32[]{:S(2)}, u32[]{:S(2)}) %collective-permute-start.8) | collective-permute-done | bytes 360480 | tf_op jit(solution)/shard_map/ppermute | solution.py:372
  94.4 3.1 %collective-permute-start.16 = (f32[336,128]{1,0:T(8,128)S(1)}, f32[336,128]{1,0:T(8,128)S(1)}, u32[]{:S(2)}, u32[]{:S(2)}) collective-permute-start(f32[336,128]{1,0:T(8,128)S(1)} %constant_dynamic-slice_fusion.3), channel_id=1, source_target_pairs={{0,16},{8,24},{16,0},{24,8},{1,17},{9,25},{17,1},{25,9},{2,18},{10... | collective-permute-start | bytes 516104 | tf_op jit(solution)/shard_map/ppermute | solution.py:372
  100.4 3.5 %collective-permute-start.19 = (f32[8,9,512]{2,1,0:T(8,128)S(1)}, f32[8,9,512]{2,1,0:T(8,128)S(1)}, u32[]{:S(2)}, u32[]{:S(2)}) collective-permute-start(f32[8,9,512]{2,1,0:T(8,128)S(1)} %get-tuple-element.86), channel_id=1, source_target_pairs={{2,0},{4,2},{6,4},{0,6},{3,1},{5,3},{7,5},{1,7},{10,8},{12,10},{14... | collective-permute-start | bytes 442376 | tf_op jit(solution)/shard_map/ppermute | solution.py:311
  105.5 4.4 %collective-permute-done.15 = f32[352,128]{1,0:T(8,128)S(1)} collective-permute-done((f32[352,128]{1,0:T(8,128)S(1)}, f32[352,128]{1,0:T(8,128)S(1)}, u32[]{:S(2)}, u32[]{:S(2)}) %collective-permute-start.15) | collective-permute-done | bytes 180256 | tf_op jit(solution)/shard_map/ppermute | solution.py:372
  110.4 4.2 %collective-permute-done.17 = f32[176,128]{1,0:T(8,128)S(1)} collective-permute-done((f32[176,128]{1,0:T(8,128)S(1)}, f32[176,128]{1,0:T(8,128)S(1)}, u32[]{:S(2)}, u32[]{:S(2)}) %collective-permute-start.17) | collective-permute-done | bytes 90144 | tf_op jit(solution)/shard_map/ppermute | solution.py:372
  117.6 10.6 %collective-permute-done.21 = f32[520,128]{1,0:T(8,128)S(1)} collective-permute-done((f32[520,128]{1,0:T(8,128)S(1)}, f32[520,128]{1,0:T(8,128)S(1)}, u32[]{:S(2)}, u32[]{:S(2)}) %collective-permute-start.21) | collective-permute-done | bytes 266272 | tf_op jit(solution)/shard_map/ppermute | solution.py:372
  130.8 2.3 %collective-permute-start.25 = (f32[176,128]{1,0:T(8,128)S(1)}, f32[176,128]{1,0:T(8,128)S(1)}, u32[]{:S(2)}, u32[]{:S(2)}) collective-permute-start(f32[176,128]{1,0:T(8,128)S(1)} %get-tuple-element.103), channel_id=1, source_target_pairs={{0,16},{8,24},{16,0},{24,8},{1,17},{9,25},{17,1},{25,9},{2,18},{10... | collective-permute-start | bytes 270344 | tf_op jit(solution)/shard_map/ppermute | solution.py:372
  133.2 2.6 %collective-permute-start.29 = (f32[336,128]{1,0:T(8,128)S(1)}, f32[336,128]{1,0:T(8,128)S(1)}, u32[]{:S(2)}, u32[]{:S(2)}) collective-permute-start(f32[336,128]{1,0:T(8,128)S(1)} %pad_maximum_fusion.6), channel_id=1, source_target_pairs={{0,16},{8,24},{16,0},{24,8},{1,17},{9,25},{17,1},{25,9},{2,18},{10... | collective-permute-start | bytes 516104 | tf_op jit(solution)/shard_map/ppermute | solution.py:372
  139.4 3.9 %collective-permute-done.24 = f32[352,128]{1,0:T(8,128)S(1)} collective-permute-done((f32[352,128]{1,0:T(8,128)S(1)}, f32[352,128]{1,0:T(8,128)S(1)}, u32[]{:S(2)}, u32[]{:S(2)}) %collective-permute-start.24) | collective-permute-done | bytes 180256 | tf_op jit(solution)/shard_map/ppermute | solution.py:372
  143.3 2.0 %collective-permute-done.28 = f32[352,128]{1,0:T(8,128)S(1)} collective-permute-done((f32[352,128]{1,0:T(8,128)S(1)}, f32[352,128]{1,0:T(8,128)S(1)}, u32[]{:S(2)}, u32[]{:S(2)}) %collective-permute-start.28) | collective-permute-done | bytes 180256 | tf_op jit(solution)/shard_map/ppermute | solution.py:372
  146.5 7.2 %collective-permute-done.31 = f32[672,128]{1,0:T(8,128)S(1)} collective-permute-done((f32[672,128]{1,0:T(8,128)S(1)}, f32[672,128]{1,0:T(8,128)S(1)}, u32[]{:S(2)}, u32[]{:S(2)}) %collective-permute-start.31) | collective-permute-done | bytes 344096 | tf_op jit(solution)/shard_map/ppermute | solution.py:372
  154.9 3.5 %collective-permute-done.32.refs_2_ = f32[4160,128]{1,0:T(8,128)} collective-permute-done((f32[4160,128]{1,0:T(8,128)S(1)}, f32[4160,128]{1,0:T(8,128)}, u32[]{:S(2)}, u32[]{:S(2)}) %collective-permute-start.32) | collective-permute-done | bytes 2129952 | tf_op jit(solution)/shard_map/ppermute | solution.py:372
  158.4 4.2 %unpack.1 = (f32[4,128]{1,0:T(4,128)}, f32[512,1536]{1,0:T(8,128)}, f32[4,128,512]{2,1,0:T(8,128)}) custom-call(s32[1]{0:T(128)} %bitcast.refs_0_, f32[4160,128]{1,0:T(8,128)S(1)} %select_dynamic-update-slice_fusion.4.refs_1_, f32[4160,128]{1,0:T(8,128)} %collective-permute-done.32.refs_2_), custom_call_target="tpu_custom_call" | custom-call | flops 1000000 | bytes 8000000 | tf_op jit(solution)/shard_map/unpack/pallas_call | solution.py:290
  (118 shorter events, 39.0 us)
Async XLA Ops:
  1.8 18.9 %collective-permute-start.3 = (f32[8,6,512]{2,1,0:T(8,128)S(1)}, f32[8,6,512]{2,1,0:T(8,128)S(1)}, u32[]{:S(2)}, u32[]{:S(2)}) collective-permute-start(f32[8,6,512]{2,1,0:T(8,128)S(1)} %get-tuple-element.105), channel_id=1, source_target_pairs={{2,0},{4,2},{6,4},{0,6},{3,1},{5,3},{7,5},{1,7},{10,8},{12,10},{14... | collective-permute-start | bytes 294920 | tf_op jit(solution)/shard_map/ppermute | solution.py:311
  6.9 13.8 %collective-permute-start.1 = (f32[8,6,512]{2,1,0:T(8,128)S(1)}, f32[8,6,512]{2,1,0:T(8,128)S(1)}, u32[]{:S(2)}, u32[]{:S(2)}) collective-permute-start(f32[8,6,512]{2,1,0:T(8,128)S(1)} %get-tuple-element.106), channel_id=1, source_target_pairs={{0,2},{2,4},{4,6},{6,0},{1,3},{3,5},{5,7},{7,1},{8,10},{10,12},{12... | collective-permute-start | bytes 294920 | tf_op jit(solution)/shard_map/ppermute | solution.py:311
  8.3 12.4 %collective-permute-start = (f32[8,8,512]{2,1,0:T(8,128)S(1)}, f32[8,8,512]{2,1,0:T(8,128)S(1)}, u32[]{:S(2)}, u32[]{:S(2)}) collective-permute-start(f32[8,8,512]{2,1,0:T(8,128)S(1)} %fusion.1), channel_id=1, source_target_pairs={{0,1},{1,0},{2,3},{3,2},{4,5},{5,4},{6,7},{7,6},{8,9},{9,8},{10,11... | collective-permute-start | bytes 393224 | tf_op jit(solution)/shard_map/ppermute | solution.py:324
  9.9 6.2 %collective-permute-start.4 = (f32[8,3,512]{2,1,0:T(4,128)S(1)}, f32[8,3,512]{2,1,0:T(4,128)S(1)}, u32[]{:S(2)}, u32[]{:S(2)}) collective-permute-start(f32[8,3,512]{2,1,0:T(4,128)S(1)} %get-tuple-element.109), channel_id=1, source_target_pairs={{0,7},{1,6},{2,1},{3,0},{4,3},{5,2},{6,5},{7,4},{8,15},{9,14},{10,... | collective-permute-start | bytes 147464 | tf_op jit(solution)/shard_map/ppermute | solution.py:320
  13.7 7.0 %collective-permute-start.2 = (f32[8,3,512]{2,1,0:T(4,128)S(1)}, f32[8,3,512]{2,1,0:T(4,128)S(1)}, u32[]{:S(2)}, u32[]{:S(2)}) collective-permute-start(f32[8,3,512]{2,1,0:T(4,128)S(1)} %get-tuple-element.110), channel_id=1, source_target_pairs={{0,3},{1,2},{2,5},{3,4},{4,7},{5,6},{6,1},{7,0},{8,11},{9,10},{10,... | collective-permute-start | bytes 147464 | tf_op jit(solution)/shard_map/ppermute | solution.py:320
  68.6 7.3 %collective-permute-start.7 = (f32[4160,128]{1,0:T(8,128)}, f32[4160,128]{1,0:T(8,128)}, u32[]{:S(2)}, u32[]{:S(2)}) collective-permute-start(f32[4160,128]{1,0:T(8,128)} %get-tuple-element.46), channel_id=1, source_target_pairs={{0,8},{8,0},{16,24},{24,16},{1,9},{9,1},{17,25},{25,17},{2,10},{10... | collective-permute-start | bytes 6389768 | tf_op jit(solution)/shard_map/ppermute | solution.py:372
  77.7 10.7 %collective-permute-start.10 = (f32[672,128]{1,0:T(8,128)}, f32[672,128]{1,0:T(8,128)}, u32[]{:S(2)}, u32[]{:S(2)}) collective-permute-start(f32[672,128]{1,0:T(8,128)} %dynamic-slice_add_fusion.2), channel_id=1, source_target_pairs={{0,2},{2,0},{4,6},{6,4},{1,3},{3,1},{5,7},{7,5},{8,10},{10,8},{12,... | collective-permute-start | bytes 1032200 | tf_op jit(solution)/shard_map/ppermute | solution.py:372
  79.9 10.9 %collective-permute-start.9 = (f32[704,128]{1,0:T(8,128)}, f32[704,128]{1,0:T(8,128)S(1)}, u32[]{:S(2)}, u32[]{:S(2)}) collective-permute-start(f32[704,128]{1,0:T(8,128)} %get-tuple-element.83), channel_id=1, source_target_pairs={{0,1},{1,0},{2,3},{3,2},{4,5},{5,4},{6,7},{7,6},{8,9},{9,8},{10,11... | collective-permute-start | bytes 1081352 | tf_op jit(solution)/shard_map/ppermute | solution.py:372
  81.4 11.4 %collective-permute-start.8 = (f32[704,128]{1,0:T(8,128)S(1)}, f32[704,128]{1,0:T(8,128)S(1)}, u32[]{:S(2)}, u32[]{:S(2)}) collective-permute-start(f32[704,128]{1,0:T(8,128)S(1)} %get-tuple-element.84), channel_id=1, source_target_pairs={{0,16},{8,24},{16,0},{24,8},{1,17},{9,25},{17,1},{25,9},{2,18},{10... | collective-permute-start | bytes 1081352 | tf_op jit(solution)/shard_map/ppermute | solution.py:372
  84.0 10.3 %collective-permute-start.11 = (f32[3,48,512]{2,1,0:T(8,128)S(1)}, f32[3,48,512]{2,1,0:T(8,128)S(1)}, u32[]{:S(2)}, u32[]{:S(2)}) collective-permute-start(f32[3,48,512]{2,1,0:T(8,128)S(1)} %copy-done.5), channel_id=1, source_target_pairs={{0,8},{8,16},{16,24},{1,9},{9,17},{17,25},{2,10},{10,18},{18,26},{... | collective-permute-start | bytes 884744 | tf_op jit(solution)/shard_map/ppermute | solution.py:311
  85.5 8.8 %collective-permute-start.12 = (f32[3,48,512]{2,1,0:T(8,128)S(1)}, f32[3,48,512]{2,1,0:T(8,128)S(1)}, u32[]{:S(2)}, u32[]{:S(2)}) collective-permute-start(f32[3,48,512]{2,1,0:T(8,128)S(1)} %copy-done.3), channel_id=1, source_target_pairs={{8,0},{16,8},{24,16},{9,1},{17,9},{25,17},{10,2},{18,10},{26,18},{... | collective-permute-start | bytes 884744 | tf_op jit(solution)/shard_map/ppermute | solution.py:311
  94.4 9.5 %collective-permute-start.16 = (f32[336,128]{1,0:T(8,128)S(1)}, f32[336,128]{1,0:T(8,128)S(1)}, u32[]{:S(2)}, u32[]{:S(2)}) collective-permute-start(f32[336,128]{1,0:T(8,128)S(1)} %constant_dynamic-slice_fusion.3), channel_id=1, source_target_pairs={{0,16},{8,24},{16,0},{24,8},{1,17},{9,25},{17,1},{25,9},{2,18},{10... | collective-permute-start | bytes 516104 | tf_op jit(solution)/shard_map/ppermute | solution.py:372
  97.5 12.4 %collective-permute-start.15 = (f32[352,128]{1,0:T(8,128)S(1)}, f32[352,128]{1,0:T(8,128)S(1)}, u32[]{:S(2)}, u32[]{:S(2)}) collective-permute-start(f32[352,128]{1,0:T(8,128)S(1)} %constant_dynamic-slice_fusion.4), channel_id=1, source_target_pairs={{0,2},{2,0},{4,6},{6,4},{1,3},{3,1},{5,7},{7,5},{8,10},{10,8},{12,... | collective-permute-start | bytes 540680 | tf_op jit(solution)/shard_map/ppermute | solution.py:372
  99.3 10.9 %collective-permute-start.13 = (f32[352,128]{1,0:T(8,128)S(1)}, f32[352,128]{1,0:T(8,128)S(1)}, u32[]{:S(2)}, u32[]{:S(2)}) collective-permute-start(f32[352,128]{1,0:T(8,128)S(1)} %constant_dynamic-slice_fusion.5), channel_id=1, source_target_pairs={{0,1},{1,0},{2,3},{3,2},{4,5},{5,4},{6,7},{7,6},{8,9},{9,8},{10,11... | collective-permute-start | bytes 540680 | tf_op jit(solution)/shard_map/ppermute | solution.py:372
  100.0 15.6 %collective-permute-start.20 = (f32[8,9,512]{2,1,0:T(8,128)S(1)}, f32[8,9,512]{2,1,0:T(8,128)S(1)}, u32[]{:S(2)}, u32[]{:S(2)}) collective-permute-start(f32[8,9,512]{2,1,0:T(8,128)S(1)} %get-tuple-element.85), channel_id=1, source_target_pairs={{0,2},{2,4},{4,6},{6,0},{1,3},{3,5},{5,7},{7,1},{8,10},{10,12},{12... | collective-permute-start | bytes 442376 | tf_op jit(solution)/shard_map/ppermute | solution.py:311
  100.4 15.3 %collective-permute-start.19 = (f32[8,9,512]{2,1,0:T(8,128)S(1)}, f32[8,9,512]{2,1,0:T(8,128)S(1)}, u32[]{:S(2)}, u32[]{:S(2)}) collective-permute-start(f32[8,9,512]{2,1,0:T(8,128)S(1)} %get-tuple-element.86), channel_id=1, source_target_pairs={{2,0},{4,2},{6,4},{0,6},{3,1},{5,3},{7,5},{1,7},{10,8},{12,10},{14... | collective-permute-start | bytes 442376 | tf_op jit(solution)/shard_map/ppermute | solution.py:311
  104.0 6.4 %collective-permute-start.18 = (f32[168,128]{1,0:T(8,128)S(1)}, f32[168,128]{1,0:T(8,128)S(1)}, u32[]{:S(2)}, u32[]{:S(2)}) collective-permute-start(f32[168,128]{1,0:T(8,128)S(1)} %constant_dynamic-slice_fusion), channel_id=1, source_target_pairs={{0,1},{1,0},{2,3},{3,2},{4,5},{5,4},{6,7},{7,6},{8,9},{9,8},{10,11... | collective-permute-start | bytes 258056 | tf_op jit(solution)/shard_map/ppermute | solution.py:372
  115.7 12.6 %collective-permute-start.21 = (f32[520,128]{1,0:T(8,128)S(1)}, f32[520,128]{1,0:T(8,128)S(1)}, u32[]{:S(2)}, u32[]{:S(2)}) collective-permute-start(f32[520,128]{1,0:T(8,128)S(1)} %pad_maximum_fusion.3), channel_id=1, source_target_pairs={{0,4},{2,6},{4,0},{6,2},{1,5},{3,7},{5,1},{7,3},{8,12},{10,14},{12... | collective-permute-start | bytes 798728 | tf_op jit(solution)/shard_map/ppermute | solution.py:372
  116.0 12.3 %collective-permute-start.22 = (f32[8,8,512]{2,1,0:T(8,128)S(1)}, f32[8,8,512]{2,1,0:T(8,128)S(1)}, u32[]{:S(2)}, u32[]{:S(2)}) collective-permute-start(f32[8,8,512]{2,1,0:T(8,128)S(1)} %fusion), channel_id=1, source_target_pairs={{0,1},{1,0},{2,3},{3,2},{4,5},{5,4},{6,7},{7,6},{8,9},{9,8},{10,11... | collective-permute-start | bytes 393224 | tf_op jit(solution)/shard_map/ppermute | solution.py:324
  133.2 6.2 %collective-permute-start.29 = (f32[336,128]{1,0:T(8,128)S(1)}, f32[336,128]{1,0:T(8,128)S(1)}, u32[]{:S(2)}, u32[]{:S(2)}) collective-permute-start(f32[336,128]{1,0:T(8,128)S(1)} %pad_maximum_fusion.6), channel_id=1, source_target_pairs={{0,16},{8,24},{16,0},{24,8},{1,17},{9,25},{17,1},{25,9},{2,18},{10... | collective-permute-start | bytes 516104 | tf_op jit(solution)/shard_map/ppermute | solution.py:372
  139.2 6.1 %collective-permute-start.28 = (f32[352,128]{1,0:T(8,128)S(1)}, f32[352,128]{1,0:T(8,128)S(1)}, u32[]{:S(2)}, u32[]{:S(2)}) collective-permute-start(f32[352,128]{1,0:T(8,128)S(1)} %pad_maximum_fusion.5), channel_id=1, source_target_pairs={{0,2},{2,0},{4,6},{6,4},{1,3},{3,1},{5,7},{7,5},{8,10},{10,8},{12,... | collective-permute-start | bytes 540680 | tf_op jit(solution)/shard_map/ppermute | solution.py:372
  145.4 8.3 %collective-permute-start.30 = (f32[704,128]{1,0:T(8,128)S(1)}, f32[704,128]{1,0:T(8,128)S(1)}, u32[]{:S(2)}, u32[]{:S(2)}) collective-permute-start(f32[704,128]{1,0:T(8,128)S(1)} %pad_maximum_fusion.1), channel_id=1, source_target_pairs={{0,1},{1,0},{2,3},{3,2},{4,5},{5,4},{6,7},{7,6},{8,9},{9,8},{10,11... | collective-permute-start | bytes 1081352 | tf_op jit(solution)/shard_map/ppermute | solution.py:372
  145.5 8.2 %collective-permute-start.27 = (f32[704,128]{1,0:T(8,128)S(1)}, f32[704,128]{1,0:T(8,128)S(1)}, u32[]{:S(2)}, u32[]{:S(2)}) collective-permute-start(f32[704,128]{1,0:T(8,128)S(1)} %pad_maximum_fusion), channel_id=1, source_target_pairs={{0,16},{8,24},{16,0},{24,8},{1,17},{9,25},{17,1},{25,9},{2,18},{10... | collective-permute-start | bytes 1081352 | tf_op jit(solution)/shard_map/ppermute | solution.py:372
  146.4 7.3 %collective-permute-start.31 = (f32[672,128]{1,0:T(8,128)S(1)}, f32[672,128]{1,0:T(8,128)S(1)}, u32[]{:S(2)}, u32[]{:S(2)}) collective-permute-start(f32[672,128]{1,0:T(8,128)S(1)} %pad_maximum_fusion.2), channel_id=1, source_target_pairs={{0,2},{2,0},{4,6},{6,4},{1,3},{3,1},{5,7},{7,5},{8,10},{10,8},{12,... | collective-permute-start | bytes 1032200 | tf_op jit(solution)/shard_map/ppermute | solution.py:372
  (19 other events, 124.4 us)

commit v3 on v2

--- a/solution.py
+++ b/solution.py
@@ -263,7 +263,7 @@
             ],
         ),
         out_shape=outs,
-        compiler_params=pltpu.CompilerParams(vmem_limit_bytes=48 * 1024 * 1024),
+        compiler_params=pltpu.CompilerParams(vmem_limit_bytes=54 * 1024 * 1024),
         cost_estimate=pl.CostEstimate(flops=20_000_000_000, bytes_accessed=24_000_000, transcendentals=2_000_000),
         name="attention",
     )(pos, top, mid, bot, gain.reshape(1, D), w_qkv, w_qkv, w_qkv, w_out, cot, bias, bias)

time: 163 us -> 161 us (0.988)
  local copies, waits for them, and re-layouts: 11.7 us -> 7.43 us
  Pallas kernels: 40.9 us -> 42.8 us
    unnamed x20 -> x18, local copies, waits for them, and re-layouts: 4.81 us -> 1.55 us
    pallas_call x1, Pallas kernels: 36.1 us -> 38.2 us  [attention(): pl.pallas_call(attention_kernel, grid_spec=pltpu.PrefetchScalarGridSpec(n...]
where the time goes in v3:
time: 161 us; the launch traced here: 160 us
  waiting for transfers between devices  54.1 us (34%)
  starting transfers between devices  47.1 us (29%)
  Pallas kernels  42.8 us (27%)
  other arithmetic  7.71 us (5%)
  local copies, waits for them, and re-layouts  7.43 us (5%)
    ppermute x21, waiting for transfers between devices, swap_bit(): lax.ppermute(x, axis, [(i, i ^ 1 << bit) for i in range(lax.axis_size(axi...  47.1 us
    pallas_call x1, Pallas kernels, attention(): pl.pallas_call(attention_kernel, grid_spec=pltpu.PrefetchScalarGridSpec(n...  38.2 us
    ppermute x21, starting transfers between devices, swap_bit(): lax.ppermute(x, axis, [(i, i ^ 1 << bit) for i in range(lax.axis_size(axi...  24 us
    ppermute x8, starting transfers between devices, shift(): return lax.ppermute(x, axis, pairs)  16.1 us
    ppermute x2, waiting for transfers between devices, shift_across(): return lax.ppermute(x, ('lon', 'lev'), pairs)  6.96 us
    pallas_call x1, Pallas kernels, unpack(): pl.pallas_call(lambda *refs: unpack_kernel(factor, *refs), in_specs=[pl.B...  4.16 us
    add x2, other arithmetic, half(): sum((lax.dynamic_slice_in_dim(x, start + which * n, n, 0) for x in terms))  3.96 us
    ppermute x2, starting transfers between devices, shift_across(): return lax.ppermute(x, ('lon', 'lev'), pairs)  3.82 us
  transfers between devices with their start and end apart: 33, of which 16 were waited for; matrix products, arithmetic and copies ran while one was open for 6% of the time, Pallas kernels for 0%

profile of v3, /device:TPU:0, one launch (start us, length us, event | category | flops | bytes accessed | tf_op | source)
XLA Modules:
  0.0 160.3 jit_solution(15323982145744848304)
XLA Ops:
  1.8 5.1 %collective-permute-start.3 = (f32[8,6,512]{2,1,0:T(8,128)S(1)}, f32[8,6,512]{2,1,0:T(8,128)S(1)}, u32[]{:S(2)}, u32[]{:S(2)}) collective-permute-start(f32[8,6,512]{2,1,0:T(8,128)S(1)} %get-tuple-element.105), channel_id=1, source_target_pairs={{2,0},{4,2},{6,4},{0,6},{3,1},{5,3},{7,5},{1,7},{10,8},{12,10},{14... | collective-permute-start | bytes 294920 | tf_op jit(solution)/shard_map/ppermute | solution.py:311
  9.9 3.8 %collective-permute-start.4 = (f32[8,3,512]{2,1,0:T(4,128)S(1)}, f32[8,3,512]{2,1,0:T(4,128)S(1)}, u32[]{:S(2)}, u32[]{:S(2)}) collective-permute-start(f32[8,3,512]{2,1,0:T(4,128)S(1)} %get-tuple-element.109), channel_id=1, source_target_pairs={{0,7},{1,6},{2,1},{3,0},{4,3},{5,2},{6,5},{7,4},{8,15},{9,14},{10,... | collective-permute-start | bytes 147464 | tf_op jit(solution)/shard_map/ppermute | solution.py:320
  13.7 2.4 %collective-permute-done.4 = f32[8,3,512]{2,1,0:T(4,128)S(1)} collective-permute-done((f32[8,3,512]{2,1,0:T(4,128)S(1)}, f32[8,3,512]{2,1,0:T(4,128)S(1)}, u32[]{:S(2)}, u32[]{:S(2)}) %collective-permute-start.4) | collective-permute-done | bytes 49184 | tf_op jit(solution)/shard_map/ppermute | solution.py:320
  16.1 4.5 %collective-permute-done.2 = f32[8,3,512]{2,1,0:T(4,128)S(1)} collective-permute-done((f32[8,3,512]{2,1,0:T(4,128)S(1)}, f32[8,3,512]{2,1,0:T(4,128)S(1)}, u32[]{:S(2)}, u32[]{:S(2)}) %collective-permute-start.2) | collective-permute-done | bytes 49184 | tf_op jit(solution)/shard_map/ppermute | solution.py:320
  22.6 3.0 %collective-permute-start.5 = (f32[3,48,512]{2,1,0:T(8,128)S(1)}, f32[3,48,512]{2,1,0:T(8,128)S(1)}, u32[]{:S(2)}, u32[]{:S(2)}) collective-permute-start(f32[3,48,512]{2,1,0:T(8,128)S(1)} %get-tuple-element.88), channel_id=1, source_target_pairs={{0,8},{8,16},{16,24},{1,9},{9,17},{17,25},{2,10},{10,18},{18,26},{... | collective-permute-start | bytes 884744 | tf_op jit(solution)/shard_map/ppermute | solution.py:311
  28.0 38.2 %attention.1 = (f32[128,512]{1,0:T(8,128)}, f32[3,48,512]{2,1,0:T(8,128)}, f32[8,48,512]{2,1,0:T(8,128)}, f32[3,48,512]{2,1,0:T(8,128)}, f32[4160,128]{1,0:T(8,128)}, /*index=5*/f32[4160,128]{1,0:T(8,128)}) custom-call(s32[3]{0:T(128)} %pad_add_fusion.1.pos_ref, f32[3,48,512]{2,1,0:T(8,128)} %copy-done.8, f32[8,48,512]{2,1,0:T(8,128)} %copy-done.2, ...), custom_call_target="tpu_custom_call" | custom-call | flops 20000000000 | bytes 24000000 | tf_op jit(solution)/shard_map/attention/pallas_call | solution.py:238
  66.2 3.1 %collective-permute-start.7 = (f32[4160,128]{1,0:T(8,128)}, f32[4160,128]{1,0:T(8,128)}, u32[]{:S(2)}, u32[]{:S(2)}) collective-permute-start(f32[4160,128]{1,0:T(8,128)} %get-tuple-element.46), channel_id=1, source_target_pairs={{0,8},{8,0},{16,24},{24,16},{1,9},{9,1},{17,25},{25,17},{2,10},{10... | collective-permute-start | bytes 6389768 | tf_op jit(solution)/shard_map/ppermute | solution.py:372
  69.3 4.2 %collective-permute-done.7 = f32[4160,128]{1,0:T(8,128)} collective-permute-done((f32[4160,128]{1,0:T(8,128)}, f32[4160,128]{1,0:T(8,128)}, u32[]{:S(2)}, u32[]{:S(2)}) %collective-permute-start.7) | collective-permute-done | bytes 2129952 | tf_op jit(solution)/shard_map/ppermute | solution.py:372
  73.5 1.8 %dynamic-slice_add_fusion.2 = f32[672,128]{1,0:T(8,128)} fusion(f32[4160,128]{1,0:T(8,128)} %collective-permute-done.7, s32[]{:T(128)S(6)} %select_n.179, f32[4160,128]{1,0:T(8,128)} %get-tuple-element.45), kind=kLoop, calls=%fused_computation.15 | loop fusion | flops 86016 | bytes 1032196 | tf_op jit(solution)/shard_map/add | solution.py:379
  75.4 2.1 %dynamic-slice_add_fusion = (f32[704,128]{1,0:T(8,128)}, f32[704,128]{1,0:T(8,128)S(1)}) fusion(f32[4160,128]{1,0:T(8,128)} %collective-permute-done.7, s32[]{:T(128)S(6)} %select_n.178, f32[4160,128]{1,0:T(8,128)} %get-tuple-element.45, s32[]{:T(128)S(6)} %select_n.177), kind=kLoop, calls=%fused_computation.8 | loop fusion | flops 180224 | bytes 2162696 | tf_op jit(solution)/shard_map/add | solution.py:379
  79.0 2.7 %collective-permute-start.8 = (f32[704,128]{1,0:T(8,128)S(1)}, f32[704,128]{1,0:T(8,128)S(1)}, u32[]{:S(2)}, u32[]{:S(2)}) collective-permute-start(f32[704,128]{1,0:T(8,128)S(1)} %get-tuple-element.84), channel_id=1, source_target_pairs={{0,16},{8,24},{16,0},{24,8},{1,17},{9,25},{17,1},{25,9},{2,18},{10... | collective-permute-start | bytes 1081352 | tf_op jit(solution)/shard_map/ppermute | solution.py:372
  88.4 2.2 %collective-permute-done.8 = f32[704,128]{1,0:T(8,128)S(1)} collective-permute-done((f32[704,128]{1,0:T(8,128)S(1)}, f32[704,128]{1,0:T(8,128)S(1)}, u32[]{:S(2)}, u32[]{:S(2)}) %collective-permute-start.8) | collective-permute-done | bytes 360480 | tf_op jit(solution)/shard_map/ppermute | solution.py:372
  91.8 3.4 %collective-permute-start.16 = (f32[336,128]{1,0:T(8,128)S(1)}, f32[336,128]{1,0:T(8,128)S(1)}, u32[]{:S(2)}, u32[]{:S(2)}) collective-permute-start(f32[336,128]{1,0:T(8,128)S(1)} %constant_dynamic-slice_fusion.3), channel_id=1, source_target_pairs={{0,16},{8,24},{16,0},{24,8},{1,17},{9,25},{17,1},{25,9},{2,18},{10... | collective-permute-start | bytes 516104 | tf_op jit(solution)/shard_map/ppermute | solution.py:372
  98.1 3.5 %collective-permute-start.19 = (f32[8,9,512]{2,1,0:T(8,128)S(1)}, f32[8,9,512]{2,1,0:T(8,128)S(1)}, u32[]{:S(2)}, u32[]{:S(2)}) collective-permute-start(f32[8,9,512]{2,1,0:T(8,128)S(1)} %get-tuple-element.86), channel_id=1, source_target_pairs={{2,0},{4,2},{6,4},{0,6},{3,1},{5,3},{7,5},{1,7},{10,8},{12,10},{14... | collective-permute-start | bytes 442376 | tf_op jit(solution)/shard_map/ppermute | solution.py:311
  103.3 4.3 %collective-permute-done.15 = f32[352,128]{1,0:T(8,128)S(1)} collective-permute-done((f32[352,128]{1,0:T(8,128)S(1)}, f32[352,128]{1,0:T(8,128)S(1)}, u32[]{:S(2)}, u32[]{:S(2)}) %collective-permute-start.15) | collective-permute-done | bytes 180256 | tf_op jit(solution)/shard_map/ppermute | solution.py:372
  108.1 4.2 %collective-permute-done.17 = f32[176,128]{1,0:T(8,128)S(1)} collective-permute-done((f32[176,128]{1,0:T(8,128)S(1)}, f32[176,128]{1,0:T(8,128)S(1)}, u32[]{:S(2)}, u32[]{:S(2)}) %collective-permute-start.17) | collective-permute-done | bytes 90144 | tf_op jit(solution)/shard_map/ppermute | solution.py:372
  115.3 10.7 %collective-permute-done.21 = f32[520,128]{1,0:T(8,128)S(1)} collective-permute-done((f32[520,128]{1,0:T(8,128)S(1)}, f32[520,128]{1,0:T(8,128)S(1)}, u32[]{:S(2)}, u32[]{:S(2)}) %collective-permute-start.21) | collective-permute-done | bytes 266272 | tf_op jit(solution)/shard_map/ppermute | solution.py:372
  128.5 2.3 %collective-permute-start.25 = (f32[176,128]{1,0:T(8,128)S(1)}, f32[176,128]{1,0:T(8,128)S(1)}, u32[]{:S(2)}, u32[]{:S(2)}) collective-permute-start(f32[176,128]{1,0:T(8,128)S(1)} %get-tuple-element.103), channel_id=1, source_target_pairs={{0,16},{8,24},{16,0},{24,8},{1,17},{9,25},{17,1},{25,9},{2,18},{10... | collective-permute-start | bytes 270344 | tf_op jit(solution)/shard_map/ppermute | solution.py:372
  130.9 2.5 %collective-permute-start.29 = (f32[336,128]{1,0:T(8,128)S(1)}, f32[336,128]{1,0:T(8,128)S(1)}, u32[]{:S(2)}, u32[]{:S(2)}) collective-permute-start(f32[336,128]{1,0:T(8,128)S(1)} %pad_maximum_fusion.6), channel_id=1, source_target_pairs={{0,16},{8,24},{16,0},{24,8},{1,17},{9,25},{17,1},{25,9},{2,18},{10... | collective-permute-start | bytes 516104 | tf_op jit(solution)/shard_map/ppermute | solution.py:372
  137.1 3.9 %collective-permute-done.24 = f32[352,128]{1,0:T(8,128)S(1)} collective-permute-done((f32[352,128]{1,0:T(8,128)S(1)}, f32[352,128]{1,0:T(8,128)S(1)}, u32[]{:S(2)}, u32[]{:S(2)}) %collective-permute-start.24) | collective-permute-done | bytes 180256 | tf_op jit(solution)/shard_map/ppermute | solution.py:372
  141.1 2.0 %collective-permute-done.28 = f32[352,128]{1,0:T(8,128)S(1)} collective-permute-done((f32[352,128]{1,0:T(8,128)S(1)}, f32[352,128]{1,0:T(8,128)S(1)}, u32[]{:S(2)}, u32[]{:S(2)}) %collective-permute-start.28) | collective-permute-done | bytes 180256 | tf_op jit(solution)/shard_map/ppermute | solution.py:372
  144.2 7.2 %collective-permute-done.31 = f32[672,128]{1,0:T(8,128)S(1)} collective-permute-done((f32[672,128]{1,0:T(8,128)S(1)}, f32[672,128]{1,0:T(8,128)S(1)}, u32[]{:S(2)}, u32[]{:S(2)}) %collective-permute-start.31) | collective-permute-done | bytes 344096 | tf_op jit(solution)/shard_map/ppermute | solution.py:372
  153.4 2.8 %collective-permute-done.32.refs_2_ = f32[4160,128]{1,0:T(8,128)} collective-permute-done((f32[4160,128]{1,0:T(8,128)S(1)}, f32[4160,128]{1,0:T(8,128)}, u32[]{:S(2)}, u32[]{:S(2)}) %collective-permute-start.32) | collective-permute-done | bytes 2129952 | tf_op jit(solution)/shard_map/ppermute | solution.py:372
  156.2 4.2 %unpack.1 = (f32[4,128]{1,0:T(4,128)}, f32[512,1536]{1,0:T(8,128)}, f32[4,128,512]{2,1,0:T(8,128)}) custom-call(s32[1]{0:T(128)} %bitcast.refs_0_, f32[4160,128]{1,0:T(8,128)S(1)} %select_dynamic-update-slice_fusion.4.refs_1_, f32[4160,128]{1,0:T(8,128)} %collective-permute-done.32.refs_2_), custom_call_target="tpu_custom_call" | custom-call | flops 1000000 | bytes 8000000 | tf_op jit(solution)/shard_map/unpack/pallas_call | solution.py:290
  (116 shorter events, 34.9 us)
Async XLA Ops:
  1.8 18.9 %collective-permute-start.3 = (f32[8,6,512]{2,1,0:T(8,128)S(1)}, f32[8,6,512]{2,1,0:T(8,128)S(1)}, u32[]{:S(2)}, u32[]{:S(2)}) collective-permute-start(f32[8,6,512]{2,1,0:T(8,128)S(1)} %get-tuple-element.105), channel_id=1, source_target_pairs={{2,0},{4,2},{6,4},{0,6},{3,1},{5,3},{7,5},{1,7},{10,8},{12,10},{14... | collective-permute-start | bytes 294920 | tf_op jit(solution)/shard_map/ppermute | solution.py:311
  6.9 13.8 %collective-permute-start.1 = (f32[8,6,512]{2,1,0:T(8,128)S(1)}, f32[8,6,512]{2,1,0:T(8,128)S(1)}, u32[]{:S(2)}, u32[]{:S(2)}) collective-permute-start(f32[8,6,512]{2,1,0:T(8,128)S(1)} %get-tuple-element.106), channel_id=1, source_target_pairs={{0,2},{2,4},{4,6},{6,0},{1,3},{3,5},{5,7},{7,1},{8,10},{10,12},{12... | collective-permute-start | bytes 294920 | tf_op jit(solution)/shard_map/ppermute | solution.py:311
  8.3 12.4 %collective-permute-start = (f32[8,8,512]{2,1,0:T(8,128)S(1)}, f32[8,8,512]{2,1,0:T(8,128)S(1)}, u32[]{:S(2)}, u32[]{:S(2)}) collective-permute-start(f32[8,8,512]{2,1,0:T(8,128)S(1)} %fusion.1), channel_id=1, source_target_pairs={{0,1},{1,0},{2,3},{3,2},{4,5},{5,4},{6,7},{7,6},{8,9},{9,8},{10,11... | collective-permute-start | bytes 393224 | tf_op jit(solution)/shard_map/ppermute | solution.py:324
  9.9 6.2 %collective-permute-start.4 = (f32[8,3,512]{2,1,0:T(4,128)S(1)}, f32[8,3,512]{2,1,0:T(4,128)S(1)}, u32[]{:S(2)}, u32[]{:S(2)}) collective-permute-start(f32[8,3,512]{2,1,0:T(4,128)S(1)} %get-tuple-element.109), channel_id=1, source_target_pairs={{0,7},{1,6},{2,1},{3,0},{4,3},{5,2},{6,5},{7,4},{8,15},{9,14},{10,... | collective-permute-start | bytes 147464 | tf_op jit(solution)/shard_map/ppermute | solution.py:320
  13.7 7.0 %collective-permute-start.2 = (f32[8,3,512]{2,1,0:T(4,128)S(1)}, f32[8,3,512]{2,1,0:T(4,128)S(1)}, u32[]{:S(2)}, u32[]{:S(2)}) collective-permute-start(f32[8,3,512]{2,1,0:T(4,128)S(1)} %get-tuple-element.110), channel_id=1, source_target_pairs={{0,3},{1,2},{2,5},{3,4},{4,7},{5,6},{6,1},{7,0},{8,11},{9,10},{10,... | collective-permute-start | bytes 147464 | tf_op jit(solution)/shard_map/ppermute | solution.py:320
  66.2 7.3 %collective-permute-start.7 = (f32[4160,128]{1,0:T(8,128)}, f32[4160,128]{1,0:T(8,128)}, u32[]{:S(2)}, u32[]{:S(2)}) collective-permute-start(f32[4160,128]{1,0:T(8,128)} %get-tuple-element.46), channel_id=1, source_target_pairs={{0,8},{8,0},{16,24},{24,16},{1,9},{9,1},{17,25},{25,17},{2,10},{10... | collective-permute-start | bytes 6389768 | tf_op jit(solution)/shard_map/ppermute | solution.py:372
  75.4 10.7 %collective-permute-start.10 = (f32[672,128]{1,0:T(8,128)}, f32[672,128]{1,0:T(8,128)}, u32[]{:S(2)}, u32[]{:S(2)}) collective-permute-start(f32[672,128]{1,0:T(8,128)} %dynamic-slice_add_fusion.2), channel_id=1, source_target_pairs={{0,2},{2,0},{4,6},{6,4},{1,3},{3,1},{5,7},{7,5},{8,10},{10,8},{12,... | collective-permute-start | bytes 1032200 | tf_op jit(solution)/shard_map/ppermute | solution.py:372
  77.5 10.9 %collective-permute-start.9 = (f32[704,128]{1,0:T(8,128)}, f32[704,128]{1,0:T(8,128)S(1)}, u32[]{:S(2)}, u32[]{:S(2)}) collective-permute-start(f32[704,128]{1,0:T(8,128)} %get-tuple-element.83), channel_id=1, source_target_pairs={{0,1},{1,0},{2,3},{3,2},{4,5},{5,4},{6,7},{7,6},{8,9},{9,8},{10,11... | collective-permute-start | bytes 1081352 | tf_op jit(solution)/shard_map/ppermute | solution.py:372
  79.0 11.5 %collective-permute-start.8 = (f32[704,128]{1,0:T(8,128)S(1)}, f32[704,128]{1,0:T(8,128)S(1)}, u32[]{:S(2)}, u32[]{:S(2)}) collective-permute-start(f32[704,128]{1,0:T(8,128)S(1)} %get-tuple-element.84), channel_id=1, source_target_pairs={{0,16},{8,24},{16,0},{24,8},{1,17},{9,25},{17,1},{25,9},{2,18},{10... | collective-permute-start | bytes 1081352 | tf_op jit(solution)/shard_map/ppermute | solution.py:372
  81.7 10.0 %collective-permute-start.11 = (f32[3,48,512]{2,1,0:T(8,128)}, f32[3,48,512]{2,1,0:T(8,128)S(1)}, u32[]{:S(2)}, u32[]{:S(2)}) collective-permute-start(f32[3,48,512]{2,1,0:T(8,128)} %get-tuple-element.50), channel_id=1, source_target_pairs={{0,8},{8,16},{16,24},{1,9},{9,17},{17,25},{2,10},{10,18},{18,26},{... | collective-permute-start | bytes 884744 | tf_op jit(solution)/shard_map/ppermute | solution.py:311
  83.2 8.5 %collective-permute-start.12 = (f32[3,48,512]{2,1,0:T(8,128)}, f32[3,48,512]{2,1,0:T(8,128)S(1)}, u32[]{:S(2)}, u32[]{:S(2)}) collective-permute-start(f32[3,48,512]{2,1,0:T(8,128)} %get-tuple-element.51), channel_id=1, source_target_pairs={{8,0},{16,8},{24,16},{9,1},{17,9},{25,17},{10,2},{18,10},{26,18},{... | collective-permute-start | bytes 884744 | tf_op jit(solution)/shard_map/ppermute | solution.py:311
  91.8 9.8 %collective-permute-start.16 = (f32[336,128]{1,0:T(8,128)S(1)}, f32[336,128]{1,0:T(8,128)S(1)}, u32[]{:S(2)}, u32[]{:S(2)}) collective-permute-start(f32[336,128]{1,0:T(8,128)S(1)} %constant_dynamic-slice_fusion.3), channel_id=1, source_target_pairs={{0,16},{8,24},{16,0},{24,8},{1,17},{9,25},{17,1},{25,9},{2,18},{10... | collective-permute-start | bytes 516104 | tf_op jit(solution)/shard_map/ppermute | solution.py:372
  95.2 12.4 %collective-permute-start.15 = (f32[352,128]{1,0:T(8,128)S(1)}, f32[352,128]{1,0:T(8,128)S(1)}, u32[]{:S(2)}, u32[]{:S(2)}) collective-permute-start(f32[352,128]{1,0:T(8,128)S(1)} %constant_dynamic-slice_fusion.4), channel_id=1, source_target_pairs={{0,2},{2,0},{4,6},{6,4},{1,3},{3,1},{5,7},{7,5},{8,10},{10,8},{12,... | collective-permute-start | bytes 540680 | tf_op jit(solution)/shard_map/ppermute | solution.py:372
  97.0 10.9 %collective-permute-start.13 = (f32[352,128]{1,0:T(8,128)S(1)}, f32[352,128]{1,0:T(8,128)S(1)}, u32[]{:S(2)}, u32[]{:S(2)}) collective-permute-start(f32[352,128]{1,0:T(8,128)S(1)} %constant_dynamic-slice_fusion.5), channel_id=1, source_target_pairs={{0,1},{1,0},{2,3},{3,2},{4,5},{5,4},{6,7},{7,6},{8,9},{9,8},{10,11... | collective-permute-start | bytes 540680 | tf_op jit(solution)/shard_map/ppermute | solution.py:372
  97.8 15.6 %collective-permute-start.20 = (f32[8,9,512]{2,1,0:T(8,128)S(1)}, f32[8,9,512]{2,1,0:T(8,128)S(1)}, u32[]{:S(2)}, u32[]{:S(2)}) collective-permute-start(f32[8,9,512]{2,1,0:T(8,128)S(1)} %get-tuple-element.85), channel_id=1, source_target_pairs={{0,2},{2,4},{4,6},{6,0},{1,3},{3,5},{5,7},{7,1},{8,10},{10,12},{12... | collective-permute-start | bytes 442376 | tf_op jit(solution)/shard_map/ppermute | solution.py:311
  98.1 15.3 %collective-permute-start.19 = (f32[8,9,512]{2,1,0:T(8,128)S(1)}, f32[8,9,512]{2,1,0:T(8,128)S(1)}, u32[]{:S(2)}, u32[]{:S(2)}) collective-permute-start(f32[8,9,512]{2,1,0:T(8,128)S(1)} %get-tuple-element.86), channel_id=1, source_target_pairs={{2,0},{4,2},{6,4},{0,6},{3,1},{5,3},{7,5},{1,7},{10,8},{12,10},{14... | collective-permute-start | bytes 442376 | tf_op jit(solution)/shard_map/ppermute | solution.py:311
  101.7 6.4 %collective-permute-start.18 = (f32[168,128]{1,0:T(8,128)S(1)}, f32[168,128]{1,0:T(8,128)S(1)}, u32[]{:S(2)}, u32[]{:S(2)}) collective-permute-start(f32[168,128]{1,0:T(8,128)S(1)} %constant_dynamic-slice_fusion), channel_id=1, source_target_pairs={{0,1},{1,0},{2,3},{3,2},{4,5},{5,4},{6,7},{7,6},{8,9},{9,8},{10,11... | collective-permute-start | bytes 258056 | tf_op jit(solution)/shard_map/ppermute | solution.py:372
  113.4 12.6 %collective-permute-start.21 = (f32[520,128]{1,0:T(8,128)S(1)}, f32[520,128]{1,0:T(8,128)S(1)}, u32[]{:S(2)}, u32[]{:S(2)}) collective-permute-start(f32[520,128]{1,0:T(8,128)S(1)} %pad_maximum_fusion.3), channel_id=1, source_target_pairs={{0,4},{2,6},{4,0},{6,2},{1,5},{3,7},{5,1},{7,3},{8,12},{10,14},{12... | collective-permute-start | bytes 798728 | tf_op jit(solution)/shard_map/ppermute | solution.py:372
  113.8 12.3 %collective-permute-start.22 = (f32[8,8,512]{2,1,0:T(8,128)S(1)}, f32[8,8,512]{2,1,0:T(8,128)S(1)}, u32[]{:S(2)}, u32[]{:S(2)}) collective-permute-start(f32[8,8,512]{2,1,0:T(8,128)S(1)} %fusion), channel_id=1, source_target_pairs={{0,1},{1,0},{2,3},{3,2},{4,5},{5,4},{6,7},{7,6},{8,9},{9,8},{10,11... | collective-permute-start | bytes 393224 | tf_op jit(solution)/shard_map/ppermute | solution.py:324
  130.9 6.1 %collective-permute-start.29 = (f32[336,128]{1,0:T(8,128)S(1)}, f32[336,128]{1,0:T(8,128)S(1)}, u32[]{:S(2)}, u32[]{:S(2)}) collective-permute-start(f32[336,128]{1,0:T(8,128)S(1)} %pad_maximum_fusion.6), channel_id=1, source_target_pairs={{0,16},{8,24},{16,0},{24,8},{1,17},{9,25},{17,1},{25,9},{2,18},{10... | collective-permute-start | bytes 516104 | tf_op jit(solution)/shard_map/ppermute | solution.py:372
  137.0 6.1 %collective-permute-start.28 = (f32[352,128]{1,0:T(8,128)S(1)}, f32[352,128]{1,0:T(8,128)S(1)}, u32[]{:S(2)}, u32[]{:S(2)}) collective-permute-start(f32[352,128]{1,0:T(8,128)S(1)} %pad_maximum_fusion.5), channel_id=1, source_target_pairs={{0,2},{2,0},{4,6},{6,4},{1,3},{3,1},{5,7},{7,5},{8,10},{10,8},{12,... | collective-permute-start | bytes 540680 | tf_op jit(solution)/shard_map/ppermute | solution.py:372
  143.1 8.4 %collective-permute-start.30 = (f32[704,128]{1,0:T(8,128)S(1)}, f32[704,128]{1,0:T(8,128)S(1)}, u32[]{:S(2)}, u32[]{:S(2)}) collective-permute-start(f32[704,128]{1,0:T(8,128)S(1)} %pad_maximum_fusion.1), channel_id=1, source_target_pairs={{0,1},{1,0},{2,3},{3,2},{4,5},{5,4},{6,7},{7,6},{8,9},{9,8},{10,11... | collective-permute-start | bytes 1081352 | tf_op jit(solution)/shard_map/ppermute | solution.py:372
  143.2 8.2 %collective-permute-start.27 = (f32[704,128]{1,0:T(8,128)S(1)}, f32[704,128]{1,0:T(8,128)S(1)}, u32[]{:S(2)}, u32[]{:S(2)}) collective-permute-start(f32[704,128]{1,0:T(8,128)S(1)} %pad_maximum_fusion), channel_id=1, source_target_pairs={{0,16},{8,24},{16,0},{24,8},{1,17},{9,25},{17,1},{25,9},{2,18},{10... | collective-permute-start | bytes 1081352 | tf_op jit(solution)/shard_map/ppermute | solution.py:372
  144.1 7.3 %collective-permute-start.31 = (f32[672,128]{1,0:T(8,128)S(1)}, f32[672,128]{1,0:T(8,128)S(1)}, u32[]{:S(2)}, u32[]{:S(2)}) collective-permute-start(f32[672,128]{1,0:T(8,128)S(1)} %pad_maximum_fusion.2), channel_id=1, source_target_pairs={{0,2},{2,0},{4,6},{6,4},{1,3},{3,1},{5,7},{7,5},{8,10},{10,8},{12,... | collective-permute-start | bytes 1032200 | tf_op jit(solution)/shard_map/ppermute | solution.py:372
  (18 other events, 147.0 us)

commit v4 on v3

--- a/solution.py
+++ b/solution.py
@@ -263,7 +263,7 @@
             ],
         ),
         out_shape=outs,
-        compiler_params=pltpu.CompilerParams(vmem_limit_bytes=54 * 1024 * 1024),
+        compiler_params=pltpu.CompilerParams(vmem_limit_bytes=58 * 1024 * 1024),
         cost_estimate=pl.CostEstimate(flops=20_000_000_000, bytes_accessed=24_000_000, transcendentals=2_000_000),
         name="attention",
     )(pos, top, mid, bot, gain.reshape(1, D), w_qkv, w_qkv, w_qkv, w_out, cot, bias, bias)

time: 161 us -> 161 us (level)
  no operation moved by 1% of the time
where the time goes in v4:
time: 161 us; the launch traced here: 160 us
  waiting for transfers between devices  54.1 us (34%)
  starting transfers between devices  47.1 us (29%)
  Pallas kernels  42.8 us (27%)
  other arithmetic  7.71 us (5%)
  local copies, waits for them, and re-layouts  7.43 us (5%)
    ppermute x21, waiting for transfers between devices, swap_bit(): lax.ppermute(x, axis, [(i, i ^ 1 << bit) for i in range(lax.axis_size(axi...  47.1 us
    pallas_call x1, Pallas kernels, attention(): pl.pallas_call(attention_kernel, grid_spec=pltpu.PrefetchScalarGridSpec(n...  38.2 us
    ppermute x21, starting transfers between devices, swap_bit(): lax.ppermute(x, axis, [(i, i ^ 1 << bit) for i in range(lax.axis_size(axi...  24 us
    ppermute x8, starting transfers between devices, shift(): return lax.ppermute(x, axis, pairs)  16.1 us
    ppermute x2, waiting for transfers between devices, shift_across(): return lax.ppermute(x, ('lon', 'lev'), pairs)  6.96 us
    pallas_call x1, Pallas kernels, unpack(): pl.pallas_call(lambda *refs: unpack_kernel(factor, *refs), in_specs=[pl.B...  4.16 us
    add x2, other arithmetic, half(): sum((lax.dynamic_slice_in_dim(x, start + which * n, n, 0) for x in terms))  3.96 us
    ppermute x2, starting transfers between devices, shift_across(): return lax.ppermute(x, ('lon', 'lev'), pairs)  3.82 us
  transfers between devices with their start and end apart: 33, of which 16 were waited for; matrix products, arithmetic and copies ran while one was open for 6% of the time, Pallas kernels for 0%

profile of v4, /device:TPU:0, one launch (start us, length us, event | category | flops | bytes accessed | tf_op | source)
XLA Modules:
  0.0 160.3 jit_solution(15323982145744848304)
XLA Ops:
  1.8 5.1 %collective-permute-start.3 = (f32[8,6,512]{2,1,0:T(8,128)S(1)}, f32[8,6,512]{2,1,0:T(8,128)S(1)}, u32[]{:S(2)}, u32[]{:S(2)}) collective-permute-start(f32[8,6,512]{2,1,0:T(8,128)S(1)} %get-tuple-element.105), channel_id=1, source_target_pairs={{2,0},{4,2},{6,4},{0,6},{3,1},{5,3},{7,5},{1,7},{10,8},{12,10},{14... | collective-permute-start | bytes 294920 | tf_op jit(solution)/shard_map/ppermute | solution.py:311
  9.9 3.8 %collective-permute-start.4 = (f32[8,3,512]{2,1,0:T(4,128)S(1)}, f32[8,3,512]{2,1,0:T(4,128)S(1)}, u32[]{:S(2)}, u32[]{:S(2)}) collective-permute-start(f32[8,3,512]{2,1,0:T(4,128)S(1)} %get-tuple-element.109), channel_id=1, source_target_pairs={{0,7},{1,6},{2,1},{3,0},{4,3},{5,2},{6,5},{7,4},{8,15},{9,14},{10,... | collective-permute-start | bytes 147464 | tf_op jit(solution)/shard_map/ppermute | solution.py:320
  13.7 2.4 %collective-permute-done.4 = f32[8,3,512]{2,1,0:T(4,128)S(1)} collective-permute-done((f32[8,3,512]{2,1,0:T(4,128)S(1)}, f32[8,3,512]{2,1,0:T(4,128)S(1)}, u32[]{:S(2)}, u32[]{:S(2)}) %collective-permute-start.4) | collective-permute-done | bytes 49184 | tf_op jit(solution)/shard_map/ppermute | solution.py:320
  16.1 4.5 %collective-permute-done.2 = f32[8,3,512]{2,1,0:T(4,128)S(1)} collective-permute-done((f32[8,3,512]{2,1,0:T(4,128)S(1)}, f32[8,3,512]{2,1,0:T(4,128)S(1)}, u32[]{:S(2)}, u32[]{:S(2)}) %collective-permute-start.2) | collective-permute-done | bytes 49184 | tf_op jit(solution)/shard_map/ppermute | solution.py:320
  22.6 3.0 %collective-permute-start.5 = (f32[3,48,512]{2,1,0:T(8,128)S(1)}, f32[3,48,512]{2,1,0:T(8,128)S(1)}, u32[]{:S(2)}, u32[]{:S(2)}) collective-permute-start(f32[3,48,512]{2,1,0:T(8,128)S(1)} %get-tuple-element.88), channel_id=1, source_target_pairs={{0,8},{8,16},{16,24},{1,9},{9,17},{17,25},{2,10},{10,18},{18,26},{... | collective-permute-start | bytes 884744 | tf_op jit(solution)/shard_map/ppermute | solution.py:311
  28.0 38.2 %attention.1 = (f32[128,512]{1,0:T(8,128)}, f32[3,48,512]{2,1,0:T(8,128)}, f32[8,48,512]{2,1,0:T(8,128)}, f32[3,48,512]{2,1,0:T(8,128)}, f32[4160,128]{1,0:T(8,128)}, /*index=5*/f32[4160,128]{1,0:T(8,128)}) custom-call(s32[3]{0:T(128)} %pad_add_fusion.1.pos_ref, f32[3,48,512]{2,1,0:T(8,128)} %copy-done.8, f32[8,48,512]{2,1,0:T(8,128)} %copy-done.2, ...), custom_call_target="tpu_custom_call" | custom-call | flops 20000000000 | bytes 24000000 | tf_op jit(solution)/shard_map/attention/pallas_call | solution.py:238
  66.2 3.1 %collective-permute-start.7 = (f32[4160,128]{1,0:T(8,128)}, f32[4160,128]{1,0:T(8,128)}, u32[]{:S(2)}, u32[]{:S(2)}) collective-permute-start(f32[4160,128]{1,0:T(8,128)} %get-tuple-element.46), channel_id=1, source_target_pairs={{0,8},{8,0},{16,24},{24,16},{1,9},{9,1},{17,25},{25,17},{2,10},{10... | collective-permute-start | bytes 6389768 | tf_op jit(solution)/shard_map/ppermute | solution.py:372
  69.3 4.2 %collective-permute-done.7 = f32[4160,128]{1,0:T(8,128)} collective-permute-done((f32[4160,128]{1,0:T(8,128)}, f32[4160,128]{1,0:T(8,128)}, u32[]{:S(2)}, u32[]{:S(2)}) %collective-permute-start.7) | collective-permute-done | bytes 2129952 | tf_op jit(solution)/shard_map/ppermute | solution.py:372
  73.5 1.8 %dynamic-slice_add_fusion.2 = f32[672,128]{1,0:T(8,128)} fusion(f32[4160,128]{1,0:T(8,128)} %collective-permute-done.7, s32[]{:T(128)S(6)} %select_n.179, f32[4160,128]{1,0:T(8,128)} %get-tuple-element.45), kind=kLoop, calls=%fused_computation.15 | loop fusion | flops 86016 | bytes 1032196 | tf_op jit(solution)/shard_map/add | solution.py:379
  75.4 2.1 %dynamic-slice_add_fusion = (f32[704,128]{1,0:T(8,128)}, f32[704,128]{1,0:T(8,128)S(1)}) fusion(f32[4160,128]{1,0:T(8,128)} %collective-permute-done.7, s32[]{:T(128)S(6)} %select_n.178, f32[4160,128]{1,0:T(8,128)} %get-tuple-element.45, s32[]{:T(128)S(6)} %select_n.177), kind=kLoop, calls=%fused_computation.8 | loop fusion | flops 180224 | bytes 2162696 | tf_op jit(solution)/shard_map/add | solution.py:379
  79.0 2.7 %collective-permute-start.8 = (f32[704,128]{1,0:T(8,128)S(1)}, f32[704,128]{1,0:T(8,128)S(1)}, u32[]{:S(2)}, u32[]{:S(2)}) collective-permute-start(f32[704,128]{1,0:T(8,128)S(1)} %get-tuple-element.84), channel_id=1, source_target_pairs={{0,16},{8,24},{16,0},{24,8},{1,17},{9,25},{17,1},{25,9},{2,18},{10... | collective-permute-start | bytes 1081352 | tf_op jit(solution)/shard_map/ppermute | solution.py:372
  88.4 2.2 %collective-permute-done.8 = f32[704,128]{1,0:T(8,128)S(1)} collective-permute-done((f32[704,128]{1,0:T(8,128)S(1)}, f32[704,128]{1,0:T(8,128)S(1)}, u32[]{:S(2)}, u32[]{:S(2)}) %collective-permute-start.8) | collective-permute-done | bytes 360480 | tf_op jit(solution)/shard_map/ppermute | solution.py:372
  91.8 3.4 %collective-permute-start.16 = (f32[336,128]{1,0:T(8,128)S(1)}, f32[336,128]{1,0:T(8,128)S(1)}, u32[]{:S(2)}, u32[]{:S(2)}) collective-permute-start(f32[336,128]{1,0:T(8,128)S(1)} %constant_dynamic-slice_fusion.3), channel_id=1, source_target_pairs={{0,16},{8,24},{16,0},{24,8},{1,17},{9,25},{17,1},{25,9},{2,18},{10... | collective-permute-start | bytes 516104 | tf_op jit(solution)/shard_map/ppermute | solution.py:372
  98.1 3.5 %collective-permute-start.19 = (f32[8,9,512]{2,1,0:T(8,128)S(1)}, f32[8,9,512]{2,1,0:T(8,128)S(1)}, u32[]{:S(2)}, u32[]{:S(2)}) collective-permute-start(f32[8,9,512]{2,1,0:T(8,128)S(1)} %get-tuple-element.86), channel_id=1, source_target_pairs={{2,0},{4,2},{6,4},{0,6},{3,1},{5,3},{7,5},{1,7},{10,8},{12,10},{14... | collective-permute-start | bytes 442376 | tf_op jit(solution)/shard_map/ppermute | solution.py:311
  103.3 4.3 %collective-permute-done.15 = f32[352,128]{1,0:T(8,128)S(1)} collective-permute-done((f32[352,128]{1,0:T(8,128)S(1)}, f32[352,128]{1,0:T(8,128)S(1)}, u32[]{:S(2)}, u32[]{:S(2)}) %collective-permute-start.15) | collective-permute-done | bytes 180256 | tf_op jit(solution)/shard_map/ppermute | solution.py:372
  108.1 4.2 %collective-permute-done.17 = f32[176,128]{1,0:T(8,128)S(1)} collective-permute-done((f32[176,128]{1,0:T(8,128)S(1)}, f32[176,128]{1,0:T(8,128)S(1)}, u32[]{:S(2)}, u32[]{:S(2)}) %collective-permute-start.17) | collective-permute-done | bytes 90144 | tf_op jit(solution)/shard_map/ppermute | solution.py:372
  115.3 10.7 %collective-permute-done.21 = f32[520,128]{1,0:T(8,128)S(1)} collective-permute-done((f32[520,128]{1,0:T(8,128)S(1)}, f32[520,128]{1,0:T(8,128)S(1)}, u32[]{:S(2)}, u32[]{:S(2)}) %collective-permute-start.21) | collective-permute-done | bytes 266272 | tf_op jit(solution)/shard_map/ppermute | solution.py:372
  128.5 2.3 %collective-permute-start.25 = (f32[176,128]{1,0:T(8,128)S(1)}, f32[176,128]{1,0:T(8,128)S(1)}, u32[]{:S(2)}, u32[]{:S(2)}) collective-permute-start(f32[176,128]{1,0:T(8,128)S(1)} %get-tuple-element.103), channel_id=1, source_target_pairs={{0,16},{8,24},{16,0},{24,8},{1,17},{9,25},{17,1},{25,9},{2,18},{10... | collective-permute-start | bytes 270344 | tf_op jit(solution)/shard_map/ppermute | solution.py:372
  130.9 2.5 %collective-permute-start.29 = (f32[336,128]{1,0:T(8,128)S(1)}, f32[336,128]{1,0:T(8,128)S(1)}, u32[]{:S(2)}, u32[]{:S(2)}) collective-permute-start(f32[336,128]{1,0:T(8,128)S(1)} %pad_maximum_fusion.6), channel_id=1, source_target_pairs={{0,16},{8,24},{16,0},{24,8},{1,17},{9,25},{17,1},{25,9},{2,18},{10... | collective-permute-start | bytes 516104 | tf_op jit(solution)/shard_map/ppermute | solution.py:372
  137.1 3.9 %collective-permute-done.24 = f32[352,128]{1,0:T(8,128)S(1)} collective-permute-done((f32[352,128]{1,0:T(8,128)S(1)}, f32[352,128]{1,0:T(8,128)S(1)}, u32[]{:S(2)}, u32[]{:S(2)}) %collective-permute-start.24) | collective-permute-done | bytes 180256 | tf_op jit(solution)/shard_map/ppermute | solution.py:372
  141.1 2.0 %collective-permute-done.28 = f32[352,128]{1,0:T(8,128)S(1)} collective-permute-done((f32[352,128]{1,0:T(8,128)S(1)}, f32[352,128]{1,0:T(8,128)S(1)}, u32[]{:S(2)}, u32[]{:S(2)}) %collective-permute-start.28) | collective-permute-done | bytes 180256 | tf_op jit(solution)/shard_map/ppermute | solution.py:372
  144.2 7.2 %collective-permute-done.31 = f32[672,128]{1,0:T(8,128)S(1)} collective-permute-done((f32[672,128]{1,0:T(8,128)S(1)}, f32[672,128]{1,0:T(8,128)S(1)}, u32[]{:S(2)}, u32[]{:S(2)}) %collective-permute-start.31) | collective-permute-done | bytes 344096 | tf_op jit(solution)/shard_map/ppermute | solution.py:372
  153.4 2.8 %collective-permute-done.32.refs_2_ = f32[4160,128]{1,0:T(8,128)} collective-permute-done((f32[4160,128]{1,0:T(8,128)S(1)}, f32[4160,128]{1,0:T(8,128)}, u32[]{:S(2)}, u32[]{:S(2)}) %collective-permute-start.32) | collective-permute-done | bytes 2129952 | tf_op jit(solution)/shard_map/ppermute | solution.py:372
  156.2 4.2 %unpack.1 = (f32[4,128]{1,0:T(4,128)}, f32[512,1536]{1,0:T(8,128)}, f32[4,128,512]{2,1,0:T(8,128)}) custom-call(s32[1]{0:T(128)} %bitcast.refs_0_, f32[4160,128]{1,0:T(8,128)S(1)} %select_dynamic-update-slice_fusion.4.refs_1_, f32[4160,128]{1,0:T(8,128)} %collective-permute-done.32.refs_2_), custom_call_target="tpu_custom_call" | custom-call | flops 1000000 | bytes 8000000 | tf_op jit(solution)/shard_map/unpack/pallas_call | solution.py:290
  (116 shorter events, 34.9 us)
Async XLA Ops:
  1.8 18.9 %collective-permute-start.3 = (f32[8,6,512]{2,1,0:T(8,128)S(1)}, f32[8,6,512]{2,1,0:T(8,128)S(1)}, u32[]{:S(2)}, u32[]{:S(2)}) collective-permute-start(f32[8,6,512]{2,1,0:T(8,128)S(1)} %get-tuple-element.105), channel_id=1, source_target_pairs={{2,0},{4,2},{6,4},{0,6},{3,1},{5,3},{7,5},{1,7},{10,8},{12,10},{14... | collective-permute-start | bytes 294920 | tf_op jit(solution)/shard_map/ppermute | solution.py:311
  6.9 13.8 %collective-permute-start.1 = (f32[8,6,512]{2,1,0:T(8,128)S(1)}, f32[8,6,512]{2,1,0:T(8,128)S(1)}, u32[]{:S(2)}, u32[]{:S(2)}) collective-permute-start(f32[8,6,512]{2,1,0:T(8,128)S(1)} %get-tuple-element.106), channel_id=1, source_target_pairs={{0,2},{2,4},{4,6},{6,0},{1,3},{3,5},{5,7},{7,1},{8,10},{10,12},{12... | collective-permute-start | bytes 294920 | tf_op jit(solution)/shard_map/ppermute | solution.py:311
  8.3 12.4 %collective-permute-start = (f32[8,8,512]{2,1,0:T(8,128)S(1)}, f32[8,8,512]{2,1,0:T(8,128)S(1)}, u32[]{:S(2)}, u32[]{:S(2)}) collective-permute-start(f32[8,8,512]{2,1,0:T(8,128)S(1)} %fusion.1), channel_id=1, source_target_pairs={{0,1},{1,0},{2,3},{3,2},{4,5},{5,4},{6,7},{7,6},{8,9},{9,8},{10,11... | collective-permute-start | bytes 393224 | tf_op jit(solution)/shard_map/ppermute | solution.py:324
  9.9 6.2 %collective-permute-start.4 = (f32[8,3,512]{2,1,0:T(4,128)S(1)}, f32[8,3,512]{2,1,0:T(4,128)S(1)}, u32[]{:S(2)}, u32[]{:S(2)}) collective-permute-start(f32[8,3,512]{2,1,0:T(4,128)S(1)} %get-tuple-element.109), channel_id=1, source_target_pairs={{0,7},{1,6},{2,1},{3,0},{4,3},{5,2},{6,5},{7,4},{8,15},{9,14},{10,... | collective-permute-start | bytes 147464 | tf_op jit(solution)/shard_map/ppermute | solution.py:320
  13.7 7.0 %collective-permute-start.2 = (f32[8,3,512]{2,1,0:T(4,128)S(1)}, f32[8,3,512]{2,1,0:T(4,128)S(1)}, u32[]{:S(2)}, u32[]{:S(2)}) collective-permute-start(f32[8,3,512]{2,1,0:T(4,128)S(1)} %get-tuple-element.110), channel_id=1, source_target_pairs={{0,3},{1,2},{2,5},{3,4},{4,7},{5,6},{6,1},{7,0},{8,11},{9,10},{10,... | collective-permute-start | bytes 147464 | tf_op jit(solution)/shard_map/ppermute | solution.py:320
  66.2 7.3 %collective-permute-start.7 = (f32[4160,128]{1,0:T(8,128)}, f32[4160,128]{1,0:T(8,128)}, u32[]{:S(2)}, u32[]{:S(2)}) collective-permute-start(f32[4160,128]{1,0:T(8,128)} %get-tuple-element.46), channel_id=1, source_target_pairs={{0,8},{8,0},{16,24},{24,16},{1,9},{9,1},{17,25},{25,17},{2,10},{10... | collective-permute-start | bytes 6389768 | tf_op jit(solution)/shard_map/ppermute | solution.py:372
  75.4 10.7 %collective-permute-start.10 = (f32[672,128]{1,0:T(8,128)}, f32[672,128]{1,0:T(8,128)}, u32[]{:S(2)}, u32[]{:S(2)}) collective-permute-start(f32[672,128]{1,0:T(8,128)} %dynamic-slice_add_fusion.2), channel_id=1, source_target_pairs={{0,2},{2,0},{4,6},{6,4},{1,3},{3,1},{5,7},{7,5},{8,10},{10,8},{12,... | collective-permute-start | bytes 1032200 | tf_op jit(solution)/shard_map/ppermute | solution.py:372
  77.5 10.9 %collective-permute-start.9 = (f32[704,128]{1,0:T(8,128)}, f32[704,128]{1,0:T(8,128)S(1)}, u32[]{:S(2)}, u32[]{:S(2)}) collective-permute-start(f32[704,128]{1,0:T(8,128)} %get-tuple-element.83), channel_id=1, source_target_pairs={{0,1},{1,0},{2,3},{3,2},{4,5},{5,4},{6,7},{7,6},{8,9},{9,8},{10,11... | collective-permute-start | bytes 1081352 | tf_op jit(solution)/shard_map/ppermute | solution.py:372
  79.0 11.5 %collective-permute-start.8 = (f32[704,128]{1,0:T(8,128)S(1)}, f32[704,128]{1,0:T(8,128)S(1)}, u32[]{:S(2)}, u32[]{:S(2)}) collective-permute-start(f32[704,128]{1,0:T(8,128)S(1)} %get-tuple-element.84), channel_id=1, source_target_pairs={{0,16},{8,24},{16,0},{24,8},{1,17},{9,25},{17,1},{25,9},{2,18},{10... | collective-permute-start | bytes 1081352 | tf_op jit(solution)/shard_map/ppermute | solution.py:372
  81.7 10.0 %collective-permute-start.11 = (f32[3,48,512]{2,1,0:T(8,128)}, f32[3,48,512]{2,1,0:T(8,128)S(1)}, u32[]{:S(2)}, u32[]{:S(2)}) collective-permute-start(f32[3,48,512]{2,1,0:T(8,128)} %get-tuple-element.50), channel_id=1, source_target_pairs={{0,8},{8,16},{16,24},{1,9},{9,17},{17,25},{2,10},{10,18},{18,26},{... | collective-permute-start | bytes 884744 | tf_op jit(solution)/shard_map/ppermute | solution.py:311
  83.2 8.5 %collective-permute-start.12 = (f32[3,48,512]{2,1,0:T(8,128)}, f32[3,48,512]{2,1,0:T(8,128)S(1)}, u32[]{:S(2)}, u32[]{:S(2)}) collective-permute-start(f32[3,48,512]{2,1,0:T(8,128)} %get-tuple-element.51), channel_id=1, source_target_pairs={{8,0},{16,8},{24,16},{9,1},{17,9},{25,17},{10,2},{18,10},{26,18},{... | collective-permute-start | bytes 884744 | tf_op jit(solution)/shard_map/ppermute | solution.py:311
  91.8 9.8 %collective-permute-start.16 = (f32[336,128]{1,0:T(8,128)S(1)}, f32[336,128]{1,0:T(8,128)S(1)}, u32[]{:S(2)}, u32[]{:S(2)}) collective-permute-start(f32[336,128]{1,0:T(8,128)S(1)} %constant_dynamic-slice_fusion.3), channel_id=1, source_target_pairs={{0,16},{8,24},{16,0},{24,8},{1,17},{9,25},{17,1},{25,9},{2,18},{10... | collective-permute-start | bytes 516104 | tf_op jit(solution)/shard_map/ppermute | solution.py:372
  95.2 12.4 %collective-permute-start.15 = (f32[352,128]{1,0:T(8,128)S(1)}, f32[352,128]{1,0:T(8,128)S(1)}, u32[]{:S(2)}, u32[]{:S(2)}) collective-permute-start(f32[352,128]{1,0:T(8,128)S(1)} %constant_dynamic-slice_fusion.4), channel_id=1, source_target_pairs={{0,2},{2,0},{4,6},{6,4},{1,3},{3,1},{5,7},{7,5},{8,10},{10,8},{12,... | collective-permute-start | bytes 540680 | tf_op jit(solution)/shard_map/ppermute | solution.py:372
  97.0 10.9 %collective-permute-start.13 = (f32[352,128]{1,0:T(8,128)S(1)}, f32[352,128]{1,0:T(8,128)S(1)}, u32[]{:S(2)}, u32[]{:S(2)}) collective-permute-start(f32[352,128]{1,0:T(8,128)S(1)} %constant_dynamic-slice_fusion.5), channel_id=1, source_target_pairs={{0,1},{1,0},{2,3},{3,2},{4,5},{5,4},{6,7},{7,6},{8,9},{9,8},{10,11... | collective-permute-start | bytes 540680 | tf_op jit(solution)/shard_map/ppermute | solution.py:372
  97.8 15.6 %collective-permute-start.20 = (f32[8,9,512]{2,1,0:T(8,128)S(1)}, f32[8,9,512]{2,1,0:T(8,128)S(1)}, u32[]{:S(2)}, u32[]{:S(2)}) collective-permute-start(f32[8,9,512]{2,1,0:T(8,128)S(1)} %get-tuple-element.85), channel_id=1, source_target_pairs={{0,2},{2,4},{4,6},{6,0},{1,3},{3,5},{5,7},{7,1},{8,10},{10,12},{12... | collective-permute-start | bytes 442376 | tf_op jit(solution)/shard_map/ppermute | solution.py:311
  98.1 15.3 %collective-permute-start.19 = (f32[8,9,512]{2,1,0:T(8,128)S(1)}, f32[8,9,512]{2,1,0:T(8,128)S(1)}, u32[]{:S(2)}, u32[]{:S(2)}) collective-permute-start(f32[8,9,512]{2,1,0:T(8,128)S(1)} %get-tuple-element.86), channel_id=1, source_target_pairs={{2,0},{4,2},{6,4},{0,6},{3,1},{5,3},{7,5},{1,7},{10,8},{12,10},{14... | collective-permute-start | bytes 442376 | tf_op jit(solution)/shard_map/ppermute | solution.py:311
  101.7 6.4 %collective-permute-start.18 = (f32[168,128]{1,0:T(8,128)S(1)}, f32[168,128]{1,0:T(8,128)S(1)}, u32[]{:S(2)}, u32[]{:S(2)}) collective-permute-start(f32[168,128]{1,0:T(8,128)S(1)} %constant_dynamic-slice_fusion), channel_id=1, source_target_pairs={{0,1},{1,0},{2,3},{3,2},{4,5},{5,4},{6,7},{7,6},{8,9},{9,8},{10,11... | collective-permute-start | bytes 258056 | tf_op jit(solution)/shard_map/ppermute | solution.py:372
  113.4 12.6 %collective-permute-start.21 = (f32[520,128]{1,0:T(8,128)S(1)}, f32[520,128]{1,0:T(8,128)S(1)}, u32[]{:S(2)}, u32[]{:S(2)}) collective-permute-start(f32[520,128]{1,0:T(8,128)S(1)} %pad_maximum_fusion.3), channel_id=1, source_target_pairs={{0,4},{2,6},{4,0},{6,2},{1,5},{3,7},{5,1},{7,3},{8,12},{10,14},{12... | collective-permute-start | bytes 798728 | tf_op jit(solution)/shard_map/ppermute | solution.py:372
  113.8 12.3 %collective-permute-start.22 = (f32[8,8,512]{2,1,0:T(8,128)S(1)}, f32[8,8,512]{2,1,0:T(8,128)S(1)}, u32[]{:S(2)}, u32[]{:S(2)}) collective-permute-start(f32[8,8,512]{2,1,0:T(8,128)S(1)} %fusion), channel_id=1, source_target_pairs={{0,1},{1,0},{2,3},{3,2},{4,5},{5,4},{6,7},{7,6},{8,9},{9,8},{10,11... | collective-permute-start | bytes 393224 | tf_op jit(solution)/shard_map/ppermute | solution.py:324
  130.9 6.1 %collective-permute-start.29 = (f32[336,128]{1,0:T(8,128)S(1)}, f32[336,128]{1,0:T(8,128)S(1)}, u32[]{:S(2)}, u32[]{:S(2)}) collective-permute-start(f32[336,128]{1,0:T(8,128)S(1)} %pad_maximum_fusion.6), channel_id=1, source_target_pairs={{0,16},{8,24},{16,0},{24,8},{1,17},{9,25},{17,1},{25,9},{2,18},{10... | collective-permute-start | bytes 516104 | tf_op jit(solution)/shard_map/ppermute | solution.py:372
  137.0 6.1 %collective-permute-start.28 = (f32[352,128]{1,0:T(8,128)S(1)}, f32[352,128]{1,0:T(8,128)S(1)}, u32[]{:S(2)}, u32[]{:S(2)}) collective-permute-start(f32[352,128]{1,0:T(8,128)S(1)} %pad_maximum_fusion.5), channel_id=1, source_target_pairs={{0,2},{2,0},{4,6},{6,4},{1,3},{3,1},{5,7},{7,5},{8,10},{10,8},{12,... | collective-permute-start | bytes 540680 | tf_op jit(solution)/shard_map/ppermute | solution.py:372
  143.1 8.4 %collective-permute-start.30 = (f32[704,128]{1,0:T(8,128)S(1)}, f32[704,128]{1,0:T(8,128)S(1)}, u32[]{:S(2)}, u32[]{:S(2)}) collective-permute-start(f32[704,128]{1,0:T(8,128)S(1)} %pad_maximum_fusion.1), channel_id=1, source_target_pairs={{0,1},{1,0},{2,3},{3,2},{4,5},{5,4},{6,7},{7,6},{8,9},{9,8},{10,11... | collective-permute-start | bytes 1081352 | tf_op jit(solution)/shard_map/ppermute | solution.py:372
  143.2 8.2 %collective-permute-start.27 = (f32[704,128]{1,0:T(8,128)S(1)}, f32[704,128]{1,0:T(8,128)S(1)}, u32[]{:S(2)}, u32[]{:S(2)}) collective-permute-start(f32[704,128]{1,0:T(8,128)S(1)} %pad_maximum_fusion), channel_id=1, source_target_pairs={{0,16},{8,24},{16,0},{24,8},{1,17},{9,25},{17,1},{25,9},{2,18},{10... | collective-permute-start | bytes 1081352 | tf_op jit(solution)/shard_map/ppermute | solution.py:372
  144.1 7.3 %collective-permute-start.31 = (f32[672,128]{1,0:T(8,128)S(1)}, f32[672,128]{1,0:T(8,128)S(1)}, u32[]{:S(2)}, u32[]{:S(2)}) collective-permute-start(f32[672,128]{1,0:T(8,128)S(1)} %pad_maximum_fusion.2), channel_id=1, source_target_pairs={{0,2},{2,0},{4,6},{6,4},{1,3},{3,1},{5,7},{7,5},{8,10},{10,8},{12,... | collective-permute-start | bytes 1032200 | tf_op jit(solution)/shard_map/ppermute | solution.py:372
  (18 other events, 147.0 us)
